TPU v7x, 256 devices: a whole 4x4x8 slice. The times are simulated.
256 devices in a mesh: prefix: 16 (over z, core), branch: 16 (over y, x).
Axes of the slice: x: 4, y: 4, z: 8, core: 2. Of those that a mesh axis runs over, the one named last changes fastest.
Arguments:
- token_ids: int32 [4, 768], P(None, 'prefix'), may hold values from 0 to 127999
- prompt_of: int32 [768, 1], P('prefix'), may hold values from 0 to 31; in each aligned block of 48 rows (0 to 47, 48 to 95, ...) at most 6 rows name the same one
- suffix_len: int32 [768], P('prefix'), may hold values from 1 to 8, 3072 in all
- table: bfloat16 [128000, 4608], P('prefix', 'branch'), may hold values from -12 to 12
- pre_gain: float32 [4608], replicated, may hold values from 0.1 to 1.9
- w_query: bfloat16 [4608, 4096], P(None, 'branch'), may hold values from -0.09375 to 0.09375
- w_keyval: bfloat16 [2, 4608, 2048], P(None, None, 'branch'), may hold values from -0.09375 to 0.09375
- w_out: bfloat16 [4096, 4608], P('branch'), may hold values from -2.5 to 2.5
- post_gain: float32 [4608], P('branch'), may hold values from 0.1 to 1.9
- prefix_keys: bfloat16 [32, 1024, 2048], P('prefix', None, 'branch'), may hold values from -6 to 6
- prefix_values: bfloat16 [32, 1024, 2048], P('prefix', None, 'branch'), may hold values from -4 to 4
- suffix_keys: bfloat16 [768, 8, 2048], P('prefix', None, 'branch'), may hold values from -6 to 6
- suffix_values: bfloat16 [768, 8, 2048], P('prefix', None, 'branch'), may hold values from -6 to 6
Outputs:
- layer_out: bfloat16 [4, 768, 4608], P(None, 'prefix', 'branch')
Inputs may be any that keep to these rules, and one draw needn't show every extreme that they name: `prompt_of`: at most 6 of the rows of one index of prefix name the same prompt; in every draw some index reaches 6 for some prompt, and every prompt is named by some row. `suffix_len`: some row fills all 8 slots.
All inputs are finite; a program needn't handle non-finite values. No bound on the sum of `suffix_len` on one device may be relied on, other than what follows from the above.
Results may differ from a plain program's by a relative error of at most 0.017.
Values may be sent and summed in bfloat16 or wider, within the bound.
No kernel may reach another device: no remote copies, remote signals or barrier semaphores. Data moves between devices by JAX's collectives and lax.ppermute only.
A program may use at most 64 MiB of HBM per device.

v0:
```python
import jax
import jax.numpy as jnp
from jax import lax
from jax.sharding import PartitionSpec as P

D = 4608
HEADS = 32
KV_HEADS = 16
HEAD = 128
SUF = 8
MOST = 6


SOFT_CAP = 50.0
EPSILON = 1e-06


def rotary(values, positions):
    half_size = values.shape[-1] // 2
    frequency = 10000.0 ** (-(jnp.arange(half_size, dtype=jnp.float32) * 2.0 / values.shape[-1]))
    angles = positions[..., None] * frequency
    cosines = jnp.cos(angles)
    sines = jnp.sin(angles)
    lower_half = values[..., :half_size]
    upper_half = values[..., half_size:]
    return jnp.concatenate(
        [lower_half * cosines - upper_half * sines, upper_half * cosines + lower_half * sines],
        axis=-1,
    )


def capped_exp(scores):
    return jnp.exp(SOFT_CAP * jnp.tanh(scores / SOFT_CAP))


def per_device(
    token_ids,
    prompt_of,
    suffix_len,
    table,
    pre_gain,
    w_query,
    w_keyval,
    w_out,
    post_gain,
    prefix_keys,
    prefix_values,
    suffix_keys,
    suffix_values,
):
    step_count, row_count = token_ids.shape
    group = HEADS // KV_HEADS
    score_scale = float(D // HEADS) ** (-0.5)
    kv_local = w_keyval.shape[2] // HEAD
    prompt_local = prefix_keys.shape[0]
    prompt_len = prefix_keys.shape[1]
    owners = lax.axis_size("prefix")
    prompts_all = prompt_local * owners
    ids_all = lax.all_gather(token_ids, "prefix", axis=1, tiled=True)
    vocab_local = table.shape[0]
    local_ids = ids_all - lax.axis_index("prefix") * vocab_local
    inside = (local_ids >= 0) & (local_ids < vocab_local)
    picked = jnp.take(table, jnp.clip(local_ids, 0, vocab_local - 1), axis=0)
    partial_rows = jnp.where(inside[..., None], picked, jnp.zeros_like(picked))
    embedded = (
        lax.psum_scatter(partial_rows, "prefix", scatter_dimension=1, tiled=True)
        .astype(jnp.float32)
        .astype(jnp.bfloat16)
    )
    share_width = embedded.shape[2]
    full_rows = lax.all_gather(embedded, "branch", axis=2, tiled=True)
    wide = full_rows.astype(jnp.float32)
    normed = (
        wide * lax.rsqrt(jnp.mean(wide * wide, axis=-1, keepdims=True) + EPSILON) * pre_gain
    ).astype(jnp.bfloat16)
    flat = normed.reshape(step_count * row_count, D)
    positions = (prompt_len + suffix_len[None, :] + jnp.arange(step_count)[:, None]).astype(
        jnp.float32
    )[..., None]
    queries = rotary(
        jnp.dot(flat, w_query, preferred_element_type=jnp.float32).reshape(
            step_count, row_count, kv_local * group, HEAD
        ),
        positions,
    ).astype(jnp.bfloat16)
    new_keys = rotary(
        jnp.dot(flat, w_keyval[0], preferred_element_type=jnp.float32).reshape(
            step_count, row_count, kv_local, HEAD
        ),
        positions,
    ).astype(jnp.bfloat16)
    new_values = (
        jnp.dot(flat, w_keyval[1], preferred_element_type=jnp.float32)
        .reshape(step_count, row_count, kv_local, HEAD)
        .astype(jnp.bfloat16)
    )
    chosen = prompt_of[:, 0]
    one_hot = (chosen[:, None] == jnp.arange(prompts_all)[None, :]).astype(jnp.int32)
    slot_index = jnp.sum((jnp.cumsum(one_hot, axis=0) - 1) * one_hot, axis=1)
    target = chosen * MOST + slot_index
    placing = (jnp.arange(prompts_all * MOST)[:, None] == target[None, :]).astype(jnp.bfloat16)
    query_rows = (
        queries.reshape(step_count, row_count, kv_local, group, HEAD)
        .transpose(1, 2, 0, 3, 4)
        .reshape(row_count, kv_local * step_count * group * HEAD)
    )
    send_slots = jnp.dot(placing, query_rows, preferred_element_type=jnp.float32).astype(
        jnp.bfloat16
    )
    send_slots = send_slots.reshape(owners, prompt_local, MOST, kv_local, step_count * group, HEAD)
    cache_keys = prefix_keys.reshape(prompt_local, prompt_len, kv_local, HEAD)
    cache_values = prefix_values.reshape(prompt_local, prompt_len, kv_local, HEAD)
    copies = lax.all_gather(send_slots, "prefix", axis=0, tiled=True)
    copies = copies.reshape((owners, owners) + send_slots.shape[1:])
    own_slots = lax.dynamic_index_in_dim(copies, lax.axis_index("prefix"), 1, keepdims=False)
    scores = (
        jnp.einsum("njmcge,jkce->njmcgk", own_slots, cache_keys, preferred_element_type=jnp.float32)
        * score_scale
    )
    weights = capped_exp(scores).astype(jnp.bfloat16)
    numer = jnp.einsum(
        "njmcgk,jkce->njmcge", weights, cache_values, preferred_element_type=jnp.float32
    )
    denom = jnp.sum(weights.astype(jnp.float32), axis=-1)
    numer_back, denom_back = (
        lax.all_to_all(
            numer.astype(jnp.bfloat16), "prefix", split_axis=0, concat_axis=0, tiled=True
        ).astype(numer.dtype),
        lax.all_to_all(
            denom.astype(jnp.bfloat16), "prefix", split_axis=0, concat_axis=0, tiled=True
        ).astype(denom.dtype),
    )
    prefix_numer = jnp.take(numer_back.reshape(prompts_all * MOST, -1), target, axis=0)
    prefix_numer = prefix_numer.reshape(row_count, kv_local, step_count, group, HEAD).transpose(
        2, 0, 1, 3, 4
    )
    prefix_denom = jnp.take(denom_back.reshape(prompts_all * MOST, -1), target, axis=0)
    prefix_denom = prefix_denom.reshape(row_count, kv_local, step_count, group).transpose(
        2, 0, 1, 3
    )
    local_keys = jnp.concatenate(
        [suffix_keys.reshape(row_count, SUF, kv_local, HEAD), new_keys.transpose(1, 0, 2, 3)],
        axis=1,
    )
    local_values = jnp.concatenate(
        [suffix_values.reshape(row_count, SUF, kv_local, HEAD), new_values.transpose(1, 0, 2, 3)],
        axis=1,
    )
    slot_ids = jnp.arange(SUF + step_count)[None, None, :]
    step_ids = jnp.arange(step_count)[:, None, None]
    usable = jnp.where(
        slot_ids < SUF, slot_ids < suffix_len[None, :, None], slot_ids - SUF <= step_ids
    )
    query_local = queries.reshape(step_count, row_count, kv_local, group, HEAD)
    local_scores = (
        jnp.einsum("trcge,rjce->trcgj", query_local, local_keys, preferred_element_type=jnp.float32)
        * score_scale
    )
    local_weights = jnp.where(usable[:, :, None, None, :], capped_exp(local_scores), 0.0).astype(
        jnp.bfloat16
    )
    local_numer = jnp.einsum(
        "trcgj,rjce->trcge", local_weights, local_values, preferred_element_type=jnp.float32
    )
    local_denom = jnp.sum(local_weights.astype(jnp.float32), axis=-1)
    attended = ((prefix_numer + local_numer) / (prefix_denom + local_denom)[..., None]).astype(
        jnp.bfloat16
    )
    attended = attended.reshape(step_count * row_count, kv_local * group * HEAD)
    residual = embedded.astype(jnp.float32).reshape(step_count * row_count, share_width)
    own_block = (
        lax.psum_scatter(
            lax.dot_general(
                w_out, attended, (((0,), (1,)), ((), ())), preferred_element_type=jnp.float32
            ).astype(jnp.bfloat16),
            "branch",
            scatter_dimension=0,
            tiled=True,
        )
        .astype(jnp.float32)
        .T
    )
    squares = lax.psum(jnp.sum(own_block * own_block, axis=1, keepdims=True), "branch")
    scaled = own_block * lax.rsqrt(squares / D + EPSILON) * post_gain
    layer_out = (residual + scaled).astype(jnp.bfloat16)
    return layer_out.reshape(step_count, row_count, share_width)


def solution(mesh):
    placed = (
        P(None, "prefix"),
        P("prefix", None),
        P("prefix"),
        P("prefix", "branch"),
        P(),
        P(None, "branch"),
        P(None, None, "branch"),
        P("branch", None),
        P("branch"),
        P("prefix", None, "branch"),
        P("prefix", None, "branch"),
        P("prefix", None, "branch"),
        P("prefix", None, "branch"),
    )
    return jax.shard_map(
        per_device,
        mesh=mesh,
        in_specs=placed,
        out_specs=P(None, "prefix", "branch"),
        check_vma=False,
    )
```

profile of v0, /device:TPU:32, one launch (start us, length us, event | category | flops | bytes accessed | tf_op | source)
XLA Modules:
  0.0 400.9 jit_solution(10619789897603872824)
XLA Ops:
  6.5 18.3 %all-gather = s32[16,48,4]{1,2,0:T(4,128)S(1)} all-gather(s32[1,48,4]{1,2,0:T(4,128)} %bitcast.203), channel_id=1, replica_groups=mesh['prefix'=16,'branch'=16] {'prefix'}, dimensions={0}, use_global_device_ids=true | all-gather | bytes 13056 | tf_op jit(solution)/shard_map/all_gather | solution.py:59
  24.8 0.1 reshape.390
  24.9 0.1 reshape.391
  25.1 7.8 %copy.82 = bf16[8000,288]{1,0:T(8,128)(2,1)} copy(bf16[8000,288]{0,1:T(8,128)(2,1)} %param.16) | data formatting | bytes 9216000 | tf_op args[3]
  32.9 16.4 %gather_fusion = bf16[3072,288]{1,0:T(8,128)(2,1)} fusion(bf16[8000,288]{1,0:T(8,128)(2,1)} %copy.82, s32[3072]{0:T(1024)S(1)} %broadcast_clamp_fusion), kind=kCustom, calls=%fused_computation | custom fusion | bytes 3551232 | tf_op jit(solution)/shard_map/jit(_take)/gather | solution.py:63
  49.2 4.5 %select_select_fusion = bf16[4,768,288]{2,1,0:T(8,128)(2,1)} fusion(bf16[4,768,288]{2,1,0:T(8,128)(2,1)} %bitcast.187, pred[4,768]{1,0:T(4,128)(4,1)S(1)} %compare_and_fusion.1, pred[4,768]{1,0:T(4,128)(4,1)S(1)} %bitcast.198), kind=kLoop, calls=%fused_computation.14 | loop fusion | flops 1769472 | bytes 3545088 | tf_op jit(solution)/shard_map/jit(_where)/select_n | solution.py:64
  53.7 0.0 reduce-scatter.5.cloned.1.call-update
  53.7 0.0 all-gather.4.cloned.1.call-start
  53.8 56.6 %reduce-scatter.5.cloned.1.call-done = bf16[4,48,288]{2,1,0:T(8,128)(2,1)} async-done(((bf16[4,768,288]{2,1,0:T(8,128)(2,1)}), bf16[4,48,288]{2,1,0:T(8,128)(2,1)}) %reduce-scatter.5.cloned.1.call-update) | async-done | bytes 110608 | tf_op jit(solution)/shard_map/reduce_scatter | solution.py:66
  110.4 1.8 copy.83
  112.3 0.0 all-gather.6.cloned.1.call-start
  112.4 4.3 %copy.106 = bf16[256,4608]{1,0:T(8,128)(2,1)} copy(bf16[256,4608]{0,1:T(8,128)(2,1)} %bitcast.189) | data formatting | bytes 4718592 | tf_op jit(solution)/shard_map/dot_general | solution.py:81
  116.7 0.1 fusion.68
  116.7 0.1 reduce_window_sum.11
  116.8 0.2 select_reduce_fusion
  117.0 0.4 multiply_cosine_fusion.1
  117.5 56.2 %all-gather.4.cloned.1.call-done = bf16[4,48,4608]{1,0,2:T(4,128)(2,1)} async-done(((bf16[4,48,288]{1,0,2:T(4,128)(2,1)}), bf16[4,48,4608]{1,0,2:T(4,128)(2,1)}) %all-gather.4.cloned.1.call-update) | async-done | bytes 1769488 | tf_op jit(solution)/shard_map/all_gather | solution.py:71
  173.6 7.1 %copy.84 = bf16[4,48,4608]{2,1,0:T(8,128)(2,1)} copy(bf16[4,48,4608]{1,0,2:T(4,128)(2,1)} %all-gather.4.cloned.1.call-done) | data formatting | bytes 3538944 | tf_op jit(solution)/shard_map/all_gather | solution.py:71
  180.7 1.9 fusion.1
  182.6 3.2 fusion.6
  185.8 0.1 subtract_convert_fusion
  185.9 0.1 maximum_bitcast_fusion.4
  186.0 0.1 copy.86
  186.2 0.2 fusion.11
  186.4 0.8 copy.112
  187.2 0.0 all-gather.6.cloned.1.call-update
  187.3 0.1 iota_compare_fusion.2
  187.4 0.6 broadcast_select_fusion
  188.0 2.5 fusion.28
  190.6 0.5 fusion.58
  191.0 0.1 maximum_bitcast_fusion.5
  191.1 0.6 copy.92
  191.8 41.1 %all-gather.6.cloned.1.call-done = bf16[256,2,6,1,8,128]{5,4,3,2,1,0:T(8,128)(2,1)} async-done(((bf16[16,2,6,1,8,128]{5,4,3,2,1,0:T(8,128)(2,1)}), bf16[256,2,6,1,8,128]{5,4,3,2,1,0:T(8,128)(2,1)}) %all-gather.6.cloned.1.call-update) | async-done | bytes 6291472 | tf_op jit(solution)/shard_map/all_gather | solution.py:113
  232.8 4.8 %bitcast_reduce_fusion = (bf16[16,2,6,8]{3,2,0,1:T(8,128)(2,1)S(1)}, bf16[2,16,6,8,1024]{4,3,2,1,0:T(8,128)(2,1)}) fusion(bf16[2,1024,128]{2,1,0:T(8,128)(2,1)} %param.22, bf16[16,16,2,6,1,8,128]{6,5,3,2,1,0,4:T(8,128)(2,1)} %bitcast.205, s32[]{:T(128)S(6)} %select_n.64), kind=kOutput, calls=%fused_computation.13 | convolution fusion | flops 408943104 | bytes 4066308 | tf_op jit(solution)/shard_map/njmcge,jkce->njmcgk/dot_general | solution.py:117
  237.6 0.7 copy.94
  238.2 5.2 %all-to-all-start.1 = ((bf16[16,2,6,1,8]{4,1,3,2,0:T(2,128)(2,1)}), bf16[16,2,6,1,8]{4,1,3,2,0:T(2,128)(2,1)S(1)}, u32[]{:S(2)}, u32[]{:S(2)}) async-start(bf16[16,2,6,1,8]{4,1,3,2,0:T(2,128)(2,1)} %copy.94), calls=%async_computation.2 | async-start | bytes 98304 | tf_op jit(solution)/shard_map/all_to_all | solution.py:129
  243.5 2.9 fusion.12
  246.3 0.8 copy.89
  247.1 2.7 all-to-all-done.1
  249.8 4.9 %all-to-all-start = ((bf16[16,2,6,1,8,128]{5,4,2,1,3,0:T(8,128)(2,1)}), bf16[16,2,6,1,8,128]{5,4,2,1,3,0:T(8,128)(2,1)S(1)}, u32[]{:S(2)}, u32[]{:S(2)}) async-start(bf16[16,2,6,1,8,128]{5,4,2,1,3,0:T(8,128)(2,1)} %copy.89), calls=%async_computation.1 | async-start | bytes 786432 | tf_op jit(solution)/shard_map/all_to_all | solution.py:126
  254.7 0.2 reduce-scatter.7.cloned.1.call-start
  254.9 2.5 fusion.34
  257.4 0.6 copy.91
  258.1 0.1 pad_maximum_fusion
  258.2 0.9 convert_reduce_fusion
  259.1 0.1 copy.95
  259.2 0.1 copy.107
  259.4 0.6 gather_fusion.2
  260.0 0.1 copy.98
  260.0 0.1 copy.99
  260.2 0.7 fusion.65
  260.9 5.5 %all-to-all-done = bf16[16,2,6,1,8,128]{5,4,2,1,3,0:T(8,128)(2,1)S(1)} async-done(((bf16[16,2,6,1,8,128]{5,4,2,1,3,0:T(8,128)(2,1)}), bf16[16,2,6,1,8,128]{5,4,2,1,3,0:T(8,128)(2,1)S(1)}, u32[]{:S(2)}, u32[]{:S(2)}) %all-to-all-start) | async-done | bytes 393248 | tf_op jit(solution)/shard_map/all_to_all | solution.py:126
  266.4 0.1 copy.136
  266.5 0.7 gather_fusion.1
  267.2 0.2 gather.18
  267.3 1.2 fusion.27
  268.6 0.1 copy.100
  268.7 1.8 fusion
  270.5 4.0 copy.108
  274.5 79.8 %reduce-scatter.7.cloned.1.call-done = bf16[288,192]{1,0:T(8,128)(2,1)} async-done(((bf16[4608,192]{1,0:T(8,128)(2,1)}), bf16[288,192]{1,0:T(8,128)(2,1)}) %reduce-scatter.7.cloned.1.call-update) | async-done | bytes 110608
  354.3 1.0 copy.109
  355.3 0.1 fusion.44
  355.4 38.1 %psum.7 = f32[192,1]{0,1:T(1,128)S(1)} all-reduce(f32[192,1]{0,1:T(1,128)S(1)} %bitcast.202), channel_id=1, replica_groups=mesh['prefix'=16,'branch'=16] {'branch'}, use_global_device_ids=true, to_apply=%region_8.9 | all-reduce | flops 192 | bytes 1536 | tf_op jit(solution)/shard_map/psum | solution.py:183
  393.6 0.8 fusion.48
  (42 shorter events, 0.3 us)
Async XLA Ops:
  6.5 262.1 %copy-start = (bf16[256,4608]{1,0:T(8,128)(2,1)S(1)}, bf16[256,4608]{1,0:T(8,128)(2,1)}, u32[]{:S(2)}) copy-start(bf16[256,4608]{1,0:T(8,128)(2,1)} %param.20) | copy-start | bytes 7077892
  6.5 103.9 %reduce-scatter.5.cloned.1.call-start = ((), (), s32[]{:S(2)}) async-start(), calls=%async_computation.4 | async-start | bytes 2506752 | tf_op jit(solution)/shard_map/reduce_scatter | solution.py:66
  53.7 119.9 %all-gather.4.cloned.1.call-start = ((), (), s32[]{:S(2)}) async-start(), calls=%async_computation.5 | async-start | bytes 5013504 | tf_op jit(solution)/shard_map/all_gather | solution.py:71
  112.3 120.6 %all-gather.6.cloned.1.call-start = ((), (), s32[]{:S(2)}) async-start(), calls=%async_computation.6 | async-start | bytes 6684672 | tf_op jit(solution)/shard_map/all_gather | solution.py:113
  112.3 4.3 %copy-start.5 = (s32[48,1]{0,1:T(1,128)S(1)}, s32[48,1]{0,1:T(1,128)}, u32[]{:S(2)}) copy-start(s32[48,1]{0,1:T(1,128)} %param.14) | copy-start | bytes 580
  112.3 4.7 %copy-start.7 = (s32[48]{0:T(128)S(1)}, s32[48]{0:T(128)}, u32[]{:S(2)}) copy-start(s32[48]{0:T(128)} %param.15) | copy-start | bytes 580
  117.5 65.2 %copy-start.9 = (f32[4608]{0:T(1024)S(1)}, f32[4608]{0:T(1024)}, u32[]{:S(2)}) copy-start(f32[4608]{0:T(1024)} %param.17) | copy-start | bytes 55300
  232.8 10.6 %copy-start.2 = (bf16[2,1024,128]{2,1,0:T(8,128)(2,1)S(1)}, bf16[2,1024,128]{2,1,0:T(8,128)(2,1)}, u32[]{:S(2)}) copy-start(bf16[2,1024,128]{2,1,0:T(8,128)(2,1)} %param.23) | copy-start | bytes 1572868
  238.2 11.5 %all-to-all-start.1 = ((bf16[16,2,6,1,8]{4,1,3,2,0:T(2,128)(2,1)}), bf16[16,2,6,1,8]{4,1,3,2,0:T(2,128)(2,1)S(1)}, u32[]{:S(2)}, u32[]{:S(2)}) async-start(bf16[16,2,6,1,8]{4,1,3,2,0:T(2,128)(2,1)} %copy.94), calls=%async_computation.2 | async-start | bytes 98304 | tf_op jit(solution)/shard_map/all_to_all | solution.py:129
  249.8 16.7 %all-to-all-start = ((bf16[16,2,6,1,8,128]{5,4,2,1,3,0:T(8,128)(2,1)}), bf16[16,2,6,1,8,128]{5,4,2,1,3,0:T(8,128)(2,1)S(1)}, u32[]{:S(2)}, u32[]{:S(2)}) async-start(bf16[16,2,6,1,8,128]{5,4,2,1,3,0:T(8,128)(2,1)} %copy.89), calls=%async_computation.1 | async-start | bytes 786432 | tf_op jit(solution)/shard_map/all_to_all | solution.py:126
  254.6 3.5 copy-start.3
  254.6 3.5 copy-start.4
  254.7 3.5 copy-start.8
  254.7 99.6 %reduce-scatter.7.cloned.1.call-start = ((), (), s32[]{:S(2)}) async-start(), calls=%async_computation.7 | async-start | bytes 2506752
  274.5 119.1 %copy-start.1 = (bf16[4,48,288]{2,1,0:T(8,128)(2,1)S(1)}, bf16[4,48,288]{2,1,0:T(8,128)(2,1)}, u32[]{:S(2)}) copy-start(bf16[4,48,288]{2,1,0:T(8,128)(2,1)} %reduce-scatter.5.cloned.1.call-done) | copy-start | bytes 331780
  274.5 119.1 %copy-start.6 = (f32[288]{0:T(512)S(1)}, f32[288]{0:T(512)}, u32[]{:S(2)}) copy-start(f32[288]{0:T(512)} %param.21) | copy-start | bytes 3460
Sparse Core Ops, SparseCore 0:
  53.9 56.5 reduce-scatter.4
  112.9 60.7 all-gather.3
  187.4 45.3 all-gather.5
  274.6 79.5 reduce-scatter.6
where the time goes:
time: 402 us; the launch traced here: 401 us
  waiting for transfers between devices  242 us (60%)
  blocking collectives  56.4 us (14%)
  local copies, waits for them, and re-layouts  48.3 us (12%)
  matrix products  20 us (5%)
  between operations  13.5 us (3%)
  other arithmetic  10.5 us (3%)
  starting transfers between devices  10.4 us (3%)
    unnamed x5, waiting for transfers between devices  79.8 us
    reduce_scatter x1, waiting for transfers between devices, per_device(): lax.psum_scatter(partial_rows, 'prefix', scatter_dimension=1, tiled=True)  56.6 us
    all_gather x1, waiting for transfers between devices, per_device(): full_rows = lax.all_gather(embedded, 'branch', axis=2, tiled=True)  56.2 us
    all_gather x1, waiting for transfers between devices, per_device(): copies = lax.all_gather(send_slots, 'prefix', axis=0, tiled=True)  41.1 us
    psum x1, blocking collectives, per_device(): lax.psum(jnp.sum(own_block * own_block, axis=1, keepdims=True), 'branch')  38.1 us
    all_gather x1, blocking collectives, per_device(): ids_all = lax.all_gather(token_ids, 'prefix', axis=1, tiled=True)  18.3 us
    gather x1, local copies, waits for them, and re-layouts, per_device(): picked = jnp.take(table, jnp.clip(local_ids, 0, vocab_local - 1), axis=0)  16.4 us
    unnamed x25, local copies, waits for them, and re-layouts  13.8 us
  transfers between devices with their start and end apart: 6, of which 6 were waited for; matrix products, arithmetic and copies ran while one was open for 5% of the time, Pallas kernels for 0%

commit v1 on v0

v1 whole, which is shorter than its diff:
```python
import functools

import jax
import jax.numpy as jnp
from jax import lax
from jax.experimental import pallas as pl
from jax.experimental.pallas import tpu as pltpu
from jax.sharding import PartitionSpec as P

D = 4608
HEADS = 32
KV_HEADS = 16
HEAD = 128
SUF = 8
SOFT_CAP = 50.0
EPSILON = 1e-06
SCALE = float(D // HEADS) ** (-0.5)

RING = 16
STEPS = 4
ROWS = 48
TOKENS = STEPS * ROWS
SHARE = D // RING
TAIL = SHARE - 2 * HEAD
PACKED = 2 * TOKENS + ROWS
TAKE = 24
ROOM = 32
ENDS = ROOM + 16
SLOT = 8
GROUP = HEADS // KV_HEADS
PAIRS = STEPS * GROUP
WIDE = PAIRS * HEAD
BACK = WIDE + HEAD

F32 = jnp.float32
BF16 = jnp.bfloat16
VMEM = pl.BlockSpec(memory_space=pltpu.VMEM)
ANY = pl.BlockSpec(memory_space=pl.ANY)


def call(kernel, out_shape, args, flops=0, left=(), scratch=(), limit=24):
    nbytes = sum(a.size * a.dtype.itemsize for a in args)
    many = isinstance(out_shape, (list, tuple))
    return pl.pallas_call(
        kernel,
        out_shape=out_shape,
        in_specs=[ANY if n in left else VMEM for n in range(len(args))],
        out_specs=[VMEM] * len(out_shape) if many else VMEM,
        scratch_shapes=list(scratch),
        compiler_params=pltpu.CompilerParams(vmem_limit_bytes=limit * 1024 * 1024),
        cost_estimate=pl.CostEstimate(flops=flops, bytes_accessed=nbytes, transcendentals=0),
    )(*args)


def dot(a, b, contract=((1,), (0,))):
    return lax.dot_general(a, b, (contract, ((), ())), preferred_element_type=F32)


def iota(shape, axis):
    return lax.broadcasted_iota(jnp.int32, shape, axis)


def capped_exp(scores):
    return jnp.exp(SOFT_CAP * jnp.tanh(scores * (SCALE / SOFT_CAP)))


def lane_group(shape):
    return lax.shift_right_logical(iota(shape, 1), 5)


def column_of(row):
    n = row.shape[1]
    diagonal = iota((n, n), 0) == iota((n, n), 1)
    return jnp.sum(jnp.where(diagonal, row, 0), axis=1, keepdims=True)


def ask_kernel(vocab, ids_ref, prompt_ref, notes_ref, at_ref, columns_ref, lines_ref):
    def owner_of(ids):
        total = jnp.zeros(ids.shape, jnp.int32)
        for d in range(1, RING):
            total = total + (ids >= d * vocab).astype(jnp.int32)
        return total

    rows = [ids_ref[t : t + 1, :] for t in range(STEPS)]
    column = jnp.concatenate([column_of(row) for row in rows], axis=0)
    owner = owner_of(column)
    base = owner * vocab
    down = iota((TOKENS, ROWS), 0)
    over = iota((TOKENS, ROWS), 1)
    rank = jnp.zeros((TOKENS, ROWS), jnp.int32)
    new_rows = []
    for t in range(STEPS):
        seen = (column == rows[t]) & (down < over + t * ROWS)
        new = 1 - jnp.max(seen.astype(jnp.int32), axis=0, keepdims=True)
        new_rows.append(new)
        rank = rank + jnp.where((rows[t] >= base) & (rows[t] < column), new, 0)
    rank = jnp.sum(rank, axis=1, keepdims=True)
    fits = rank < TAKE
    at_ref[...] = jnp.where(fits, owner * TAKE + rank, -1)
    value = column - base + 1
    cell = jnp.where(fits, rank, -1) == iota((TOKENS, HEAD), 1)
    coarse = jnp.where(cell, lax.shift_right_logical(value, 6), 0).astype(F32).astype(BF16)
    fine = jnp.where(cell, value & 63, 0).astype(F32).astype(BF16)
    holders = iota((RING, ROWS), 0)
    high = jnp.zeros((RING, HEAD), F32)
    low = jnp.zeros((RING, HEAD), F32)
    for t in range(STEPS):
        part = slice(t * ROWS, (t + 1) * ROWS)
        mine = jnp.where(owner_of(rows[t]) == holders, new_rows[t], 0).astype(F32).astype(BF16)
        high = high + dot(mine, coarse[part])
        low = low + dot(mine, fine[part])
    asked = high.astype(jnp.int32) * 64 + low.astype(jnp.int32) - 1

    prompt = prompt_ref[...]
    prompt_column = column_of(prompt)
    holder = lax.shift_right_logical(prompt, 1)
    holder_column = lax.shift_right_logical(prompt_column, 1)
    down = iota((ROWS, ROWS), 0)
    over = iota((ROWS, ROWS), 1)
    same = holder == holder_column
    turn = jnp.sum((same & (down < over)).astype(jnp.int32), axis=0, keepdims=True)
    turn_column = jnp.sum((same & (over < down)).astype(jnp.int32), axis=1, keepdims=True)
    mine = (holder == holders).astype(F32).astype(BF16)
    odd = jnp.where(turn_column + ROOM == iota((ROWS, HEAD), 1), prompt_column & 1, 0)
    odds = dot(mine, odd.astype(F32).astype(BF16)).astype(jnp.int32)
    lane = iota((RING, HEAD), 1)
    notes = jnp.where(lane < ROOM, asked, odds)
    most = jnp.max(rank, axis=0, keepdims=True) + 1
    notes = jnp.where(lane == ENDS, most, notes)
    most = jnp.max(turn_column, axis=0, keepdims=True) + 1
    notes_ref[...] = jnp.where(lane == ENDS + 1, most, notes)

    def slots(holder, turn):
        now = jnp.where(turn < SLOT, holder * SLOT + turn, -1)
        later = jnp.where(turn >= SLOT, holder * SLOT + turn - SLOT, -1)
        return now, later

    columns_ref[...] = jnp.concatenate(slots(holder_column, turn_column), axis=1)
    lines_ref[...] = jnp.concatenate(slots(holder, turn), axis=0)


PIECE = 1024


def pick_kernel(notes_ref, rest_ref, table_ref, out_ref, held_ref, done):
    whole = held_ref.shape[1]
    copies = []
    for start in range(0, whole, PIECE):
        part = pl.ds(start, min(PIECE, whole - start))
        copy = pltpu.make_async_copy(
            table_ref.at[:, part], held_ref.at[:, part], done.at[start // PIECE]
        )
        copy.start()
        copies.append(copy)
    group = lane_group((1, HEAD))
    blocks = []
    for first in range(0, RING, 4):
        block = jnp.full((1, HEAD), -1, jnp.int32)
        for i in range(4):
            row = notes_ref[first + i : first + i + 1, :]
            row = pltpu.roll(row, ROOM * i, 1) if i else row
            block = jnp.where(group == i, row, block)
        blocks.append(block)
    ids = jnp.concatenate(blocks, axis=1)
    count = RING * ROOM
    step = 256
    lines = iota((step, count), 0).astype(F32).astype(BF16)

    def picked(start, rows):
        size = rows.shape[1]
        hots = []
        for at in range(start, start + size, step):
            here = (ids >= at) & (ids < at + step)
            near = jnp.where(here, ids - at, -1).astype(F32).astype(BF16)
            some = lines[: min(step, start + size - at)]
            hots.append(jnp.where(some == near, jnp.ones((), BF16), jnp.zeros((), BF16)))
        return dot(rows, jnp.concatenate(hots, axis=0) if len(hots) > 1 else hots[0])

    total = picked(whole, rest_ref[...])
    for start in range(0, whole, PIECE):
        copies[start // PIECE].wait()
        total = total + picked(start, held_ref[:, start : min(start + PIECE, whole)])
    total = total.T
    for d in range(RING):
        out_ref[d] = total[d * ROOM : d * ROOM + TAKE].astype(BF16)


def pack(rows, packed_ref):
    low = rows[:, :HEAD].astype(BF16)
    high = rows[:, HEAD : 2 * HEAD].astype(BF16)
    tail = jnp.concatenate([rows[:, 2 * HEAD :], jnp.zeros((TOKENS, HEAD - TAIL), F32)], axis=1)
    mixed = tail[:ROWS]
    for t in range(1, STEPS):
        mixed = mixed + pltpu.roll(tail[t * ROWS : (t + 1) * ROWS], TAIL * t, 1)
    mixed = mixed.astype(BF16)
    for b in range(RING):
        packed_ref[b, :TOKENS, :] = low
        packed_ref[b, TOKENS : 2 * TOKENS, :] = high
        packed_ref[b, 2 * TOKENS :, :] = mixed


def unpack_kernel(at_ref, got_ref, out_ref, packed_ref):
    hot = (at_ref[...] == iota((TOKENS, RING * TAKE), 1)).astype(F32).astype(BF16)
    rows = dot(hot, got_ref[...])
    out_ref[...] = rows.astype(BF16)
    pack(rows, packed_ref)


def pack_kernel(rows_ref, packed_ref):
    pack(rows_ref[...].astype(F32), packed_ref)


def normed_times(all_ref, gain_ref, weights):
    group = lane_group((ROWS, HEAD))
    squares = jnp.zeros((TOKENS, HEAD), F32)
    tail_squares = jnp.zeros((ROWS, HEAD), F32)
    product = jnp.zeros((TOKENS, 2 * HEAD), F32)
    tail_blocks, tail_weights = [], []
    for b in range(RING):
        low = all_ref[b, :TOKENS, :].astype(F32)
        high = all_ref[b, TOKENS : 2 * TOKENS, :].astype(F32)
        tail = all_ref[b, 2 * TOKENS :, :].astype(F32)
        main_weights, more_weights = weights(b)
        squares = squares + (low * low + high * high)
        tail_squares = tail_squares + tail * tail
        both = jnp.concatenate(
            [
                (low * gain_ref[0, b : b + 1, :]).astype(BF16),
                (high * gain_ref[1, b : b + 1, :]).astype(BF16),
            ],
            axis=1,
        )
        product = product + dot(both, main_weights)
        tail_weights.append(more_weights)
        scaled = tail * gain_ref[2, b : b + 1, :]
        place = b % 4
        if place == 0:
            tail_blocks.append([jnp.zeros((ROWS, HEAD), F32) for _ in range(STEPS)])
        for t in range(STEPS):
            shift = (TAIL * (place - t)) % HEAD
            moved = pltpu.roll(scaled, shift, 1) if shift else scaled
            tail_blocks[-1][t] = jnp.where(group == place, moved, tail_blocks[-1][t])
    tails = jnp.concatenate(
        [jnp.concatenate(block, axis=0).astype(BF16) for block in tail_blocks], axis=1
    )
    product = product + dot(tails, jnp.concatenate(tail_weights, axis=0))
    total = jnp.sum(squares, axis=1, keepdims=True) + jnp.concatenate(
        [
            jnp.sum(jnp.where(group == t, tail_squares, 0.0), axis=1, keepdims=True)
            for t in range(STEPS)
        ],
        axis=0,
    )
    return product * lax.rsqrt(total * (1.0 / D) + EPSILON)


def rotary(u, cos_ref, sin_ref):
    return u * cos_ref[...] + pltpu.roll(u, HEAD // 2, 1) * sin_ref[...]


def query_kernel(
    all_ref, gain_ref, cos_ref, sin_ref, slot_ref, wq_ref, q_ref, send_ref, held_ref, done
):
    copies = []
    for b in range(RING):
        rows = pl.ds(b * SHARE, SHARE)
        copies.append(pltpu.make_async_copy(wq_ref.at[rows, :], held_ref.at[b], done.at[b]))
        copies[-1].start()

    def weights(b):
        copies[b].wait()
        return held_ref[b, : 2 * HEAD, :], held_ref[b, 2 * HEAD :, :]

    query = normed_times(all_ref, gain_ref, weights)
    turned = jnp.concatenate(
        [
            rotary(query[:, :HEAD], cos_ref, sin_ref).astype(BF16),
            rotary(query[:, HEAD:], cos_ref, sin_ref).astype(BF16),
        ],
        axis=1,
    )
    q_ref[...] = turned
    wide = jnp.concatenate([turned[t * ROWS : (t + 1) * ROWS] for t in range(STEPS)], axis=1)
    hot = (iota((RING * SLOT, ROWS), 0) == slot_ref[0:1, :]).astype(F32).astype(BF16)
    send_ref[...] = dot(hot, wide).astype(BF16)


def place_kernel(q_ref, slot_ref, send_ref):
    turned = q_ref[...]
    wide = jnp.concatenate([turned[t * ROWS : (t + 1) * ROWS] for t in range(STEPS)], axis=1)
    hot = (iota((RING * SLOT, ROWS), 0) == slot_ref[1:2, :]).astype(F32).astype(BF16)
    send_ref[...] = dot(hot, wide).astype(BF16)


def prefix_kernel(turn, own_ref, notes_ref, keys_ref, values_ref, out_ref):
    lanes = iota((RING, SLOT, HEAD), 2) - (ROOM + turn) == iota((RING, SLOT, HEAD), 1)
    notes = jnp.where(lanes, notes_ref[...][:, None, :], 0).reshape(RING * SLOT, HEAD)
    odd = jnp.sum(notes, axis=1, keepdims=True) == 1
    keys = jnp.concatenate([keys_ref[0], keys_ref[1]], axis=1)
    values = jnp.concatenate([values_ref[0], values_ref[1]], axis=1)
    slots = RING * SLOT
    lanes = iota((slots, HEAD), 1)
    denoms = jnp.zeros((slots, HEAD), F32)
    batch = 4
    for first in range(0, PAIRS, batch):
        some = range(first, first + batch)
        parts = []
        for i in some:
            q = own_ref[:, i * HEAD : (i + 1) * HEAD].astype(F32)
            parts.append(
                jnp.concatenate(
                    [jnp.where(odd, 0.0, q).astype(BF16), jnp.where(odd, q, 0.0).astype(BF16)],
                    axis=1,
                )
            )
        scores = dot(jnp.concatenate(parts, axis=0), keys, ((1,), (1,)))
        weights = capped_exp(scores).astype(BF16)
        numer = dot(weights, values)
        denom = jnp.sum(weights.astype(F32), axis=1, keepdims=True)
        for n, i in enumerate(some):
            part = numer[n * slots : (n + 1) * slots]
            out_ref[:, i * HEAD : (i + 1) * HEAD] = jnp.where(
                odd, part[:, HEAD:], part[:, :HEAD]
            ).astype(BF16)
            denoms = jnp.where(lanes == i, denom[n * slots : (n + 1) * slots], denoms)
    out_ref[:, WIDE:] = denoms.astype(BF16)


def local_kernel(
    all_ref, gain_ref, cos_ref, sin_ref, wkv_ref, q_ref, sk_ref, sv_ref, len_ref, out_ref
):
    def weights(b):
        start = b * SHARE
        return [
            jnp.concatenate([wkv_ref[0, rows, :], wkv_ref[1, rows, :]], axis=1)
            for rows in (
                slice(start, start + 2 * HEAD),
                slice(start + 2 * HEAD, start + SHARE),
            )
        ]

    keyval = normed_times(all_ref, gain_ref, weights)
    new_keys = rotary(keyval[:, :HEAD], cos_ref, sin_ref).astype(BF16)
    new_values = keyval[:, HEAD:].astype(BF16)
    suffix = ROWS * SUF
    keys = jnp.concatenate([sk_ref[...], new_keys], axis=0)
    values = jnp.concatenate([sv_ref[...], new_values], axis=0)
    columns = suffix + TOKENS
    column = iota((ROWS, columns), 1)
    row = iota((ROWS, columns), 0)
    first = row * SUF
    in_suffix = (column >= first) & (column < first + len_ref[...])
    lanes = iota((ROWS, HEAD), 1)
    denoms = jnp.zeros((ROWS, HEAD), F32)
    usable = in_suffix
    for t in range(STEPS):
        usable = usable | (column == row + (suffix + t * ROWS))
        for g in range(GROUP):
            i = t * GROUP + g
            q = q_ref[t * ROWS : (t + 1) * ROWS, g * HEAD : (g + 1) * HEAD]
            scores = dot(q, keys, ((1,), (1,)))
            weights = jnp.where(usable, capped_exp(scores), 0.0).astype(BF16)
            out_ref[:, i * HEAD : (i + 1) * HEAD] = dot(weights, values)
            denom = jnp.sum(weights.astype(F32), axis=1, keepdims=True)
            denoms = jnp.where(lanes == i, denom, denoms)
    out_ref[:, WIDE:] = denoms


def select_kernel(slot_ref, back_ref, local_ref, out_ref):
    hot = (slot_ref[:, 1:2] == iota((ROWS, RING * SLOT), 1)).astype(F32).astype(BF16)
    out_ref[...] = dot(hot, back_ref[...]) + local_ref[...]


def output_kernel(slot_ref, back_ref, local_ref, w_ref, out_ref):
    hot = (slot_ref[:, 0:1] == iota((ROWS, RING * SLOT), 1)).astype(F32).astype(BF16)
    total = dot(hot, back_ref[...]) + local_ref[...]
    rows = []
    for t in range(STEPS):
        heads = []
        for g in range(GROUP):
            i = t * GROUP + g
            heads.append(
                (
                    total[:, i * HEAD : (i + 1) * HEAD] / total[:, WIDE + i : WIDE + i + 1]
                ).astype(BF16)
            )
        rows.append(jnp.concatenate(heads, axis=1))
    attended = jnp.concatenate(rows, axis=0)
    lanes = iota((TOKENS, HEAD), 1)
    group = lane_group((ROWS, HEAD))
    quad = 4 * SHARE
    for first in range(0, RING, 4):
        part = dot(attended, w_ref[:, first * SHARE : first * SHARE + quad])
        for i in range(4):
            b = first + i
            tiles = [part[:, (2 * i + n) * HEAD : (2 * i + n + 1) * HEAD] for n in range(3)]
            away = TAIL * i
            if away:
                moved = [pltpu.roll(tile, HEAD - away, 1) for tile in tiles]
                low = jnp.where(lanes < HEAD - away, moved[0], moved[1])
                high = jnp.where(lanes < HEAD - away, moved[1], moved[2])
            else:
                low, high = tiles[0], tiles[1]
            out_ref[b, :TOKENS, :] = low.astype(BF16)
            out_ref[b, TOKENS : 2 * TOKENS, :] = high.astype(BF16)
            mixed = jnp.zeros((ROWS, HEAD), F32)
            for t in range(STEPS):
                tail = tiles[2][t * ROWS : (t + 1) * ROWS]
                shift = (TAIL * (t - i)) % HEAD
                tail = pltpu.roll(tail, shift, 1) if shift else tail
                mixed = jnp.where(group == t, tail, mixed)
            out_ref[b, 2 * TOKENS :, :] = mixed.astype(BF16)


def reduce_kernel(parts_ref, sum_ref, squares_ref):
    total = parts_ref[0].astype(F32)
    for b in range(1, RING):
        total = total + parts_ref[b].astype(F32)
    sum_ref[...] = total
    low, high, tail = total[:TOKENS], total[TOKENS : 2 * TOKENS], total[2 * TOKENS :]
    group = lane_group((ROWS, HEAD))
    squares = jnp.sum(low * low + high * high, axis=1, keepdims=True) + jnp.concatenate(
        [
            jnp.sum(jnp.where(group == t, tail * tail, 0.0), axis=1, keepdims=True)
            for t in range(STEPS)
        ],
        axis=0,
    )
    diagonal = iota((HEAD, HEAD), 0) == iota((HEAD, HEAD), 1)
    one = jnp.sum(jnp.where(diagonal, squares[:HEAD], 0.0), axis=0, keepdims=True)
    rest = TOKENS - HEAD
    two = jnp.sum(jnp.where(diagonal[:rest], squares[HEAD:], 0.0), axis=0, keepdims=True)
    line = jnp.concatenate([one, two], axis=0)
    for b in range(RING):
        squares_ref[b] = line


def finish_kernel(squares_ref, sum_ref, rows_ref, gain_ref, out_ref):
    line = squares_ref[0]
    for b in range(1, RING):
        line = line + squares_ref[b]
    line = lax.rsqrt(line * (1.0 / D) + EPSILON)
    diagonal = iota((HEAD, HEAD), 0) == iota((HEAD, HEAD), 1)
    rest = TOKENS - HEAD
    one = jnp.sum(jnp.where(diagonal, line[0:1], 0.0), axis=1, keepdims=True)
    two = jnp.sum(jnp.where(diagonal[:rest], line[1:2], 0.0), axis=1, keepdims=True)
    root = jnp.concatenate([one, two], axis=0)
    rows = rows_ref[...].astype(F32)
    gain = gain_ref[...]
    total = sum_ref[...]
    low = total[:TOKENS] * root * gain[:, :HEAD]
    high = total[TOKENS : 2 * TOKENS] * root * gain[:, HEAD : 2 * HEAD]
    tails = []
    for t in range(STEPS):
        tail = total[2 * TOKENS :]
        tails.append(pltpu.roll(tail, HEAD - TAIL * t, 1) if t else tail)
    tail = jnp.concatenate(tails, axis=0)[:, :TAIL] * root * gain[:, 2 * HEAD :]
    scaled = jnp.concatenate([low, high, tail], axis=1)
    out_ref[...] = (rows + scaled).astype(BF16)


def exchange(x, axis):
    return lax.all_to_all(x, axis, split_axis=0, concat_axis=0, tiled=True)


def per_device(
    token_ids,
    prompt_of,
    suffix_len,
    table,
    pre_gain,
    w_query,
    w_keyval,
    w_out,
    post_gain,
    prefix_keys,
    prefix_values,
    suffix_keys,
    suffix_values,
):
    vocab = table.shape[0]
    prompt_len = prefix_keys.shape[1]
    shape = jax.ShapeDtypeStruct

    notes, at, slot_columns, slot_lines = call(
        functools.partial(ask_kernel, vocab),
        [
            shape((RING, HEAD), jnp.int32),
            shape((TOKENS, 1), jnp.int32),
            shape((ROWS, 2), jnp.int32),
            shape((2, ROWS), jnp.int32),
        ],
        (token_ids, prompt_of.reshape(1, ROWS)),
    )
    notes = exchange(notes.reshape(RING, 1, HEAD), "prefix").reshape(RING, HEAD)
    ends = jnp.max(notes[:, ENDS : ENDS + 2], axis=0)

    whole = vocab // 256 * 256
    picked = call(
        pick_kernel,
        shape((RING, TAKE, SHARE), BF16),
        (notes, table[whole:].T, table.T),
        flops=2 * vocab * RING * ROOM * SHARE,
        left=(2,),
        scratch=(
            pltpu.VMEM((SHARE, whole), BF16),
            pltpu.SemaphoreType.DMA((-(-whole // PIECE),)),
        ),
    )
    got = exchange(picked, "prefix").reshape(RING * TAKE, SHARE)
    own = shape((TOKENS, SHARE), BF16), shape((RING, PACKED, HEAD), BF16)
    placed = tuple(call(unpack_kernel, list(own), (at, got)))

    def take_all(_):
        everyone = exchange(jnp.broadcast_to(token_ids, (RING, STEPS, ROWS)), "prefix")
        inside_at = everyone - lax.axis_index("prefix") * vocab
        inside = (inside_at >= 0) & (inside_at < vocab)
        rows = jnp.take(table, jnp.clip(inside_at, 0, vocab - 1), axis=0)
        rows = jnp.where(inside[..., None], rows, jnp.zeros_like(rows))
        rows = exchange(rows, "prefix").astype(F32).sum(axis=0).astype(BF16)
        rows = rows.reshape(TOKENS, SHARE)
        return rows, call(pack_kernel, own[1], (rows,))

    embedded, packed = lax.cond(ends[0] > TAKE, take_all, lambda placed: placed, placed)
    everywhere = exchange(packed, "branch")

    half = HEAD // 2
    frequency = 10000.0 ** (-(jnp.arange(half, dtype=F32) * 2.0 / HEAD))
    positions = (prompt_len + suffix_len[None, :] + jnp.arange(STEPS)[:, None]).astype(F32)
    angles = positions.reshape(TOKENS, 1) * frequency
    cosines = jnp.cos(angles)
    sines = jnp.sin(angles)
    cosines = jnp.concatenate([cosines, cosines], axis=1)
    sines = jnp.concatenate([-sines, sines], axis=1)
    gains = pre_gain.reshape(RING, SHARE)
    gains = jnp.stack(
        [gains[:, :HEAD], gains[:, HEAD : 2 * HEAD], jnp.tile(gains[:, 2 * HEAD :], (1, 4))]
    )
    queries, sent = call(
        query_kernel,
        [shape((TOKENS, GROUP * HEAD), BF16), shape((RING * SLOT, WIDE), BF16)],
        (everywhere, gains, cosines, sines, slot_lines, w_query),
        flops=2 * TOKENS * D * 2 * HEAD,
        left=(5,),
        scratch=(
            pltpu.VMEM((RING, SHARE, GROUP * HEAD), BF16),
            pltpu.SemaphoreType.DMA((RING,)),
        ),
    )

    def ask(sent):
        return exchange(sent.reshape(RING, SLOT, WIDE), "prefix").reshape(RING * SLOT, WIDE)

    def answer(own, turn):
        sums = call(
            functools.partial(prefix_kernel, turn),
            shape((RING * SLOT, BACK), BF16),
            (own, notes, prefix_keys, prefix_values),
            flops=8 * RING * SLOT * prompt_len * WIDE,
        )
        return exchange(sums.reshape(RING, SLOT, BACK), "prefix").reshape(RING * SLOT, BACK)

    own = ask(sent)
    local = call(
        local_kernel,
        shape((ROWS, BACK), F32),
        (
            everywhere,
            gains,
            cosines,
            sines,
            w_keyval,
            queries,
            suffix_keys.reshape(ROWS * SUF, HEAD),
            suffix_values.reshape(ROWS * SUF, HEAD),
            suffix_len.reshape(ROWS, 1),
        ),
        flops=2 * TOKENS * D * 2 * HEAD + 4 * ROWS * WIDE * (ROWS * SUF + TOKENS),
    )
    own, local = lax.optimization_barrier((own, local))

    def second_round(local):
        sent = call(
            place_kernel,
            shape((RING * SLOT, WIDE), BF16),
            (queries, slot_lines),
        )
        back = answer(ask(sent), SLOT)
        return call(
            select_kernel,
            shape((ROWS, BACK), F32),
            (slot_columns, back, local),
        )

    local = lax.cond(ends[1] > SLOT, second_round, lambda local: local, local)
    own, local = lax.optimization_barrier((own, local))
    back = answer(own, 0)

    shares = call(
        output_kernel,
        shape((RING, PACKED, HEAD), BF16),
        (slot_columns, back, local, w_out),
        flops=2 * TOKENS * GROUP * HEAD * D,
    )
    shares = exchange(shares, "branch")
    total, squares = call(
        reduce_kernel,
        [shape((PACKED, HEAD), F32), shape((RING, 2, HEAD), F32)],
        (shares,),
    )
    squares = exchange(squares, "branch")
    layer_out = call(
        finish_kernel,
        shape((TOKENS, SHARE), BF16),
        (squares, total, embedded, post_gain.reshape(1, SHARE)),
    )
    return layer_out.reshape(STEPS, ROWS, SHARE)


def solution(mesh):
    placed = (
        P(None, "prefix"),
        P("prefix", None),
        P("prefix"),
        P("prefix", "branch"),
        P(),
        P(None, "branch"),
        P(None, None, "branch"),
        P("branch", None),
        P("branch"),
        P("prefix", None, "branch"),
        P("prefix", None, "branch"),
        P("prefix", None, "branch"),
        P("prefix", None, "branch"),
    )
    return jax.shard_map(
        per_device,
        mesh=mesh,
        in_specs=placed,
        out_specs=P(None, "prefix", "branch"),
        check_vma=False,
    )
```

time: 402 us -> 164 us (0.41)
  waiting for transfers between devices: 242 us -> 53.7 us
  local copies, waits for them, and re-layouts: 48.3 us -> 5.91 us
  Pallas kernels: 0 us -> 24.5 us
  starting transfers between devices: 10.4 us -> 30.8 us
  matrix products: 20 us -> 0 us
  blocking collectives: 56.4 us -> 43.9 us
  between operations: 13.5 us -> 1.52 us
  other arithmetic: 10.5 us -> 0.65 us
    all_gather x2 -> x0, waiting for transfers between devices: 97.2 us -> none  [the longest x1 56.2 us: per_device(): full_rows = lax.all_gather(embedded, 'branch', axis=2, tiled=True)]
    unnamed x5 -> x0, waiting for transfers between devices: 79.8 us -> none
    reduce_scatter x1 -> x0, waiting for transfers between devices: 56.6 us -> none  [per_device(): lax.psum_scatter(partial_rows, 'prefix', scatter_dimension=1, tiled=True)]
    all_to_all x2 -> x5, waiting for transfers between devices: 8.21 us -> 53.7 us  [exchange(): return lax.all_to_all(x, axis, split_axis=0, concat_axis=0, tiled=True)]
    all_to_all x0 -> x2, blocking collectives: none -> 43.9 us  [exchange(): return lax.all_to_all(x, axis, split_axis=0, concat_axis=0, tiled=True)]
    psum x1 -> x0, blocking collectives: 38.1 us -> none  [per_device(): lax.psum(jnp.sum(own_block * own_block, axis=1, keepdims=True), 'branch')]
    pallas_call x0 -> x9, Pallas kernels: none -> 24.5 us  [call(): pl.pallas_call(kernel, out_shape=out_shape, in_specs=[ANY if n in left el...]
    all_to_all x2 -> x5, starting transfers between devices: 10.1 us -> 30.8 us  [exchange(): return lax.all_to_all(x, axis, split_axis=0, concat_axis=0, tiled=True)]
  transfers between devices with their start and end apart: 6 -> 5, of which waited for: 6 -> 5; matrix products, arithmetic and copies ran while one was open for 5% -> 2% of each run, Pallas kernels for 0% -> 2%
where the time goes in v1:
time: 164 us; the launch traced here: 161 us
  waiting for transfers between devices  53.7 us (33%)
  blocking collectives  43.9 us (27%)
  starting transfers between devices  30.8 us (19%)
  Pallas kernels  24.5 us (15%)
  local copies, waits for them, and re-layouts  5.91 us (4%)
    all_to_all x5, waiting for transfers between devices, exchange(): return lax.all_to_all(x, axis, split_axis=0, concat_axis=0, tiled=True)  53.7 us
    all_to_all x2, blocking collectives, exchange(): return lax.all_to_all(x, axis, split_axis=0, concat_axis=0, tiled=True)  43.9 us
    all_to_all x5, starting transfers between devices, exchange(): return lax.all_to_all(x, axis, split_axis=0, concat_axis=0, tiled=True)  30.8 us
    pallas_call x9, Pallas kernels, call(): pl.pallas_call(kernel, out_shape=out_shape, in_specs=[ANY if n in left el...  24.5 us
    unnamed x22, local copies, waits for them, and re-layouts  4.01 us
  transfers between devices with their start and end apart: 5, of which 5 were waited for; matrix products, arithmetic and copies ran while one was open for 2% of the time, Pallas kernels for 2%

profile of v1, /device:TPU:32, one launch (start us, length us, event | category | flops | bytes accessed | tf_op | source)
XLA Modules:
  0.0 161.0 jit_solution(11762254855661248095)
XLA Ops:
  0.0 0.0 copy-start.5
  0.0 0.7 copy-done.5
  0.7 2.0 %shard_map.127 = (s32[16,128]{1,0:T(8,128)}, s32[192,1]{1,0:T(8,128)S(1)}, s32[48,2]{1,0:T(8,128)S(1)}, s32[2,48]{1,0:T(2,128)S(1)}) custom-call(s32[4,48]{1,0:T(4,128)} %ids_ref.1, s32[1,48]{1,0:T(1,128)S(1)} %bitcast.38), custom_call_target="tpu_custom_call" | custom-call | bytes 960 | tf_op jit(solution)/shard_map/pallas_call | solution.py:44
  2.6 8.6 %all-to-all-start.4 = ((s32[16,1,128]{2,1,0:T(1,128)}), s32[16,1,128]{2,1,0:T(1,128)S(1)}, u32[]{:S(2)}, u32[]{:S(2)}) async-start(s32[16,1,128]{2,1,0:T(1,128)} %bitcast.8), calls=%async_computation.4 | async-start | bytes 16384 | tf_op jit(solution)/shard_map/all_to_all | solution.py:463
  11.2 0.9 slice_bitcast_fusion.rest_ref
  12.1 5.2 %all-to-all-done.4 = s32[16,1,128]{2,1,0:T(1,128)S(1)} async-done(((s32[16,1,128]{2,1,0:T(1,128)}), s32[16,1,128]{2,1,0:T(1,128)S(1)}, u32[]{:S(2)}, u32[]{:S(2)}) %all-to-all-start.4) | async-done | bytes 8224 | tf_op jit(solution)/shard_map/all_to_all | solution.py:463
  17.3 0.0 copy-start.7
  17.3 5.0 %shard_map.128 = bf16[16,24,288]{2,1,0:T(8,128)(2,1)} custom-call(s32[16,128]{1,0:T(8,128)S(1)} %bitcast.41, bf16[288,64]{1,0:T(8,128)(2,1)S(1)} %slice_bitcast_fusion.rest_ref, bf16[288,8000]{1,0:T(8,128)(2,1)} %bitcast.40), custom_call_target="tpu_custom_call" | custom-call | flops 2359296000 | bytes 4653056 | tf_op jit(solution)/shard_map/pallas_call | solution.py:44
  22.3 4.8 %all-to-all-start.5 = ((bf16[16,24,288]{2,1,0:T(8,128)(2,1)}), bf16[16,24,288]{2,1,0:T(8,128)(2,1)S(1)}, u32[]{:S(2)}, u32[]{:S(2)}) async-start(bf16[16,24,288]{2,1,0:T(8,128)(2,1)} %shard_map.128), calls=%async_computation.5 | async-start | bytes 589824 | tf_op jit(solution)/shard_map/all_to_all | solution.py:463
  27.2 0.1 slice_reduce_fusion
  27.3 0.7 fusion.1
  28.6 8.8 %all-to-all-done.5 = bf16[16,24,288]{2,1,0:T(8,128)(2,1)S(1)} async-done(((bf16[16,24,288]{2,1,0:T(8,128)(2,1)}), bf16[16,24,288]{2,1,0:T(8,128)(2,1)S(1)}, u32[]{:S(2)}, u32[]{:S(2)}) %all-to-all-start.5) | async-done | bytes 221216 | tf_op jit(solution)/shard_map/all_to_all | solution.py:463
  37.4 1.7 %shard_map.129 = (bf16[192,288]{1,0:T(8,128)(2,1)}, bf16[16,432,128]{2,1,0:T(8,128)(2,1)}) custom-call(s32[192,1]{1,0:T(8,128)S(1)} %get-tuple-element.56.at_ref, bf16[384,288]{1,0:T(8,128)(2,1)S(1)} %bitcast.30), custom_call_target="tpu_custom_call" | custom-call | bytes 221952 | tf_op jit(solution)/shard_map/pallas_call | solution.py:44
  39.1 0.0 copy-done.7
  39.1 0.0 copy-start.9
  39.1 0.0 copy-start.6
  39.1 7.2 %all-to-all-start.6 = ((bf16[16,432,128]{2,1,0:T(8,128)(2,1)}), bf16[16,432,128]{2,1,0:T(8,128)(2,1)S(1)}, u32[]{:S(2)}, u32[]{:S(2)}) async-start(bf16[16,432,128]{2,1,0:T(8,128)(2,1)} %get-tuple-element.57), calls=%async_computation.6 | async-start | bytes 3538944 | tf_op jit(solution)/shard_map/all_to_all | solution.py:463
  46.3 0.0 copy-done.9
  46.3 0.1 convert_element_type.27
  46.4 0.0 copy-done.6
  46.4 0.1 reshape.106
  46.5 0.1 tile.9
  46.6 0.4 fusion
  47.0 0.1 pad_maximum_fusion
  47.1 27.8 %all-to-all-done.6.all_ref = bf16[16,432,128]{2,1,0:T(8,128)(2,1)S(1)} async-done(((bf16[16,432,128]{2,1,0:T(8,128)(2,1)}), bf16[16,432,128]{2,1,0:T(8,128)(2,1)S(1)}, u32[]{:S(2)}, u32[]{:S(2)}) %all-to-all-start.6) | async-done | bytes 1769504 | tf_op jit(solution)/shard_map/all_to_all | solution.py:463
  75.0 0.0 copy-start
  75.0 1.7 %copy-done = bf16[4608,256]{1,0:T(8,128)(2,1)S(1)} copy-done((bf16[4608,256]{1,0:T(8,128)(2,1)S(1)}, bf16[4608,256]{1,0:T(8,128)(2,1)}, u32[]{:S(2)}) %copy-start) | copy-done | bytes 2359320
  76.6 0.0 copy-start.3
  76.6 0.0 copy-start.4
  76.6 6.3 %shard_map.130 = (bf16[192,256]{1,0:T(8,128)(2,1)S(1)}, bf16[128,1024]{1,0:T(8,128)(2,1)}) custom-call(bf16[16,432,128]{2,1,0:T(8,128)(2,1)S(1)} %all-to-all-done.6.all_ref, f32[3,16,128]{2,1,0:T(8,128)S(1)} %pad_maximum_fusion.2.gain_ref, f32[192,128]{1,0:T(8,128)S(1)} %get-tuple-element.82.cos_ref, f32[192,128]{1,0:T(8,128)S(1)} %get-tuple-element.83.sin_ref, ...), custom_call_target="tpu_custom_call" | custom-call | flops 452984832 | bytes 4350336 | tf_op jit(solution)/shard_map/pallas_call | solution.py:44
  83.0 6.8 %all-to-all-start.7 = ((bf16[16,8,1024]{2,1,0:T(8,128)(2,1)}), bf16[16,8,1024]{2,1,0:T(8,128)(2,1)S(1)}, u32[]{:S(2)}, u32[]{:S(2)}) async-start(bf16[16,8,1024]{2,1,0:T(8,128)(2,1)} %bitcast.16), calls=%async_computation.7 | async-start | bytes 524288 | tf_op jit(solution)/shard_map/all_to_all | solution.py:463
  89.7 0.1 copy.18.len_ref
  90.5 0.0 copy-done.3
  90.5 0.0 copy-done.4
  90.5 0.0 copy-start.1
  90.5 1.7 %copy-done.1 = bf16[2,4608,128]{2,1,0:T(8,128)(2,1)S(1)} copy-done((bf16[2,4608,128]{2,1,0:T(8,128)(2,1)S(1)}, bf16[2,4608,128]{2,1,0:T(8,128)(2,1)}, u32[]{:S(2)}) %copy-start.1) | copy-done | bytes 2359320
  92.2 0.0 copy-start.10
  92.2 2.9 %shard_map.131 = f32[48,1152]{1,0:T(8,128)S(1)} custom-call(bf16[16,432,128]{2,1,0:T(8,128)(2,1)S(1)} %all-to-all-done.6.all_ref, f32[3,16,128]{2,1,0:T(8,128)S(1)} %pad_maximum_fusion.2.gain_ref, f32[192,128]{1,0:T(8,128)S(1)} %get-tuple-element.82.cos_ref, f32[192,128]{1,0:T(8,128)S(1)} %get-tuple-element.83.sin_ref, bf16[2,4608,128]{2,1,0:T(8,128)(2,1)S(1)} %copy-done.1, ...), custom_call_target="tpu_custom_call" | custom-call | flops 566231040 | bytes 4645056 | tf_op jit(solution)/shard_map/pallas_call | solution.py:44
  95.2 4.3 %all-to-all-done.7 = bf16[16,8,1024]{2,1,0:T(8,128)(2,1)S(1)} async-done(((bf16[16,8,1024]{2,1,0:T(8,128)(2,1)}), bf16[16,8,1024]{2,1,0:T(8,128)(2,1)S(1)}, u32[]{:S(2)}, u32[]{:S(2)}) %all-to-all-start.7) | async-done | bytes 262176 | tf_op jit(solution)/shard_map/all_to_all | solution.py:463
  99.4 0.0 copy-done.10
  99.4 0.0 copy-start.2
  99.4 2.7 %shard_map.132 = bf16[128,1152]{1,0:T(8,128)(2,1)S(1)} custom-call(bf16[128,1024]{1,0:T(8,128)(2,1)S(1)} %bitcast.34, s32[16,128]{1,0:T(8,128)S(1)} %bitcast.44, bf16[2,1024,128]{2,1,0:T(8,128)(2,1)S(1)} %copy-done.10, bf16[2,1024,128]{2,1,0:T(8,128)(2,1)} %values_ref.1), custom_call_target="tpu_custom_call" | custom-call | flops 1073741824 | bytes 1318912 | tf_op jit(solution)/shard_map/pallas_call | solution.py:44
  102.1 14.9 %all_to_all.53 = bf16[16,8,1152]{2,1,0:T(8,128)(2,1)S(1)} all-to-all(bf16[16,8,1152]{2,1,0:T(8,128)(2,1)S(1)} %bitcast.33), channel_id=1, replica_groups=mesh['prefix'=16,'branch'=16] {'prefix'}, dimensions={0} | all-to-all | bytes 589824 | tf_op jit(solution)/shard_map/all_to_all | solution.py:463
  117.0 0.0 copy-done.2
  117.0 1.1 shard_map.133
  118.1 0.0 copy-start.8
  118.1 29.0 %all_to_all.54.parts_ref = bf16[16,432,128]{2,1,0:T(8,128)(2,1)S(1)} all-to-all(bf16[16,432,128]{2,1,0:T(8,128)(2,1)S(1)} %shard_map.133), channel_id=1, replica_groups=mesh['prefix'=16,'branch'=16] {'branch'}, dimensions={0} | all-to-all | bytes 3538944 | tf_op jit(solution)/shard_map/all_to_all | solution.py:463
  147.1 1.0 shard_map.134
  148.2 3.5 %all-to-all-start.10 = ((f32[16,2,128]{2,1,0:T(2,128)}), f32[16,2,128]{2,1,0:T(2,128)S(1)}, u32[]{:S(2)}, u32[]{:S(2)}) async-start(f32[16,2,128]{2,1,0:T(2,128)} %get-tuple-element.65), calls=%async_computation.10 | async-start | bytes 32768 | tf_op jit(solution)/shard_map/all_to_all | solution.py:463
  151.7 0.0 copy-done.8
  151.7 7.5 %all-to-all-done.10.squares_ref = f32[16,2,128]{2,1,0:T(2,128)S(1)} async-done(((f32[16,2,128]{2,1,0:T(2,128)}), f32[16,2,128]{2,1,0:T(2,128)S(1)}, u32[]{:S(2)}, u32[]{:S(2)}) %all-to-all-start.10) | async-done | bytes 16416 | tf_op jit(solution)/shard_map/all_to_all | solution.py:463
  159.2 1.8 %shard_map.135 = bf16[192,288]{1,0:T(8,128)(2,1)} custom-call(f32[16,2,128]{2,1,0:T(2,128)S(1)} %all-to-all-done.10.squares_ref, f32[432,128]{1,0:T(8,128)S(1)} %get-tuple-element.66.sum_ref, bf16[192,288]{1,0:T(8,128)(2,1)} %get-tuple-element.67.rows_ref, f32[1,288]{1,0:T(1,128)S(1)} %reshape.114.gain_ref), custom_call_target="tpu_custom_call" | custom-call | bytes 349312 | tf_op jit(solution)/shard_map/pallas_call | solution.py:44
  (10 shorter events, 0.0 us)
Async XLA Ops:
  0.0 0.7 copy-start.5
  2.6 14.7 %all-to-all-start.4 = ((s32[16,1,128]{2,1,0:T(1,128)}), s32[16,1,128]{2,1,0:T(1,128)S(1)}, u32[]{:S(2)}, u32[]{:S(2)}) async-start(s32[16,1,128]{2,1,0:T(1,128)} %bitcast.8), calls=%async_computation.4 | async-start | bytes 16384 | tf_op jit(solution)/shard_map/all_to_all | solution.py:463
  17.3 21.7 %copy-start.7 = (s32[4,48]{1,0:T(4,128)S(1)}, s32[4,48]{1,0:T(4,128)}, u32[]{:S(2)}) copy-start(s32[4,48]{1,0:T(4,128)} %ids_ref.1) | copy-start | bytes 2308
  22.3 15.1 %all-to-all-start.5 = ((bf16[16,24,288]{2,1,0:T(8,128)(2,1)}), bf16[16,24,288]{2,1,0:T(8,128)(2,1)S(1)}, u32[]{:S(2)}, u32[]{:S(2)}) async-start(bf16[16,24,288]{2,1,0:T(8,128)(2,1)} %shard_map.128), calls=%async_computation.5 | async-start | bytes 589824 | tf_op jit(solution)/shard_map/all_to_all | solution.py:463
  39.1 7.2 %copy-start.9 = (s32[48]{0:T(128)S(1)}, s32[48]{0:T(128)}, u32[]{:S(2)}) copy-start(s32[48]{0:T(128)} %param.19) | copy-start | bytes 580
  39.1 7.3 %copy-start.6 = (f32[4608]{0:T(1024)S(1)}, f32[4608]{0:T(1024)}, u32[]{:S(2)}) copy-start(f32[4608]{0:T(1024)} %param.21) | copy-start | bytes 55300
  39.1 35.9 %all-to-all-start.6 = ((bf16[16,432,128]{2,1,0:T(8,128)(2,1)}), bf16[16,432,128]{2,1,0:T(8,128)(2,1)S(1)}, u32[]{:S(2)}, u32[]{:S(2)}) async-start(bf16[16,432,128]{2,1,0:T(8,128)(2,1)} %get-tuple-element.57), calls=%async_computation.6 | async-start | bytes 3538944 | tf_op jit(solution)/shard_map/all_to_all | solution.py:463
  75.0 1.7 %copy-start = (bf16[4608,256]{1,0:T(8,128)(2,1)S(1)}, bf16[4608,256]{1,0:T(8,128)(2,1)}, u32[]{:S(2)}) copy-start(bf16[4608,256]{1,0:T(8,128)(2,1)} %wq_ref.1) | copy-start | bytes 7077892
  76.6 13.9 %copy-start.3 = (bf16[48,8,128]{2,1,0:T(8,128)(2,1)S(1)}, bf16[48,8,128]{2,1,0:T(8,128)(2,1)}, u32[]{:S(2)}) copy-start(bf16[48,8,128]{2,1,0:T(8,128)(2,1)} %param.28) | copy-start | bytes 294916
  76.6 13.9 %copy-start.4 = (bf16[48,8,128]{2,1,0:T(8,128)(2,1)S(1)}, bf16[48,8,128]{2,1,0:T(8,128)(2,1)}, u32[]{:S(2)}) copy-start(bf16[48,8,128]{2,1,0:T(8,128)(2,1)} %param.29) | copy-start | bytes 294916
  83.0 16.5 %all-to-all-start.7 = ((bf16[16,8,1024]{2,1,0:T(8,128)(2,1)}), bf16[16,8,1024]{2,1,0:T(8,128)(2,1)S(1)}, u32[]{:S(2)}, u32[]{:S(2)}) async-start(bf16[16,8,1024]{2,1,0:T(8,128)(2,1)} %bitcast.16), calls=%async_computation.7 | async-start | bytes 524288 | tf_op jit(solution)/shard_map/all_to_all | solution.py:463
  90.5 1.7 %copy-start.1 = (bf16[2,4608,128]{2,1,0:T(8,128)(2,1)S(1)}, bf16[2,4608,128]{2,1,0:T(8,128)(2,1)}, u32[]{:S(2)}) copy-start(bf16[2,4608,128]{2,1,0:T(8,128)(2,1)} %wkv_ref.1) | copy-start | bytes 7077892
  92.2 7.2 %copy-start.10 = (bf16[2,1024,128]{2,1,0:T(8,128)(2,1)S(1)}, bf16[2,1024,128]{2,1,0:T(8,128)(2,1)}, u32[]{:S(2)}) copy-start(bf16[2,1024,128]{2,1,0:T(8,128)(2,1)} %keys_ref.1) | copy-start | bytes 1572868
  99.4 17.6 %copy-start.2 = (bf16[256,4608]{1,0:T(8,128)(2,1)S(1)}, bf16[256,4608]{1,0:T(8,128)(2,1)}, u32[]{:S(2)}) copy-start(bf16[256,4608]{1,0:T(8,128)(2,1)} %w_ref.1) | copy-start | bytes 7077892
  118.1 33.6 %copy-start.8 = (f32[288]{0:T(512)S(1)}, f32[288]{0:T(512)}, u32[]{:S(2)}) copy-start(f32[288]{0:T(512)} %param.25) | copy-start | bytes 3460
  148.2 11.0 %all-to-all-start.10 = ((f32[16,2,128]{2,1,0:T(2,128)}), f32[16,2,128]{2,1,0:T(2,128)S(1)}, u32[]{:S(2)}, u32[]{:S(2)}) async-start(f32[16,2,128]{2,1,0:T(2,128)} %get-tuple-element.65), calls=%async_computation.10 | async-start | bytes 32768 | tf_op jit(solution)/shard_map/all_to_all | solution.py:463

commit v2 on v1

--- a/solution.py
+++ b/solution.py
@@ -26,6 +26,8 @@
 TAKE = 24
 ROOM = 32
 ENDS = ROOM + 16
+COUNTS = 64
+ALL = 256
 SLOT = 8
 GROUP = HEADS // KV_HEADS
 PAIRS = STEPS * GROUP
@@ -35,16 +37,19 @@
 F32 = jnp.float32
 BF16 = jnp.bfloat16
 VMEM = pl.BlockSpec(memory_space=pltpu.VMEM)
+SMEM = pl.BlockSpec(memory_space=pltpu.SMEM)
 ANY = pl.BlockSpec(memory_space=pl.ANY)
 
 
-def call(kernel, out_shape, args, flops=0, left=(), scratch=(), limit=24):
+def call(kernel, out_shape, args, flops=0, scalars=0, left=(), scratch=(), limit=24):
     nbytes = sum(a.size * a.dtype.itemsize for a in args)
     many = isinstance(out_shape, (list, tuple))
     return pl.pallas_call(
         kernel,
         out_shape=out_shape,
-        in_specs=[ANY if n in left else VMEM for n in range(len(args))],
+        in_specs=[
+            SMEM if n < scalars else ANY if n in left else VMEM for n in range(len(args))
+        ],
         out_specs=[VMEM] * len(out_shape) if many else VMEM,
         scratch_shapes=list(scratch),
         compiler_params=pltpu.CompilerParams(vmem_limit_bytes=limit * 1024 * 1024),
@@ -104,9 +109,12 @@
     holders = iota((RING, ROWS), 0)
     high = jnp.zeros((RING, HEAD), F32)
     low = jnp.zeros((RING, HEAD), F32)
+    count = jnp.zeros((RING, ROWS), F32)
     for t in range(STEPS):
         part = slice(t * ROWS, (t + 1) * ROWS)
-        mine = jnp.where(owner_of(rows[t]) == holders, new_rows[t], 0).astype(F32).astype(BF16)
+        mine = jnp.where(owner_of(rows[t]) == holders, new_rows[t], 0).astype(F32)
+        count = count + mine
+        mine = mine.astype(BF16)
         high = high + dot(mine, coarse[part])
         low = low + dot(mine, fine[part])
     asked = high.astype(jnp.int32) * 64 + low.astype(jnp.int32) - 1
@@ -128,7 +136,13 @@
     most = jnp.max(rank, axis=0, keepdims=True) + 1
     notes = jnp.where(lane == ENDS, most, notes)
     most = jnp.max(turn_column, axis=0, keepdims=True) + 1
-    notes_ref[...] = jnp.where(lane == ENDS + 1, most, notes)
+    notes = jnp.where(lane == ENDS + 1, most, notes)
+    count = jnp.sum(count, axis=1, keepdims=True).astype(jnp.int32)
+    notes = jnp.where(lane == ENDS + 2, count, notes)
+    counts = jnp.where(lane == iota((RING, HEAD), 0) + COUNTS, count, 0)
+    counts = jnp.sum(counts, axis=0, keepdims=True)
+    listed = (lane >= COUNTS) & (lane < COUNTS + RING)
+    notes_ref[...] = jnp.where(listed, counts, notes)
 
     def slots(holder, turn):
         now = jnp.where(turn < SLOT, holder * SLOT + turn, -1)
@@ -139,10 +153,11 @@
     lines_ref[...] = jnp.concatenate(slots(holder, turn), axis=0)
 
 
+LONG = 20_000_000_000
 PIECE = 1024
 
 
-def pick_kernel(notes_ref, rest_ref, table_ref, out_ref, held_ref, done):
+def pick_kernel(counts_ref, notes_ref, rest_ref, table_ref, out_ref, held_ref, rows_ref, done):
     whole = held_ref.shape[1]
     copies = []
     for start in range(0, whole, PIECE):
@@ -152,17 +167,19 @@
         )
         copy.start()
         copies.append(copy)
-    group = lane_group((1, HEAD))
-    blocks = []
-    for first in range(0, RING, 4):
-        block = jnp.full((1, HEAD), -1, jnp.int32)
-        for i in range(4):
-            row = notes_ref[first + i : first + i + 1, :]
-            row = pltpu.roll(row, ROOM * i, 1) if i else row
-            block = jnp.where(group == i, row, block)
-        blocks.append(block)
-    ids = jnp.concatenate(blocks, axis=1)
-    count = RING * ROOM
+    lane = iota((8, HEAD), 1)
+    ids = jnp.zeros((8, ALL), jnp.int32)
+    start = 0
+    starts = []
+    for d in range(RING):
+        starts.append(start)
+        row = jnp.broadcast_to(notes_ref[d : d + 1, :], (8, HEAD))
+        row = jnp.where(lane < ROOM, row + 1, 0)
+        row = jnp.concatenate([row, jnp.zeros((8, ALL - HEAD), jnp.int32)], axis=1)
+        ids = ids + (pltpu.roll(row, start & (ALL - 1), 1) if d else row)
+        start = jnp.minimum(start + counts_ref[d, ENDS + 2], ALL)
+    ids = ids[0:1] - 1
+    count = ALL
     step = 256
     lines = iota((step, count), 0).astype(F32).astype(BF16)
 
@@ -180,9 +197,16 @@
     for start in range(0, whole, PIECE):
         copies[start // PIECE].wait()
         total = total + picked(start, held_ref[:, start : min(start + PIECE, whole)])
-    total = total.T
+    rows_ref[:ALL, :] = total.T
+    rows_ref[ALL:, :] = jnp.zeros((ROOM, SHARE), F32)
     for d in range(RING):
-        out_ref[d] = total[d * ROOM : d * ROOM + TAKE].astype(BF16)
+        if d:
+            whole_start = pl.multiple_of(starts[d] - (starts[d] & 7), 8)
+            some = rows_ref[pl.ds(whole_start, ROOM), :]
+            some = pltpu.roll(some, (ROOM - (starts[d] & 7)) & (ROOM - 1), 0)
+        else:
+            some = rows_ref[:ROOM, :]
+        out_ref[d] = some[:TAKE].astype(BF16)
 
 
 def pack(rows, packed_ref):
@@ -258,18 +282,10 @@
     return u * cos_ref[...] + pltpu.roll(u, HEAD // 2, 1) * sin_ref[...]
 
 
-def query_kernel(
-    all_ref, gain_ref, cos_ref, sin_ref, slot_ref, wq_ref, q_ref, send_ref, held_ref, done
-):
-    copies = []
-    for b in range(RING):
-        rows = pl.ds(b * SHARE, SHARE)
-        copies.append(pltpu.make_async_copy(wq_ref.at[rows, :], held_ref.at[b], done.at[b]))
-        copies[-1].start()
-
+def query_kernel(all_ref, gain_ref, cos_ref, sin_ref, slot_ref, wq_ref, q_ref, send_ref):
     def weights(b):
-        copies[b].wait()
-        return held_ref[b, : 2 * HEAD, :], held_ref[b, 2 * HEAD :, :]
+        start = b * SHARE
+        return wq_ref[start : start + 2 * HEAD, :], wq_ref[start + 2 * HEAD : start + SHARE, :]
 
     query = normed_times(all_ref, gain_ref, weights)
     turned = jnp.concatenate(
@@ -435,7 +451,18 @@
         squares_ref[b] = line
 
 
-def finish_kernel(squares_ref, sum_ref, rows_ref, gain_ref, out_ref):
+def scale_kernel(sum_ref, gain_ref, out_ref):
+    total = sum_ref[...]
+    tails = []
+    for t in range(STEPS):
+        tail = total[2 * TOKENS :]
+        tails.append(pltpu.roll(tail, HEAD - TAIL * t, 1) if t else tail)
+    tail = jnp.concatenate(tails, axis=0)[:, :TAIL]
+    placed = jnp.concatenate([total[:TOKENS], total[TOKENS : 2 * TOKENS], tail], axis=1)
+    out_ref[...] = placed * gain_ref[...]
+
+
+def finish_kernel(squares_ref, scaled_ref, rows_ref, out_ref):
     line = squares_ref[0]
     for b in range(1, RING):
         line = line + squares_ref[b]
@@ -445,18 +472,7 @@
     one = jnp.sum(jnp.where(diagonal, line[0:1], 0.0), axis=1, keepdims=True)
     two = jnp.sum(jnp.where(diagonal[:rest], line[1:2], 0.0), axis=1, keepdims=True)
     root = jnp.concatenate([one, two], axis=0)
-    rows = rows_ref[...].astype(F32)
-    gain = gain_ref[...]
-    total = sum_ref[...]
-    low = total[:TOKENS] * root * gain[:, :HEAD]
-    high = total[TOKENS : 2 * TOKENS] * root * gain[:, HEAD : 2 * HEAD]
-    tails = []
-    for t in range(STEPS):
-        tail = total[2 * TOKENS :]
-        tails.append(pltpu.roll(tail, HEAD - TAIL * t, 1) if t else tail)
-    tail = jnp.concatenate(tails, axis=0)[:, :TAIL] * root * gain[:, 2 * HEAD :]
-    scaled = jnp.concatenate([low, high, tail], axis=1)
-    out_ref[...] = (rows + scaled).astype(BF16)
+    out_ref[...] = (rows_ref[...].astype(F32) + scaled_ref[...] * root).astype(BF16)
 
 
 def exchange(x, axis):
@@ -494,36 +510,11 @@
     )
     notes = exchange(notes.reshape(RING, 1, HEAD), "prefix").reshape(RING, HEAD)
     ends = jnp.max(notes[:, ENDS : ENDS + 2], axis=0)
+    asked = jnp.max(jnp.sum(notes[:, COUNTS : COUNTS + RING], axis=0))
+    crowded = (ends[0] > TAKE) | (asked > ALL)
 
     whole = vocab // 256 * 256
-    picked = call(
-        pick_kernel,
-        shape((RING, TAKE, SHARE), BF16),
-        (notes, table[whole:].T, table.T),
-        flops=2 * vocab * RING * ROOM * SHARE,
-        left=(2,),
-        scratch=(
-            pltpu.VMEM((SHARE, whole), BF16),
-            pltpu.SemaphoreType.DMA((-(-whole // PIECE),)),
-        ),
-    )
-    got = exchange(picked, "prefix").reshape(RING * TAKE, SHARE)
-    own = shape((TOKENS, SHARE), BF16), shape((RING, PACKED, HEAD), BF16)
-    placed = tuple(call(unpack_kernel, list(own), (at, got)))
-
-    def take_all(_):
-        everyone = exchange(jnp.broadcast_to(token_ids, (RING, STEPS, ROWS)), "prefix")
-        inside_at = everyone - lax.axis_index("prefix") * vocab
-        inside = (inside_at >= 0) & (inside_at < vocab)
-        rows = jnp.take(table, jnp.clip(inside_at, 0, vocab - 1), axis=0)
-        rows = jnp.where(inside[..., None], rows, jnp.zeros_like(rows))
-        rows = exchange(rows, "prefix").astype(F32).sum(axis=0).astype(BF16)
-        rows = rows.reshape(TOKENS, SHARE)
-        return rows, call(pack_kernel, own[1], (rows,))
-
-    embedded, packed = lax.cond(ends[0] > TAKE, take_all, lambda placed: placed, placed)
-    everywhere = exchange(packed, "branch")
-
+    rest = table[whole:].T
     half = HEAD // 2
     frequency = 10000.0 ** (-(jnp.arange(half, dtype=F32) * 2.0 / HEAD))
     positions = (prompt_len + suffix_len[None, :] + jnp.arange(STEPS)[:, None]).astype(F32)
@@ -536,16 +527,45 @@
     gains = jnp.stack(
         [gains[:, :HEAD], gains[:, HEAD : 2 * HEAD], jnp.tile(gains[:, 2 * HEAD :], (1, 4))]
     )
+    lengths = suffix_len.reshape(ROWS, 1)
+    notes, rest, cosines, sines, gains, lengths = lax.optimization_barrier(
+        (notes, rest, cosines, sines, gains, lengths)
+    )
+    picked = call(
+        pick_kernel,
+        shape((RING, TAKE, SHARE), BF16),
+        (notes, notes, rest, table.T),
+        flops=2 * vocab * ALL * SHARE,
+        scalars=1,
+        left=(3,),
+        scratch=(
+            pltpu.VMEM((SHARE, whole), BF16),
+            pltpu.VMEM((ALL + ROOM, SHARE), F32),
+            pltpu.SemaphoreType.DMA((-(-whole // PIECE),)),
+        ),
+    )
+    got = exchange(picked, "prefix").reshape(RING * TAKE, SHARE)
+    own = shape((TOKENS, SHARE), BF16), shape((RING, PACKED, HEAD), BF16)
+    placed = tuple(call(unpack_kernel, list(own), (at, got), flops=LONG))
+
+    def take_all(_):
+        everyone = exchange(jnp.broadcast_to(token_ids, (RING, STEPS, ROWS)), "prefix")
+        inside_at = everyone - lax.axis_index("prefix") * vocab
+        inside = (inside_at >= 0) & (inside_at < vocab)
+        rows = jnp.take(table, jnp.clip(inside_at, 0, vocab - 1), axis=0)
+        rows = jnp.where(inside[..., None], rows, jnp.zeros_like(rows))
+        rows = exchange(rows, "prefix").astype(F32).sum(axis=0).astype(BF16)
+        rows = rows.reshape(TOKENS, SHARE)
+        return rows, call(pack_kernel, own[1], (rows,))
+
+    embedded, packed = lax.cond(crowded, take_all, lambda placed: placed, placed)
+    everywhere = exchange(packed, "branch")
+
     queries, sent = call(
         query_kernel,
         [shape((TOKENS, GROUP * HEAD), BF16), shape((RING * SLOT, WIDE), BF16)],
         (everywhere, gains, cosines, sines, slot_lines, w_query),
-        flops=2 * TOKENS * D * 2 * HEAD,
-        left=(5,),
-        scratch=(
-            pltpu.VMEM((RING, SHARE, GROUP * HEAD), BF16),
-            pltpu.SemaphoreType.DMA((RING,)),
-        ),
+        flops=LONG,
     )
 
     def ask(sent):
@@ -573,7 +593,7 @@
             queries,
             suffix_keys.reshape(ROWS * SUF, HEAD),
             suffix_values.reshape(ROWS * SUF, HEAD),
-            suffix_len.reshape(ROWS, 1),
+            lengths,
         ),
         flops=2 * TOKENS * D * 2 * HEAD + 4 * ROWS * WIDE * (ROWS * SUF + TOKENS),
     )
@@ -609,10 +629,13 @@
         (shares,),
     )
     squares = exchange(squares, "branch")
+    scaled = call(
+        scale_kernel, shape((TOKENS, SHARE), F32), (total, post_gain.reshape(1, SHARE))
+    )
     layer_out = call(
         finish_kernel,
         shape((TOKENS, SHARE), BF16),
-        (squares, total, embedded, post_gain.reshape(1, SHARE)),
+        (squares, scaled, embedded),
     )
     return layer_out.reshape(STEPS, ROWS, SHARE)
 

time: 164 us -> 155 us (0.945)
  blocking collectives: 43.9 us -> 76.3 us
  waiting for transfers between devices: 53.7 us -> 22.3 us
  starting transfers between devices: 30.8 us -> 23.5 us
  Pallas kernels: 24.5 us -> 20.5 us
    all_to_all x2 -> x3, blocking collectives: 43.9 us -> 76.3 us  [exchange(): return lax.all_to_all(x, axis, split_axis=0, concat_axis=0, tiled=True)]
    all_to_all x5 -> x4, waiting for transfers between devices: 53.7 us -> 22.3 us  [exchange(): return lax.all_to_all(x, axis, split_axis=0, concat_axis=0, tiled=True)]
    all_to_all x5 -> x4, starting transfers between devices: 30.8 us -> 23.5 us  [exchange(): return lax.all_to_all(x, axis, split_axis=0, concat_axis=0, tiled=True)]
    pallas_call x9 -> x10, Pallas kernels: 24.5 us -> 20.5 us  [call(): pl.pallas_call(kernel, out_shape=out_shape, in_specs=[SMEM if n < scalars...]
  transfers between devices with their start and end apart: 5 -> 4, of which waited for: 5 -> 4; matrix products, arithmetic and copies ran while one was open for 2% -> 3% of each run, Pallas kernels for 2% -> 2%
where the time goes in v2:
time: 155 us; the launch traced here: 153 us
  blocking collectives  76.3 us (49%)
  starting transfers between devices  23.5 us (15%)
  waiting for transfers between devices  22.3 us (14%)
  Pallas kernels  20.5 us (13%)
  local copies, waits for them, and re-layouts  6.14 us (4%)
  other arithmetic  2.03 us (1%)
  between operations  2.03 us (1%)
    all_to_all x3, blocking collectives, exchange(): return lax.all_to_all(x, axis, split_axis=0, concat_axis=0, tiled=True)  76.3 us
    all_to_all x4, starting transfers between devices, exchange(): return lax.all_to_all(x, axis, split_axis=0, concat_axis=0, tiled=True)  23.5 us
    all_to_all x4, waiting for transfers between devices, exchange(): return lax.all_to_all(x, axis, split_axis=0, concat_axis=0, tiled=True)  22.3 us
    pallas_call x10, Pallas kernels, call(): pl.pallas_call(kernel, out_shape=out_shape, in_specs=[SMEM if n < scalars...  20.5 us
    unnamed x22, local copies, waits for them, and re-layouts  3.59 us
  transfers between devices with their start and end apart: 4, of which 4 were waited for; matrix products, arithmetic and copies ran while one was open for 3% of the time, Pallas kernels for 2%

profile of v2, /device:TPU:32, one launch (start us, length us, event | category | flops | bytes accessed | tf_op | source)
XLA Modules:
  0.0 152.8 jit_solution(204145457233530337)
XLA Ops:
  0.0 0.0 copy-start.4
  0.0 0.7 copy-done.4
  0.7 2.0 %shard_map.127 = (s32[16,128]{1,0:T(8,128)}, s32[192,1]{1,0:T(8,128)S(1)}, s32[48,2]{1,0:T(8,128)S(1)}, s32[2,48]{1,0:T(2,128)S(1)}) custom-call(s32[4,48]{1,0:T(4,128)} %ids_ref.1, s32[1,48]{1,0:T(1,128)S(1)} %bitcast.38), custom_call_target="tpu_custom_call" | custom-call | bytes 960 | tf_op jit(solution)/shard_map/pallas_call | solution.py:47
  2.6 8.6 %all-to-all-start.4 = ((s32[16,1,128]{2,1,0:T(1,128)}), s32[16,1,128]{2,1,0:T(1,128)S(1)}, u32[]{:S(2)}, u32[]{:S(2)}) async-start(s32[16,1,128]{2,1,0:T(1,128)} %bitcast.8), calls=%async_computation.4 | async-start | bytes 16384 | tf_op jit(solution)/shard_map/all_to_all | solution.py:479
  11.2 0.8 reshape.103
  12.1 0.7 broadcast_add_fusion
  12.7 0.1 convert_element_type.23
  12.8 0.1 tile.9
  12.9 0.9 slice_bitcast_fusion.rest_ref
  13.8 0.4 fusion
  14.2 0.1 pad_maximum_fusion
  14.4 3.0 %all-to-all-done.4 = s32[16,1,128]{2,1,0:T(1,128)S(1)} async-done(((s32[16,1,128]{2,1,0:T(1,128)}), s32[16,1,128]{2,1,0:T(1,128)S(1)}, u32[]{:S(2)}, u32[]{:S(2)}) %all-to-all-start.4) | async-done | bytes 8224 | tf_op jit(solution)/shard_map/all_to_all | solution.py:479
  17.4 0.0 copy-start.7
  17.4 5.7 %shard_map.128 = bf16[16,24,288]{2,1,0:T(8,128)(2,1)} custom-call(s32[16,128]{1,0:T(8,128)S(1)} %bitcast.41, s32[16,128]{1,0:T(8,128)S(1)} %bitcast.42, bf16[288,64]{1,0:T(8,128)(2,1)S(1)} %slice_bitcast_fusion.rest_ref, bf16[288,8000]{1,0:T(8,128)(2,1)} %bitcast.39), custom_call_target="tpu_custom_call" | custom-call | flops 1179648000 | bytes 4661248 | tf_op jit(solution)/shard_map/pallas_call | solution.py:47
  23.1 4.8 %all-to-all-start.5 = ((bf16[16,24,288]{2,1,0:T(8,128)(2,1)}), bf16[16,24,288]{2,1,0:T(8,128)(2,1)S(1)}, u32[]{:S(2)}, u32[]{:S(2)}) async-start(bf16[16,24,288]{2,1,0:T(8,128)(2,1)} %shard_map.128), calls=%async_computation.5 | async-start | bytes 589824 | tf_op jit(solution)/shard_map/all_to_all | solution.py:479
  27.9 0.1 slice_reduce_fusion.1
  28.0 0.6 fusion.1
  29.2 0.1 slice_reduce_fusion
  29.3 0.6 reduce_max.19
  30.6 7.5 %all-to-all-done.5 = bf16[16,24,288]{2,1,0:T(8,128)(2,1)S(1)} async-done(((bf16[16,24,288]{2,1,0:T(8,128)(2,1)}), bf16[16,24,288]{2,1,0:T(8,128)(2,1)S(1)}, u32[]{:S(2)}, u32[]{:S(2)}) %all-to-all-start.5) | async-done | bytes 221216 | tf_op jit(solution)/shard_map/all_to_all | solution.py:479
  38.1 0.0 copy-done.7
  38.1 1.0 shard_map.129
  39.1 0.0 copy-start.6
  39.1 1.2 copy-done.6
  40.4 0.0 copy-start.5
  40.4 32.5 %all_to_all.53.all_ref = bf16[16,432,128]{2,1,0:T(8,128)(2,1)S(1)} all-to-all(bf16[16,432,128]{2,1,0:T(8,128)(2,1)} %copy-done.6), channel_id=1, replica_groups=mesh['prefix'=16,'branch'=16] {'branch'}, dimensions={0} | all-to-all | bytes 3538944 | tf_op jit(solution)/shard_map/all_to_all | solution.py:479
  72.9 0.0 copy-done.5
  72.9 0.0 copy-start.9
  72.9 0.0 copy-start.2
  72.9 0.0 copy-start.3
  72.9 2.0 %shard_map.130 = (bf16[192,256]{1,0:T(8,128)(2,1)S(1)}, bf16[128,1024]{1,0:T(8,128)(2,1)}) custom-call(bf16[16,432,128]{2,1,0:T(8,128)(2,1)S(1)} %all_to_all.53.all_ref, f32[3,16,128]{2,1,0:T(8,128)S(1)} %pad_maximum_fusion.2.gain_ref, f32[192,128]{1,0:T(8,128)S(1)} %get-tuple-element.67.cos_ref, f32[192,128]{1,0:T(8,128)S(1)} %get-tuple-element.68.sin_ref, ...), custom_call_target="tpu_custom_call" | custom-call | flops 20000000000 | bytes 4350336 | tf_op jit(solution)/shard_map/pallas_call | solution.py:47
  74.9 6.6 %all-to-all-start.7 = ((bf16[16,8,1024]{2,1,0:T(8,128)(2,1)}), bf16[16,8,1024]{2,1,0:T(8,128)(2,1)S(1)}, u32[]{:S(2)}, u32[]{:S(2)}) async-start(bf16[16,8,1024]{2,1,0:T(8,128)(2,1)} %bitcast.17), calls=%async_computation.7 | async-start | bytes 524288 | tf_op jit(solution)/shard_map/all_to_all | solution.py:479
  81.5 0.0 copy-done.9
  81.5 0.1 copy.18.len_ref
  82.2 0.0 copy-done.2
  82.2 0.0 copy-done.3
  82.2 0.0 copy-start
  82.2 1.7 %copy-done = bf16[2,4608,128]{2,1,0:T(8,128)(2,1)S(1)} copy-done((bf16[2,4608,128]{2,1,0:T(8,128)(2,1)S(1)}, bf16[2,4608,128]{2,1,0:T(8,128)(2,1)}, u32[]{:S(2)}) %copy-start) | copy-done | bytes 2359320
  83.9 0.0 copy-start.10
  83.9 3.0 %shard_map.131 = f32[48,1152]{1,0:T(8,128)S(1)} custom-call(bf16[16,432,128]{2,1,0:T(8,128)(2,1)S(1)} %all_to_all.53.all_ref, f32[3,16,128]{2,1,0:T(8,128)S(1)} %pad_maximum_fusion.2.gain_ref, f32[192,128]{1,0:T(8,128)S(1)} %get-tuple-element.67.cos_ref, f32[192,128]{1,0:T(8,128)S(1)} %get-tuple-element.68.sin_ref, bf16[2,4608,128]{2,1,0:T(8,128)(2,1)S(1)} %copy-done, ...), custom_call_target="tpu_custom_call" | custom-call | flops 566231040 | bytes 4645056 | tf_op jit(solution)/shard_map/pallas_call | solution.py:47
  86.8 4.4 %all-to-all-done.7 = bf16[16,8,1024]{2,1,0:T(8,128)(2,1)S(1)} async-done(((bf16[16,8,1024]{2,1,0:T(8,128)(2,1)}), bf16[16,8,1024]{2,1,0:T(8,128)(2,1)S(1)}, u32[]{:S(2)}, u32[]{:S(2)}) %all-to-all-start.7) | async-done | bytes 262176 | tf_op jit(solution)/shard_map/all_to_all | solution.py:479
  91.2 0.0 copy-done.10
  91.2 0.0 copy-start.1
  91.2 2.8 %shard_map.132 = bf16[128,1152]{1,0:T(8,128)(2,1)S(1)} custom-call(bf16[128,1024]{1,0:T(8,128)(2,1)S(1)} %bitcast.34, s32[16,128]{1,0:T(8,128)S(1)} %bitcast.46, bf16[2,1024,128]{2,1,0:T(8,128)(2,1)} %keys_ref.1, bf16[2,1024,128]{2,1,0:T(8,128)(2,1)} %values_ref.1), custom_call_target="tpu_custom_call" | custom-call | flops 1073741824 | bytes 1318912 | tf_op jit(solution)/shard_map/pallas_call | solution.py:47
  94.0 14.9 %all_to_all.54 = bf16[16,8,1152]{2,1,0:T(8,128)(2,1)S(1)} all-to-all(bf16[16,8,1152]{2,1,0:T(8,128)(2,1)S(1)} %bitcast.33), channel_id=1, replica_groups=mesh['prefix'=16,'branch'=16] {'prefix'}, dimensions={0} | all-to-all | bytes 589824 | tf_op jit(solution)/shard_map/all_to_all | solution.py:479
  108.9 0.0 copy-done.1
  108.9 1.1 shard_map.133
  110.0 0.0 copy-start.8
  110.1 28.9 %all_to_all.55.parts_ref = bf16[16,432,128]{2,1,0:T(8,128)(2,1)S(1)} all-to-all(bf16[16,432,128]{2,1,0:T(8,128)(2,1)S(1)} %shard_map.133), channel_id=1, replica_groups=mesh['prefix'=16,'branch'=16] {'branch'}, dimensions={0} | all-to-all | bytes 3538944 | tf_op jit(solution)/shard_map/all_to_all | solution.py:479
  138.9 1.0 shard_map.134
  140.0 3.5 %all-to-all-start.10 = ((f32[16,2,128]{2,1,0:T(2,128)}), f32[16,2,128]{2,1,0:T(2,128)S(1)}, u32[]{:S(2)}, u32[]{:S(2)}) async-start(f32[16,2,128]{2,1,0:T(2,128)} %get-tuple-element.77), calls=%async_computation.10 | async-start | bytes 32768 | tf_op jit(solution)/shard_map/all_to_all | solution.py:479
  143.5 0.0 copy-done.8
  143.5 0.1 shard_map.135.scaled_ref
  143.6 7.4 %all-to-all-done.10.squares_ref = f32[16,2,128]{2,1,0:T(2,128)S(1)} async-done(((f32[16,2,128]{2,1,0:T(2,128)}), f32[16,2,128]{2,1,0:T(2,128)S(1)}, u32[]{:S(2)}, u32[]{:S(2)}) %all-to-all-start.10) | async-done | bytes 16416 | tf_op jit(solution)/shard_map/all_to_all | solution.py:479
  151.0 1.8 %shard_map.136 = bf16[192,288]{1,0:T(8,128)(2,1)} custom-call(f32[16,2,128]{2,1,0:T(2,128)S(1)} %all-to-all-done.10.squares_ref, f32[192,288]{1,0:T(8,128)S(1)} %shard_map.135.scaled_ref, bf16[192,288]{1,0:T(8,128)(2,1)} %get-tuple-element.79.rows_ref), custom_call_target="tpu_custom_call" | custom-call | bytes 348160 | tf_op jit(solution)/shard_map/pallas_call | solution.py:47
  (9 shorter events, 0.0 us)
Async XLA Ops:
  0.0 0.7 copy-start.4
  2.6 14.7 %all-to-all-start.4 = ((s32[16,1,128]{2,1,0:T(1,128)}), s32[16,1,128]{2,1,0:T(1,128)S(1)}, u32[]{:S(2)}, u32[]{:S(2)}) async-start(s32[16,1,128]{2,1,0:T(1,128)} %bitcast.8), calls=%async_computation.4 | async-start | bytes 16384 | tf_op jit(solution)/shard_map/all_to_all | solution.py:479
  17.4 20.8 %copy-start.7 = (s32[4,48]{1,0:T(4,128)S(1)}, s32[4,48]{1,0:T(4,128)}, u32[]{:S(2)}) copy-start(s32[4,48]{1,0:T(4,128)} %ids_ref.1) | copy-start | bytes 2308
  23.1 15.1 %all-to-all-start.5 = ((bf16[16,24,288]{2,1,0:T(8,128)(2,1)}), bf16[16,24,288]{2,1,0:T(8,128)(2,1)S(1)}, u32[]{:S(2)}, u32[]{:S(2)}) async-start(bf16[16,24,288]{2,1,0:T(8,128)(2,1)} %shard_map.128), calls=%async_computation.5 | async-start | bytes 589824 | tf_op jit(solution)/shard_map/all_to_all | solution.py:479
  39.1 1.2 copy-start.6
  40.4 32.6 %copy-start.5 = (bf16[4608,256]{1,0:T(8,128)(2,1)S(1)}, bf16[4608,256]{1,0:T(8,128)(2,1)}, u32[]{:S(2)}) copy-start(bf16[4608,256]{1,0:T(8,128)(2,1)} %wq_ref.1) | copy-start | bytes 7077892
  72.9 8.6 %copy-start.9 = (s32[48]{0:T(128)S(1)}, s32[48]{0:T(128)}, u32[]{:S(2)}) copy-start(s32[48]{0:T(128)} %param.19) | copy-start | bytes 580
  72.9 9.2 %copy-start.2 = (bf16[48,8,128]{2,1,0:T(8,128)(2,1)S(1)}, bf16[48,8,128]{2,1,0:T(8,128)(2,1)}, u32[]{:S(2)}) copy-start(bf16[48,8,128]{2,1,0:T(8,128)(2,1)} %param.28) | copy-start | bytes 294916
  72.9 9.2 %copy-start.3 = (bf16[48,8,128]{2,1,0:T(8,128)(2,1)S(1)}, bf16[48,8,128]{2,1,0:T(8,128)(2,1)}, u32[]{:S(2)}) copy-start(bf16[48,8,128]{2,1,0:T(8,128)(2,1)} %param.29) | copy-start | bytes 294916
  74.9 16.3 %all-to-all-start.7 = ((bf16[16,8,1024]{2,1,0:T(8,128)(2,1)}), bf16[16,8,1024]{2,1,0:T(8,128)(2,1)S(1)}, u32[]{:S(2)}, u32[]{:S(2)}) async-start(bf16[16,8,1024]{2,1,0:T(8,128)(2,1)} %bitcast.17), calls=%async_computation.7 | async-start | bytes 524288 | tf_op jit(solution)/shard_map/all_to_all | solution.py:479
  82.2 1.7 %copy-start = (bf16[2,4608,128]{2,1,0:T(8,128)(2,1)S(1)}, bf16[2,4608,128]{2,1,0:T(8,128)(2,1)}, u32[]{:S(2)}) copy-start(bf16[2,4608,128]{2,1,0:T(8,128)(2,1)} %wkv_ref.1) | copy-start | bytes 7077892
  83.9 7.4 %copy-start.10 = (bf16[2,1024,128]{2,1,0:T(8,128)(2,1)S(1)}, bf16[2,1024,128]{2,1,0:T(8,128)(2,1)}, u32[]{:S(2)}) copy-start(bf16[2,1024,128]{2,1,0:T(8,128)(2,1)} %keys_ref.1) | copy-start | bytes 1572868
  91.2 17.7 %copy-start.1 = (bf16[256,4608]{1,0:T(8,128)(2,1)S(1)}, bf16[256,4608]{1,0:T(8,128)(2,1)}, u32[]{:S(2)}) copy-start(bf16[256,4608]{1,0:T(8,128)(2,1)} %w_ref.1) | copy-start | bytes 7077892
  110.0 33.4 %copy-start.8 = (f32[288]{0:T(512)S(1)}, f32[288]{0:T(512)}, u32[]{:S(2)}) copy-start(f32[288]{0:T(512)} %param.25) | copy-start | bytes 3460
  140.0 11.0 %all-to-all-start.10 = ((f32[16,2,128]{2,1,0:T(2,128)}), f32[16,2,128]{2,1,0:T(2,128)S(1)}, u32[]{:S(2)}, u32[]{:S(2)}) async-start(f32[16,2,128]{2,1,0:T(2,128)} %get-tuple-element.77), calls=%async_computation.10 | async-start | bytes 32768 | tf_op jit(solution)/shard_map/all_to_all | solution.py:479

commit v3 on v2

--- a/solution.py
+++ b/solution.py
@@ -38,18 +38,15 @@
 BF16 = jnp.bfloat16
 VMEM = pl.BlockSpec(memory_space=pltpu.VMEM)
 SMEM = pl.BlockSpec(memory_space=pltpu.SMEM)
-ANY = pl.BlockSpec(memory_space=pl.ANY)
-
-
-def call(kernel, out_shape, args, flops=0, scalars=0, left=(), scratch=(), limit=24):
+
+
+def call(kernel, out_shape, args, flops=0, scalars=0, scratch=(), limit=24):
     nbytes = sum(a.size * a.dtype.itemsize for a in args)
     many = isinstance(out_shape, (list, tuple))
     return pl.pallas_call(
         kernel,
         out_shape=out_shape,
-        in_specs=[
-            SMEM if n < scalars else ANY if n in left else VMEM for n in range(len(args))
-        ],
+        in_specs=[SMEM] * scalars + [VMEM] * (len(args) - scalars),
         out_specs=[VMEM] * len(out_shape) if many else VMEM,
         scratch_shapes=list(scratch),
         compiler_params=pltpu.CompilerParams(vmem_limit_bytes=limit * 1024 * 1024),
@@ -157,16 +154,8 @@
 PIECE = 1024
 
 
-def pick_kernel(counts_ref, notes_ref, rest_ref, table_ref, out_ref, held_ref, rows_ref, done):
-    whole = held_ref.shape[1]
-    copies = []
-    for start in range(0, whole, PIECE):
-        part = pl.ds(start, min(PIECE, whole - start))
-        copy = pltpu.make_async_copy(
-            table_ref.at[:, part], held_ref.at[:, part], done.at[start // PIECE]
-        )
-        copy.start()
-        copies.append(copy)
+def pick_kernel(counts_ref, notes_ref, table_ref, out_ref, rows_ref):
+    vocab = table_ref.shape[1]
     lane = iota((8, HEAD), 1)
     ids = jnp.zeros((8, ALL), jnp.int32)
     start = 0
@@ -193,10 +182,9 @@
             hots.append(jnp.where(some == near, jnp.ones((), BF16), jnp.zeros((), BF16)))
         return dot(rows, jnp.concatenate(hots, axis=0) if len(hots) > 1 else hots[0])
 
-    total = picked(whole, rest_ref[...])
-    for start in range(0, whole, PIECE):
-        copies[start // PIECE].wait()
-        total = total + picked(start, held_ref[:, start : min(start + PIECE, whole)])
+    total = jnp.zeros((SHARE, count), F32)
+    for start in range(0, vocab, PIECE):
+        total = total + picked(start, table_ref[:, start : min(start + PIECE, vocab)])
     rows_ref[:ALL, :] = total.T
     rows_ref[ALL:, :] = jnp.zeros((ROOM, SHARE), F32)
     for d in range(RING):
@@ -451,7 +439,7 @@
         squares_ref[b] = line
 
 
-def scale_kernel(sum_ref, gain_ref, out_ref):
+def scale_kernel(sum_ref, gain_ref, rows_ref, out_ref, wide_ref):
     total = sum_ref[...]
     tails = []
     for t in range(STEPS):
@@ -460,9 +448,10 @@
     tail = jnp.concatenate(tails, axis=0)[:, :TAIL]
     placed = jnp.concatenate([total[:TOKENS], total[TOKENS : 2 * TOKENS], tail], axis=1)
     out_ref[...] = placed * gain_ref[...]
-
-
-def finish_kernel(squares_ref, scaled_ref, rows_ref, out_ref):
+    wide_ref[...] = rows_ref[...].astype(F32)
+
+
+def finish_kernel(squares_ref, scaled_ref, wide_ref, out_ref):
     line = squares_ref[0]
     for b in range(1, RING):
         line = line + squares_ref[b]
@@ -472,7 +461,7 @@
     one = jnp.sum(jnp.where(diagonal, line[0:1], 0.0), axis=1, keepdims=True)
     two = jnp.sum(jnp.where(diagonal[:rest], line[1:2], 0.0), axis=1, keepdims=True)
     root = jnp.concatenate([one, two], axis=0)
-    out_ref[...] = (rows_ref[...].astype(F32) + scaled_ref[...] * root).astype(BF16)
+    out_ref[...] = (wide_ref[...] + scaled_ref[...] * root).astype(BF16)
 
 
 def exchange(x, axis):
@@ -507,14 +496,13 @@
             shape((2, ROWS), jnp.int32),
         ],
         (token_ids, prompt_of.reshape(1, ROWS)),
+        flops=LONG,
     )
     notes = exchange(notes.reshape(RING, 1, HEAD), "prefix").reshape(RING, HEAD)
     ends = jnp.max(notes[:, ENDS : ENDS + 2], axis=0)
     asked = jnp.max(jnp.sum(notes[:, COUNTS : COUNTS + RING], axis=0))
     crowded = (ends[0] > TAKE) | (asked > ALL)
 
-    whole = vocab // 256 * 256
-    rest = table[whole:].T
     half = HEAD // 2
     frequency = 10000.0 ** (-(jnp.arange(half, dtype=F32) * 2.0 / HEAD))
     positions = (prompt_len + suffix_len[None, :] + jnp.arange(STEPS)[:, None]).astype(F32)
@@ -528,25 +516,20 @@
         [gains[:, :HEAD], gains[:, HEAD : 2 * HEAD], jnp.tile(gains[:, 2 * HEAD :], (1, 4))]
     )
     lengths = suffix_len.reshape(ROWS, 1)
-    notes, rest, cosines, sines, gains, lengths = lax.optimization_barrier(
-        (notes, rest, cosines, sines, gains, lengths)
+    notes, cosines, sines, gains, lengths = lax.optimization_barrier(
+        (notes, cosines, sines, gains, lengths)
     )
     picked = call(
         pick_kernel,
         shape((RING, TAKE, SHARE), BF16),
-        (notes, notes, rest, table.T),
-        flops=2 * vocab * ALL * SHARE,
+        (notes, notes, table.T),
+        flops=LONG,
         scalars=1,
-        left=(3,),
-        scratch=(
-            pltpu.VMEM((SHARE, whole), BF16),
-            pltpu.VMEM((ALL + ROOM, SHARE), F32),
-            pltpu.SemaphoreType.DMA((-(-whole // PIECE),)),
-        ),
+        scratch=(pltpu.VMEM((ALL + ROOM, SHARE), F32),),
     )
     got = exchange(picked, "prefix").reshape(RING * TAKE, SHARE)
     own = shape((TOKENS, SHARE), BF16), shape((RING, PACKED, HEAD), BF16)
-    placed = tuple(call(unpack_kernel, list(own), (at, got), flops=LONG))
+    placed = tuple(call(unpack_kernel, list(own), (at, got)))
 
     def take_all(_):
         everyone = exchange(jnp.broadcast_to(token_ids, (RING, STEPS, ROWS)), "prefix")
@@ -595,7 +578,7 @@
             suffix_values.reshape(ROWS * SUF, HEAD),
             lengths,
         ),
-        flops=2 * TOKENS * D * 2 * HEAD + 4 * ROWS * WIDE * (ROWS * SUF + TOKENS),
+        flops=LONG,
     )
     own, local = lax.optimization_barrier((own, local))
 
@@ -629,13 +612,15 @@
         (shares,),
     )
     squares = exchange(squares, "branch")
-    scaled = call(
-        scale_kernel, shape((TOKENS, SHARE), F32), (total, post_gain.reshape(1, SHARE))
+    scaled, wide = call(
+        scale_kernel,
+        [shape((TOKENS, SHARE), F32)] * 2,
+        (total, post_gain.reshape(1, SHARE), embedded),
     )
     layer_out = call(
         finish_kernel,
         shape((TOKENS, SHARE), BF16),
-        (squares, scaled, embedded),
+        (squares, scaled, wide),
     )
     return layer_out.reshape(STEPS, ROWS, SHARE)
 

time: 155 us -> 159 us (1.026)
  blocking collectives: 76.3 us -> 43.9 us
  waiting for transfers between devices: 22.3 us -> 52.3 us
  starting transfers between devices: 23.5 us -> 30.7 us
    all_to_all x3 -> x2, blocking collectives: 76.3 us -> 43.9 us  [exchange(): return lax.all_to_all(x, axis, split_axis=0, concat_axis=0, tiled=True)]
    all_to_all x4 -> x5, waiting for transfers between devices: 22.3 us -> 52.3 us  [exchange(): return lax.all_to_all(x, axis, split_axis=0, concat_axis=0, tiled=True)]
    all_to_all x4 -> x5, starting transfers between devices: 23.5 us -> 30.7 us  [exchange(): return lax.all_to_all(x, axis, split_axis=0, concat_axis=0, tiled=True)]
    unnamed x22 -> x24, local copies, waits for them, and re-layouts: 3.59 us -> 5.25 us
  transfers between devices with their start and end apart: 4 -> 5, of which waited for: 4 -> 5; matrix products, arithmetic and copies ran while one was open for 3% -> 1% of each run, Pallas kernels for 2% -> 3%
where the time goes in v3:
time: 159 us; the launch traced here: 156 us
  waiting for transfers between devices  52.3 us (33%)
  blocking collectives  43.9 us (28%)
  starting transfers between devices  30.7 us (19%)
  Pallas kernels  19.6 us (12%)
  local copies, waits for them, and re-layouts  6.2 us (4%)
  between operations  2.05 us (1%)
    all_to_all x5, waiting for transfers between devices, exchange(): return lax.all_to_all(x, axis, split_axis=0, concat_axis=0, tiled=True)  52.3 us
    all_to_all x2, blocking collectives, exchange(): return lax.all_to_all(x, axis, split_axis=0, concat_axis=0, tiled=True)  43.9 us
    all_to_all x5, starting transfers between devices, exchange(): return lax.all_to_all(x, axis, split_axis=0, concat_axis=0, tiled=True)  30.7 us
    pallas_call x10, Pallas kernels, call(): pl.pallas_call(kernel, out_shape=out_shape, in_specs=[SMEM] * scalars + [...  19.6 us
    unnamed x24, local copies, waits for them, and re-layouts  5.25 us
  transfers between devices with their start and end apart: 5, of which 5 were waited for; matrix products, arithmetic and copies ran while one was open for 1% of the time, Pallas kernels for 3%

profile of v3, /device:TPU:32, one launch (start us, length us, event | category | flops | bytes accessed | tf_op | source)
XLA Modules:
  0.0 156.1 jit_solution(3232340419304002666)
XLA Ops:
  0.0 0.0 copy-start.5
  0.0 0.7 copy-done.5
  0.7 0.0 copy-start.7
  0.7 0.0 copy-start.10
  0.7 2.0 %shard_map.127 = (s32[16,128]{1,0:T(8,128)}, s32[192,1]{1,0:T(8,128)S(1)}, s32[48,2]{1,0:T(8,128)S(1)}, s32[2,48]{1,0:T(2,128)S(1)}) custom-call(s32[4,48]{1,0:T(4,128)} %ids_ref.1, s32[1,48]{1,0:T(1,128)S(1)} %bitcast.36), custom_call_target="tpu_custom_call" | custom-call | flops 20000000000 | bytes 960 | tf_op jit(solution)/shard_map/pallas_call | solution.py:46
  2.7 8.6 %all-to-all-start.4 = ((s32[16,1,128]{2,1,0:T(1,128)}), s32[16,1,128]{2,1,0:T(1,128)S(1)}, u32[]{:S(2)}, u32[]{:S(2)}) async-start(s32[16,1,128]{2,1,0:T(1,128)} %bitcast.8), calls=%async_computation.4 | async-start | bytes 16384 | tf_op jit(solution)/shard_map/all_to_all | solution.py:468
  11.3 0.0 copy-done.7
  11.3 0.1 reshape.103
  11.4 0.0 copy-done.10
  11.4 0.1 convert_element_type.23
  11.5 0.1 tile.9
  11.6 0.4 fusion
  12.0 0.1 pad_maximum_fusion
  12.1 5.2 %all-to-all-done.4 = s32[16,1,128]{2,1,0:T(1,128)S(1)} async-done(((s32[16,1,128]{2,1,0:T(1,128)}), s32[16,1,128]{2,1,0:T(1,128)S(1)}, u32[]{:S(2)}, u32[]{:S(2)}) %all-to-all-start.4) | async-done | bytes 8224 | tf_op jit(solution)/shard_map/all_to_all | solution.py:468
  17.4 0.0 copy-start.8
  17.4 4.8 %shard_map.128 = bf16[16,24,288]{2,1,0:T(8,128)(2,1)} custom-call(s32[16,128]{1,0:T(8,128)S(1)} %bitcast.39, s32[16,128]{1,0:T(8,128)S(1)} %bitcast.40, bf16[288,8000]{1,0:T(8,128)(2,1)} %bitcast.38), custom_call_target="tpu_custom_call" | custom-call | flops 20000000000 | bytes 4624384 | tf_op jit(solution)/shard_map/pallas_call | solution.py:46
  22.1 4.8 %all-to-all-start.5 = ((bf16[16,24,288]{2,1,0:T(8,128)(2,1)}), bf16[16,24,288]{2,1,0:T(8,128)(2,1)S(1)}, u32[]{:S(2)}, u32[]{:S(2)}) async-start(bf16[16,24,288]{2,1,0:T(8,128)(2,1)} %shard_map.128), calls=%async_computation.5 | async-start | bytes 589824 | tf_op jit(solution)/shard_map/all_to_all | solution.py:468
  27.0 0.1 slice_reduce_fusion.1
  27.0 0.6 fusion.1
  28.3 0.1 slice_reduce_fusion
  28.4 0.6 reduce_max.19
  29.7 7.5 %all-to-all-done.5 = bf16[16,24,288]{2,1,0:T(8,128)(2,1)S(1)} async-done(((bf16[16,24,288]{2,1,0:T(8,128)(2,1)}), bf16[16,24,288]{2,1,0:T(8,128)(2,1)S(1)}, u32[]{:S(2)}, u32[]{:S(2)}) %all-to-all-start.5) | async-done | bytes 221216 | tf_op jit(solution)/shard_map/all_to_all | solution.py:468
  37.2 0.0 copy-done.8
  37.2 1.0 shard_map.129
  38.2 0.0 copy-start.6
  38.2 1.2 copy-done.6
  39.5 7.0 %all-to-all-start.6 = ((bf16[16,432,128]{2,1,0:T(8,128)(2,1)}), bf16[16,432,128]{2,1,0:T(8,128)(2,1)S(1)}, u32[]{:S(2)}, u32[]{:S(2)}) async-start(bf16[16,432,128]{2,1,0:T(8,128)(2,1)} %copy-done.6), calls=%async_computation.6 | async-start | bytes 3538944 | tf_op jit(solution)/shard_map/all_to_all | solution.py:468
  46.5 0.1 copy.18.len_ref
  47.2 28.0 %all-to-all-done.6.all_ref = bf16[16,432,128]{2,1,0:T(8,128)(2,1)S(1)} async-done(((bf16[16,432,128]{2,1,0:T(8,128)(2,1)}), bf16[16,432,128]{2,1,0:T(8,128)(2,1)S(1)}, u32[]{:S(2)}, u32[]{:S(2)}) %all-to-all-start.6) | async-done | bytes 1769504 | tf_op jit(solution)/shard_map/all_to_all | solution.py:468
  75.2 0.0 copy-start.1
  75.2 1.7 %copy-done.1 = bf16[4608,256]{1,0:T(8,128)(2,1)S(1)} copy-done((bf16[4608,256]{1,0:T(8,128)(2,1)S(1)}, bf16[4608,256]{1,0:T(8,128)(2,1)}, u32[]{:S(2)}) %copy-start.1) | copy-done | bytes 2359320
  76.9 0.0 copy-start.3
  76.9 0.0 copy-start.4
  76.9 2.0 %shard_map.130 = (bf16[192,256]{1,0:T(8,128)(2,1)S(1)}, bf16[128,1024]{1,0:T(8,128)(2,1)}) custom-call(bf16[16,432,128]{2,1,0:T(8,128)(2,1)S(1)} %all-to-all-done.6.all_ref, f32[3,16,128]{2,1,0:T(8,128)S(1)} %pad_maximum_fusion.2.gain_ref, f32[192,128]{1,0:T(8,128)S(1)} %get-tuple-element.67.cos_ref, f32[192,128]{1,0:T(8,128)S(1)} %get-tuple-element.68.sin_ref, ...), custom_call_target="tpu_custom_call" | custom-call | flops 20000000000 | bytes 4350336 | tf_op jit(solution)/shard_map/pallas_call | solution.py:46
  78.8 6.8 %all-to-all-start.7 = ((bf16[16,8,1024]{2,1,0:T(8,128)(2,1)}), bf16[16,8,1024]{2,1,0:T(8,128)(2,1)S(1)}, u32[]{:S(2)}, u32[]{:S(2)}) async-start(bf16[16,8,1024]{2,1,0:T(8,128)(2,1)} %bitcast.16), calls=%async_computation.7 | async-start | bytes 524288 | tf_op jit(solution)/shard_map/all_to_all | solution.py:468
  85.6 0.0 copy-done.3
  85.6 0.0 copy-done.4
  85.6 0.0 copy-start.2
  85.6 1.7 %copy-done.2 = bf16[2,4608,128]{2,1,0:T(8,128)(2,1)S(1)} copy-done((bf16[2,4608,128]{2,1,0:T(8,128)(2,1)S(1)}, bf16[2,4608,128]{2,1,0:T(8,128)(2,1)}, u32[]{:S(2)}) %copy-start.2) | copy-done | bytes 2359320
  87.3 0.0 copy-start.11
  87.3 3.0 %shard_map.131 = f32[48,1152]{1,0:T(8,128)S(1)} custom-call(bf16[16,432,128]{2,1,0:T(8,128)(2,1)S(1)} %all-to-all-done.6.all_ref, f32[3,16,128]{2,1,0:T(8,128)S(1)} %pad_maximum_fusion.2.gain_ref, f32[192,128]{1,0:T(8,128)S(1)} %get-tuple-element.67.cos_ref, f32[192,128]{1,0:T(8,128)S(1)} %get-tuple-element.68.sin_ref, bf16[2,4608,128]{2,1,0:T(8,128)(2,1)S(1)} %copy-done.2, ...), custom_call_target="tpu_custom_call" | custom-call | flops 20000000000 | bytes 4645056 | tf_op jit(solution)/shard_map/pallas_call | solution.py:46
  90.3 5.0 %all-to-all-done.7 = bf16[16,8,1024]{2,1,0:T(8,128)(2,1)S(1)} async-done(((bf16[16,8,1024]{2,1,0:T(8,128)(2,1)}), bf16[16,8,1024]{2,1,0:T(8,128)(2,1)S(1)}, u32[]{:S(2)}, u32[]{:S(2)}) %all-to-all-start.7) | async-done | bytes 262176 | tf_op jit(solution)/shard_map/all_to_all | solution.py:468
  95.3 0.0 copy-done.11
  95.3 0.0 copy-start
  95.3 2.8 %shard_map.132 = bf16[128,1152]{1,0:T(8,128)(2,1)S(1)} custom-call(bf16[128,1024]{1,0:T(8,128)(2,1)S(1)} %bitcast.32, s32[16,128]{1,0:T(8,128)S(1)} %bitcast.44, bf16[2,1024,128]{2,1,0:T(8,128)(2,1)} %keys_ref.1, bf16[2,1024,128]{2,1,0:T(8,128)(2,1)} %values_ref.1), custom_call_target="tpu_custom_call" | custom-call | flops 1073741824 | bytes 1318912 | tf_op jit(solution)/shard_map/pallas_call | solution.py:46
  98.1 14.9 %all_to_all.53 = bf16[16,8,1152]{2,1,0:T(8,128)(2,1)S(1)} all-to-all(bf16[16,8,1152]{2,1,0:T(8,128)(2,1)S(1)} %bitcast.31), channel_id=1, replica_groups=mesh['prefix'=16,'branch'=16] {'prefix'}, dimensions={0} | all-to-all | bytes 589824 | tf_op jit(solution)/shard_map/all_to_all | solution.py:468
  113.0 0.0 copy-done
  113.0 1.1 shard_map.133
  114.1 0.0 copy-start.9
  114.1 29.0 %all_to_all.54.parts_ref = bf16[16,432,128]{2,1,0:T(8,128)(2,1)S(1)} all-to-all(bf16[16,432,128]{2,1,0:T(8,128)(2,1)S(1)} %shard_map.133), channel_id=1, replica_groups=mesh['prefix'=16,'branch'=16] {'branch'}, dimensions={0} | all-to-all | bytes 3538944 | tf_op jit(solution)/shard_map/all_to_all | solution.py:468
  143.2 1.0 shard_map.134
  144.2 3.5 %all-to-all-start.10 = ((f32[16,2,128]{2,1,0:T(2,128)}), f32[16,2,128]{2,1,0:T(2,128)S(1)}, u32[]{:S(2)}, u32[]{:S(2)}) async-start(f32[16,2,128]{2,1,0:T(2,128)} %get-tuple-element.77), calls=%async_computation.10 | async-start | bytes 32768 | tf_op jit(solution)/shard_map/all_to_all | solution.py:468
  147.7 0.0 copy-done.9
  147.7 1.0 shard_map.135
  148.8 6.5 %all-to-all-done.10.squares_ref = f32[16,2,128]{2,1,0:T(2,128)S(1)} async-done(((f32[16,2,128]{2,1,0:T(2,128)}), f32[16,2,128]{2,1,0:T(2,128)S(1)}, u32[]{:S(2)}, u32[]{:S(2)}) %all-to-all-start.10) | async-done | bytes 16416 | tf_op jit(solution)/shard_map/all_to_all | solution.py:468
  155.2 0.9 shard_map.136
  (10 shorter events, 0.0 us)
Async XLA Ops:
  0.0 0.7 copy-start.5
  0.7 10.6 %copy-start.7 = (f32[4608]{0:T(1024)S(1)}, f32[4608]{0:T(1024)}, u32[]{:S(2)}) copy-start(f32[4608]{0:T(1024)} %param.21) | copy-start | bytes 55300
  0.7 10.7 %copy-start.10 = (s32[48]{0:T(128)S(1)}, s32[48]{0:T(128)}, u32[]{:S(2)}) copy-start(s32[48]{0:T(128)} %param.19) | copy-start | bytes 580
  2.7 14.7 %all-to-all-start.4 = ((s32[16,1,128]{2,1,0:T(1,128)}), s32[16,1,128]{2,1,0:T(1,128)S(1)}, u32[]{:S(2)}, u32[]{:S(2)}) async-start(s32[16,1,128]{2,1,0:T(1,128)} %bitcast.8), calls=%async_computation.4 | async-start | bytes 16384 | tf_op jit(solution)/shard_map/all_to_all | solution.py:468
  17.4 19.8 %copy-start.8 = (s32[4,48]{1,0:T(4,128)S(1)}, s32[4,48]{1,0:T(4,128)}, u32[]{:S(2)}) copy-start(s32[4,48]{1,0:T(4,128)} %ids_ref.1) | copy-start | bytes 2308
  22.1 15.0 %all-to-all-start.5 = ((bf16[16,24,288]{2,1,0:T(8,128)(2,1)}), bf16[16,24,288]{2,1,0:T(8,128)(2,1)S(1)}, u32[]{:S(2)}, u32[]{:S(2)}) async-start(bf16[16,24,288]{2,1,0:T(8,128)(2,1)} %shard_map.128), calls=%async_computation.5 | async-start | bytes 589824 | tf_op jit(solution)/shard_map/all_to_all | solution.py:468
  38.2 1.2 copy-start.6
  39.5 35.7 %all-to-all-start.6 = ((bf16[16,432,128]{2,1,0:T(8,128)(2,1)}), bf16[16,432,128]{2,1,0:T(8,128)(2,1)S(1)}, u32[]{:S(2)}, u32[]{:S(2)}) async-start(bf16[16,432,128]{2,1,0:T(8,128)(2,1)} %copy-done.6), calls=%async_computation.6 | async-start | bytes 3538944 | tf_op jit(solution)/shard_map/all_to_all | solution.py:468
  75.2 1.7 %copy-start.1 = (bf16[4608,256]{1,0:T(8,128)(2,1)S(1)}, bf16[4608,256]{1,0:T(8,128)(2,1)}, u32[]{:S(2)}) copy-start(bf16[4608,256]{1,0:T(8,128)(2,1)} %wq_ref.1) | copy-start | bytes 7077892
  76.9 8.7 %copy-start.3 = (bf16[48,8,128]{2,1,0:T(8,128)(2,1)S(1)}, bf16[48,8,128]{2,1,0:T(8,128)(2,1)}, u32[]{:S(2)}) copy-start(bf16[48,8,128]{2,1,0:T(8,128)(2,1)} %param.28) | copy-start | bytes 294916
  76.9 8.7 %copy-start.4 = (bf16[48,8,128]{2,1,0:T(8,128)(2,1)S(1)}, bf16[48,8,128]{2,1,0:T(8,128)(2,1)}, u32[]{:S(2)}) copy-start(bf16[48,8,128]{2,1,0:T(8,128)(2,1)} %param.29) | copy-start | bytes 294916
  78.8 16.5 %all-to-all-start.7 = ((bf16[16,8,1024]{2,1,0:T(8,128)(2,1)}), bf16[16,8,1024]{2,1,0:T(8,128)(2,1)S(1)}, u32[]{:S(2)}, u32[]{:S(2)}) async-start(bf16[16,8,1024]{2,1,0:T(8,128)(2,1)} %bitcast.16), calls=%async_computation.7 | async-start | bytes 524288 | tf_op jit(solution)/shard_map/all_to_all | solution.py:468
  85.6 1.7 %copy-start.2 = (bf16[2,4608,128]{2,1,0:T(8,128)(2,1)S(1)}, bf16[2,4608,128]{2,1,0:T(8,128)(2,1)}, u32[]{:S(2)}) copy-start(bf16[2,4608,128]{2,1,0:T(8,128)(2,1)} %wkv_ref.1) | copy-start | bytes 7077892
  87.3 8.0 %copy-start.11 = (bf16[2,1024,128]{2,1,0:T(8,128)(2,1)S(1)}, bf16[2,1024,128]{2,1,0:T(8,128)(2,1)}, u32[]{:S(2)}) copy-start(bf16[2,1024,128]{2,1,0:T(8,128)(2,1)} %keys_ref.1) | copy-start | bytes 1572868
  95.3 17.7 %copy-start = (bf16[256,4608]{1,0:T(8,128)(2,1)S(1)}, bf16[256,4608]{1,0:T(8,128)(2,1)}, u32[]{:S(2)}) copy-start(bf16[256,4608]{1,0:T(8,128)(2,1)} %w_ref.1) | copy-start | bytes 7077892
  114.1 33.6 %copy-start.9 = (f32[288]{0:T(512)S(1)}, f32[288]{0:T(512)}, u32[]{:S(2)}) copy-start(f32[288]{0:T(512)} %param.25) | copy-start | bytes 3460
  144.2 11.0 %all-to-all-start.10 = ((f32[16,2,128]{2,1,0:T(2,128)}), f32[16,2,128]{2,1,0:T(2,128)S(1)}, u32[]{:S(2)}, u32[]{:S(2)}) async-start(f32[16,2,128]{2,1,0:T(2,128)} %get-tuple-element.77), calls=%async_computation.10 | async-start | bytes 32768 | tf_op jit(solution)/shard_map/all_to_all | solution.py:468

commit v4 on v3

--- a/solution.py
+++ b/solution.py
@@ -515,10 +515,7 @@
     gains = jnp.stack(
         [gains[:, :HEAD], gains[:, HEAD : 2 * HEAD], jnp.tile(gains[:, 2 * HEAD :], (1, 4))]
     )
-    lengths = suffix_len.reshape(ROWS, 1)
-    notes, cosines, sines, gains, lengths = lax.optimization_barrier(
-        (notes, cosines, sines, gains, lengths)
-    )
+    notes, cosines, sines, gains = lax.optimization_barrier((notes, cosines, sines, gains))
     picked = call(
         pick_kernel,
         shape((RING, TAKE, SHARE), BF16),
@@ -529,7 +526,7 @@
     )
     got = exchange(picked, "prefix").reshape(RING * TAKE, SHARE)
     own = shape((TOKENS, SHARE), BF16), shape((RING, PACKED, HEAD), BF16)
-    placed = tuple(call(unpack_kernel, list(own), (at, got)))
+    placed = tuple(call(unpack_kernel, list(own), (at, got), flops=LONG))
 
     def take_all(_):
         everyone = exchange(jnp.broadcast_to(token_ids, (RING, STEPS, ROWS)), "prefix")
@@ -550,6 +547,8 @@
         (everywhere, gains, cosines, sines, slot_lines, w_query),
         flops=LONG,
     )
+
+    queries, lengths, ends = lax.optimization_barrier((queries, suffix_len, ends))
 
     def ask(sent):
         return exchange(sent.reshape(RING, SLOT, WIDE), "prefix").reshape(RING * SLOT, WIDE)
@@ -576,7 +575,7 @@
             queries,
             suffix_keys.reshape(ROWS * SUF, HEAD),
             suffix_values.reshape(ROWS * SUF, HEAD),
-            lengths,
+            lengths.reshape(ROWS, 1),
         ),
         flops=LONG,
     )

time: 159 us -> 154 us (0.969)
  blocking collectives: 43.9 us -> 76.2 us
  waiting for transfers between devices: 52.3 us -> 24.3 us
  starting transfers between devices: 30.7 us -> 23.4 us
  local copies, waits for them, and re-layouts: 6.2 us -> 4.51 us
    all_to_all x2 -> x3, blocking collectives: 43.9 us -> 76.2 us  [exchange(): return lax.all_to_all(x, axis, split_axis=0, concat_axis=0, tiled=True)]
    all_to_all x5 -> x4, waiting for transfers between devices: 52.3 us -> 24.3 us  [exchange(): return lax.all_to_all(x, axis, split_axis=0, concat_axis=0, tiled=True)]
    all_to_all x5 -> x4, starting transfers between devices: 30.7 us -> 23.4 us  [exchange(): return lax.all_to_all(x, axis, split_axis=0, concat_axis=0, tiled=True)]
    unnamed x24, local copies, waits for them, and re-layouts: 5.25 us -> 3.59 us
  transfers between devices with their start and end apart: 5 -> 4, of which waited for: 5 -> 4; matrix products, arithmetic and copies ran while one was open for 1% -> 2% of each run, Pallas kernels for 3% -> 3%
where the time goes in v4:
time: 154 us; the launch traced here: 151 us
  blocking collectives  76.2 us (49%)
  waiting for transfers between devices  24.3 us (16%)
  starting transfers between devices  23.4 us (15%)
  Pallas kernels  19.7 us (13%)
  local copies, waits for them, and re-layouts  4.51 us (3%)
    all_to_all x3, blocking collectives, exchange(): return lax.all_to_all(x, axis, split_axis=0, concat_axis=0, tiled=True)  76.2 us
    all_to_all x4, waiting for transfers between devices, exchange(): return lax.all_to_all(x, axis, split_axis=0, concat_axis=0, tiled=True)  24.3 us
    all_to_all x4, starting transfers between devices, exchange(): return lax.all_to_all(x, axis, split_axis=0, concat_axis=0, tiled=True)  23.4 us
    pallas_call x10, Pallas kernels, call(): pl.pallas_call(kernel, out_shape=out_shape, in_specs=[SMEM] * scalars + [...  19.7 us
    unnamed x24, local copies, waits for them, and re-layouts  3.59 us
  transfers between devices with their start and end apart: 4, of which 4 were waited for; matrix products, arithmetic and copies ran while one was open for 2% of the time, Pallas kernels for 3%

profile of v4, /device:TPU:32, one launch (start us, length us, event | category | flops | bytes accessed | tf_op | source)
XLA Modules:
  0.0 151.0 jit_solution(12371010051315644471)
XLA Ops:
  0.0 0.0 copy-start.5
  0.0 0.7 copy-done.5
  0.7 0.0 copy-start.7
  0.7 0.0 copy-start.10
  0.7 2.0 %shard_map.127 = (s32[16,128]{1,0:T(8,128)}, s32[192,1]{1,0:T(8,128)S(1)}, s32[48,2]{1,0:T(8,128)S(1)}, s32[2,48]{1,0:T(2,128)S(1)}) custom-call(s32[4,48]{1,0:T(4,128)} %ids_ref.1, s32[1,48]{1,0:T(1,128)S(1)} %bitcast.37), custom_call_target="tpu_custom_call" | custom-call | flops 20000000000 | bytes 960 | tf_op jit(solution)/shard_map/pallas_call | solution.py:46
  2.7 8.6 %all-to-all-start.4 = ((s32[16,1,128]{2,1,0:T(1,128)}), s32[16,1,128]{2,1,0:T(1,128)S(1)}, u32[]{:S(2)}, u32[]{:S(2)}) async-start(s32[16,1,128]{2,1,0:T(1,128)} %bitcast.8), calls=%async_computation.4 | async-start | bytes 16384 | tf_op jit(solution)/shard_map/all_to_all | solution.py:468
  11.3 0.0 copy-done.7
  11.3 0.1 reshape.103
  11.4 0.0 copy-done.10
  11.4 0.1 convert_element_type.23
  11.5 0.1 tile.9
  11.6 0.4 fusion
  12.0 0.1 pad_maximum_fusion
  12.1 5.2 %all-to-all-done.4 = s32[16,1,128]{2,1,0:T(1,128)S(1)} async-done(((s32[16,1,128]{2,1,0:T(1,128)}), s32[16,1,128]{2,1,0:T(1,128)S(1)}, u32[]{:S(2)}, u32[]{:S(2)}) %all-to-all-start.4) | async-done | bytes 8224 | tf_op jit(solution)/shard_map/all_to_all | solution.py:468
  17.4 0.0 copy-start.8
  17.4 4.8 %shard_map.128 = bf16[16,24,288]{2,1,0:T(8,128)(2,1)} custom-call(s32[16,128]{1,0:T(8,128)S(1)} %bitcast.40, s32[16,128]{1,0:T(8,128)S(1)} %bitcast.41, bf16[288,8000]{1,0:T(8,128)(2,1)} %bitcast.39), custom_call_target="tpu_custom_call" | custom-call | flops 20000000000 | bytes 4624384 | tf_op jit(solution)/shard_map/pallas_call | solution.py:46
  22.2 4.8 %all-to-all-start.5 = ((bf16[16,24,288]{2,1,0:T(8,128)(2,1)}), bf16[16,24,288]{2,1,0:T(8,128)(2,1)S(1)}, u32[]{:S(2)}, u32[]{:S(2)}) async-start(bf16[16,24,288]{2,1,0:T(8,128)(2,1)} %shard_map.128), calls=%async_computation.5 | async-start | bytes 589824 | tf_op jit(solution)/shard_map/all_to_all | solution.py:468
  27.0 0.1 slice_reduce_fusion.1
  27.1 0.1 slice_reduce_fusion
  27.2 0.7 reduce_max.19
  28.5 8.7 %all-to-all-done.5 = bf16[16,24,288]{2,1,0:T(8,128)(2,1)S(1)} async-done(((bf16[16,24,288]{2,1,0:T(8,128)(2,1)}), bf16[16,24,288]{2,1,0:T(8,128)(2,1)S(1)}, u32[]{:S(2)}, u32[]{:S(2)}) %all-to-all-start.5) | async-done | bytes 221216 | tf_op jit(solution)/shard_map/all_to_all | solution.py:468
  37.2 0.0 copy-done.8
  37.2 1.0 shard_map.129
  38.2 0.0 copy-start.6
  38.2 1.2 copy-done.6
  39.5 0.0 copy-start.1
  39.5 32.5 %all_to_all.53.all_ref = bf16[16,432,128]{2,1,0:T(8,128)(2,1)S(1)} all-to-all(bf16[16,432,128]{2,1,0:T(8,128)(2,1)} %copy-done.6), channel_id=1, replica_groups=mesh['prefix'=16,'branch'=16] {'branch'}, dimensions={0} | all-to-all | bytes 3538944 | tf_op jit(solution)/shard_map/all_to_all | solution.py:468
  72.0 0.0 copy-done.1
  72.0 0.0 copy-start.3
  72.0 0.0 copy-start.4
  72.0 2.0 %shard_map.130 = (bf16[192,256]{1,0:T(8,128)(2,1)S(1)}, bf16[128,1024]{1,0:T(8,128)(2,1)}) custom-call(bf16[16,432,128]{2,1,0:T(8,128)(2,1)S(1)} %all_to_all.53.all_ref, f32[3,16,128]{2,1,0:T(8,128)S(1)} %pad_maximum_fusion.2.gain_ref, f32[192,128]{1,0:T(8,128)S(1)} %get-tuple-element.69.cos_ref, f32[192,128]{1,0:T(8,128)S(1)} %get-tuple-element.70.sin_ref, ...), custom_call_target="tpu_custom_call" | custom-call | flops 20000000000 | bytes 4350336 | tf_op jit(solution)/shard_map/pallas_call | solution.py:46
  74.0 0.1 copy.18.len_ref
  74.1 6.6 %all-to-all-start.7 = ((bf16[16,8,1024]{2,1,0:T(8,128)(2,1)}), bf16[16,8,1024]{2,1,0:T(8,128)(2,1)S(1)}, u32[]{:S(2)}, u32[]{:S(2)}) async-start(bf16[16,8,1024]{2,1,0:T(8,128)(2,1)} %bitcast.15), calls=%async_computation.7 | async-start | bytes 524288 | tf_op jit(solution)/shard_map/all_to_all | solution.py:468
  80.7 0.0 copy-done.3
  80.7 0.0 copy-done.4
  80.7 0.0 copy-start.2
  80.7 1.7 %copy-done.2 = bf16[2,4608,128]{2,1,0:T(8,128)(2,1)S(1)} copy-done((bf16[2,4608,128]{2,1,0:T(8,128)(2,1)S(1)}, bf16[2,4608,128]{2,1,0:T(8,128)(2,1)}, u32[]{:S(2)}) %copy-start.2) | copy-done | bytes 2359320
  82.4 0.0 copy-start.11
  82.4 3.0 %shard_map.131 = f32[48,1152]{1,0:T(8,128)S(1)} custom-call(bf16[16,432,128]{2,1,0:T(8,128)(2,1)S(1)} %all_to_all.53.all_ref, f32[3,16,128]{2,1,0:T(8,128)S(1)} %pad_maximum_fusion.2.gain_ref, f32[192,128]{1,0:T(8,128)S(1)} %get-tuple-element.69.cos_ref, f32[192,128]{1,0:T(8,128)S(1)} %get-tuple-element.70.sin_ref, bf16[2,4608,128]{2,1,0:T(8,128)(2,1)S(1)} %copy-done.2, ...), custom_call_target="tpu_custom_call" | custom-call | flops 20000000000 | bytes 4645056 | tf_op jit(solution)/shard_map/pallas_call | solution.py:46
  85.4 0.6 slice.27
  86.6 3.9 %all-to-all-done.7 = bf16[16,8,1024]{2,1,0:T(8,128)(2,1)S(1)} async-done(((bf16[16,8,1024]{2,1,0:T(8,128)(2,1)}), bf16[16,8,1024]{2,1,0:T(8,128)(2,1)S(1)}, u32[]{:S(2)}, u32[]{:S(2)}) %all-to-all-start.7) | async-done | bytes 262176 | tf_op jit(solution)/shard_map/all_to_all | solution.py:468
  90.4 0.0 copy-done.11
  90.4 0.0 copy-start
  90.4 2.8 %shard_map.132 = bf16[128,1152]{1,0:T(8,128)(2,1)S(1)} custom-call(bf16[128,1024]{1,0:T(8,128)(2,1)S(1)} %bitcast.33, s32[16,128]{1,0:T(8,128)S(1)} %bitcast.45, bf16[2,1024,128]{2,1,0:T(8,128)(2,1)} %keys_ref.1, bf16[2,1024,128]{2,1,0:T(8,128)(2,1)} %values_ref.1), custom_call_target="tpu_custom_call" | custom-call | flops 1073741824 | bytes 1318912 | tf_op jit(solution)/shard_map/pallas_call | solution.py:46
  93.3 14.9 %all_to_all.54 = bf16[16,8,1152]{2,1,0:T(8,128)(2,1)S(1)} all-to-all(bf16[16,8,1152]{2,1,0:T(8,128)(2,1)S(1)} %bitcast.32), channel_id=1, replica_groups=mesh['prefix'=16,'branch'=16] {'prefix'}, dimensions={0} | all-to-all | bytes 589824 | tf_op jit(solution)/shard_map/all_to_all | solution.py:468
  108.1 0.0 copy-done
  108.1 1.1 shard_map.133
  109.3 0.0 copy-start.9
  109.3 28.8 %all_to_all.55.parts_ref = bf16[16,432,128]{2,1,0:T(8,128)(2,1)S(1)} all-to-all(bf16[16,432,128]{2,1,0:T(8,128)(2,1)S(1)} %shard_map.133), channel_id=1, replica_groups=mesh['prefix'=16,'branch'=16] {'branch'}, dimensions={0} | all-to-all | bytes 3538944 | tf_op jit(solution)/shard_map/all_to_all | solution.py:468
  138.1 1.0 shard_map.134
  139.1 3.4 %all-to-all-start.10 = ((f32[16,2,128]{2,1,0:T(2,128)}), f32[16,2,128]{2,1,0:T(2,128)S(1)}, u32[]{:S(2)}, u32[]{:S(2)}) async-start(f32[16,2,128]{2,1,0:T(2,128)} %get-tuple-element.81), calls=%async_computation.10 | async-start | bytes 32768 | tf_op jit(solution)/shard_map/all_to_all | solution.py:468
  142.6 0.0 copy-done.9
  142.6 1.0 shard_map.135
  143.6 6.5 %all-to-all-done.10.squares_ref = f32[16,2,128]{2,1,0:T(2,128)S(1)} async-done(((f32[16,2,128]{2,1,0:T(2,128)}), f32[16,2,128]{2,1,0:T(2,128)S(1)}, u32[]{:S(2)}, u32[]{:S(2)}) %all-to-all-start.10) | async-done | bytes 16416 | tf_op jit(solution)/shard_map/all_to_all | solution.py:468
  150.1 0.9 shard_map.136
  (10 shorter events, 0.0 us)
Async XLA Ops:
  0.0 0.7 copy-start.5
  0.7 10.6 %copy-start.7 = (f32[4608]{0:T(1024)S(1)}, f32[4608]{0:T(1024)}, u32[]{:S(2)}) copy-start(f32[4608]{0:T(1024)} %param.21) | copy-start | bytes 55300
  0.7 10.7 %copy-start.10 = (s32[48]{0:T(128)S(1)}, s32[48]{0:T(128)}, u32[]{:S(2)}) copy-start(s32[48]{0:T(128)} %param.19) | copy-start | bytes 580
  2.7 14.7 %all-to-all-start.4 = ((s32[16,1,128]{2,1,0:T(1,128)}), s32[16,1,128]{2,1,0:T(1,128)S(1)}, u32[]{:S(2)}, u32[]{:S(2)}) async-start(s32[16,1,128]{2,1,0:T(1,128)} %bitcast.8), calls=%async_computation.4 | async-start | bytes 16384 | tf_op jit(solution)/shard_map/all_to_all | solution.py:468
  17.4 19.8 %copy-start.8 = (s32[4,48]{1,0:T(4,128)S(1)}, s32[4,48]{1,0:T(4,128)}, u32[]{:S(2)}) copy-start(s32[4,48]{1,0:T(4,128)} %ids_ref.1) | copy-start | bytes 2308
  22.2 15.0 %all-to-all-start.5 = ((bf16[16,24,288]{2,1,0:T(8,128)(2,1)}), bf16[16,24,288]{2,1,0:T(8,128)(2,1)S(1)}, u32[]{:S(2)}, u32[]{:S(2)}) async-start(bf16[16,24,288]{2,1,0:T(8,128)(2,1)} %shard_map.128), calls=%async_computation.5 | async-start | bytes 589824 | tf_op jit(solution)/shard_map/all_to_all | solution.py:468
  38.2 1.2 copy-start.6
  39.5 32.6 %copy-start.1 = (bf16[4608,256]{1,0:T(8,128)(2,1)S(1)}, bf16[4608,256]{1,0:T(8,128)(2,1)}, u32[]{:S(2)}) copy-start(bf16[4608,256]{1,0:T(8,128)(2,1)} %wq_ref.1) | copy-start | bytes 7077892
  72.0 8.7 %copy-start.3 = (bf16[48,8,128]{2,1,0:T(8,128)(2,1)S(1)}, bf16[48,8,128]{2,1,0:T(8,128)(2,1)}, u32[]{:S(2)}) copy-start(bf16[48,8,128]{2,1,0:T(8,128)(2,1)} %param.28) | copy-start | bytes 294916
  72.0 8.7 %copy-start.4 = (bf16[48,8,128]{2,1,0:T(8,128)(2,1)S(1)}, bf16[48,8,128]{2,1,0:T(8,128)(2,1)}, u32[]{:S(2)}) copy-start(bf16[48,8,128]{2,1,0:T(8,128)(2,1)} %param.29) | copy-start | bytes 294916
  74.1 16.3 %all-to-all-start.7 = ((bf16[16,8,1024]{2,1,0:T(8,128)(2,1)}), bf16[16,8,1024]{2,1,0:T(8,128)(2,1)S(1)}, u32[]{:S(2)}, u32[]{:S(2)}) async-start(bf16[16,8,1024]{2,1,0:T(8,128)(2,1)} %bitcast.15), calls=%async_computation.7 | async-start | bytes 524288 | tf_op jit(solution)/shard_map/all_to_all | solution.py:468
  80.7 1.7 %copy-start.2 = (bf16[2,4608,128]{2,1,0:T(8,128)(2,1)S(1)}, bf16[2,4608,128]{2,1,0:T(8,128)(2,1)}, u32[]{:S(2)}) copy-start(bf16[2,4608,128]{2,1,0:T(8,128)(2,1)} %wkv_ref.1) | copy-start | bytes 7077892
  82.4 8.0 %copy-start.11 = (bf16[2,1024,128]{2,1,0:T(8,128)(2,1)S(1)}, bf16[2,1024,128]{2,1,0:T(8,128)(2,1)}, u32[]{:S(2)}) copy-start(bf16[2,1024,128]{2,1,0:T(8,128)(2,1)} %keys_ref.1) | copy-start | bytes 1572868
  90.4 17.7 %copy-start = (bf16[256,4608]{1,0:T(8,128)(2,1)S(1)}, bf16[256,4608]{1,0:T(8,128)(2,1)}, u32[]{:S(2)}) copy-start(bf16[256,4608]{1,0:T(8,128)(2,1)} %w_ref.1) | copy-start | bytes 7077892
  109.3 33.3 %copy-start.9 = (f32[288]{0:T(512)S(1)}, f32[288]{0:T(512)}, u32[]{:S(2)}) copy-start(f32[288]{0:T(512)} %param.25) | copy-start | bytes 3460
  139.1 11.0 %all-to-all-start.10 = ((f32[16,2,128]{2,1,0:T(2,128)}), f32[16,2,128]{2,1,0:T(2,128)S(1)}, u32[]{:S(2)}, u32[]{:S(2)}) async-start(f32[16,2,128]{2,1,0:T(2,128)} %get-tuple-element.81), calls=%async_computation.10 | async-start | bytes 32768 | tf_op jit(solution)/shard_map/all_to_all | solution.py:468

commit v5 on v4

--- a/solution.py
+++ b/solution.py
@@ -38,15 +38,18 @@
 BF16 = jnp.bfloat16
 VMEM = pl.BlockSpec(memory_space=pltpu.VMEM)
 SMEM = pl.BlockSpec(memory_space=pltpu.SMEM)
-
-
-def call(kernel, out_shape, args, flops=0, scalars=0, scratch=(), limit=24):
+ANY = pl.BlockSpec(memory_space=pl.ANY)
+
+
+def call(kernel, out_shape, args, flops=0, scalars=0, left=(), scratch=(), limit=24):
     nbytes = sum(a.size * a.dtype.itemsize for a in args)
     many = isinstance(out_shape, (list, tuple))
     return pl.pallas_call(
         kernel,
         out_shape=out_shape,
-        in_specs=[SMEM] * scalars + [VMEM] * (len(args) - scalars),
+        in_specs=[
+            SMEM if n < scalars else ANY if n in left else VMEM for n in range(len(args))
+        ],
         out_specs=[VMEM] * len(out_shape) if many else VMEM,
         scratch_shapes=list(scratch),
         compiler_params=pltpu.CompilerParams(vmem_limit_bytes=limit * 1024 * 1024),
@@ -151,10 +154,12 @@
 
 
 LONG = 20_000_000_000
-PIECE = 1024
-
-
-def pick_kernel(counts_ref, notes_ref, table_ref, out_ref, rows_ref):
+PIECE = 2048
+
+
+def pick_kernel(counts_ref, notes_ref, table_ref, out_ref, rows_ref, hot_ref, held_ref, done):
+    fetch = pltpu.make_async_copy(table_ref, held_ref, done)
+    fetch.start()
     vocab = table_ref.shape[1]
     lane = iota((8, HEAD), 1)
     ids = jnp.zeros((8, ALL), jnp.int32)
@@ -172,19 +177,17 @@
     step = 256
     lines = iota((step, count), 0).astype(F32).astype(BF16)
 
-    def picked(start, rows):
-        size = rows.shape[1]
-        hots = []
-        for at in range(start, start + size, step):
-            here = (ids >= at) & (ids < at + step)
-            near = jnp.where(here, ids - at, -1).astype(F32).astype(BF16)
-            some = lines[: min(step, start + size - at)]
-            hots.append(jnp.where(some == near, jnp.ones((), BF16), jnp.zeros((), BF16)))
-        return dot(rows, jnp.concatenate(hots, axis=0) if len(hots) > 1 else hots[0])
-
+    for start in range(0, vocab, step):
+        size = min(step, vocab - start)
+        here = (ids >= start) & (ids < start + step)
+        near = jnp.where(here, ids - start, -1).astype(F32).astype(BF16)
+        hot = jnp.where(lines[:size] == near, jnp.ones((), BF16), jnp.zeros((), BF16))
+        hot_ref[start : start + size, :] = hot
+    fetch.wait()
     total = jnp.zeros((SHARE, count), F32)
     for start in range(0, vocab, PIECE):
-        total = total + picked(start, table_ref[:, start : min(start + PIECE, vocab)])
+        part = slice(start, min(start + PIECE, vocab))
+        total = total + dot(held_ref[:, part], hot_ref[part, :])
     rows_ref[:ALL, :] = total.T
     rows_ref[ALL:, :] = jnp.zeros((ROOM, SHARE), F32)
     for d in range(RING):
@@ -216,10 +219,6 @@
     rows = dot(hot, got_ref[...])
     out_ref[...] = rows.astype(BF16)
     pack(rows, packed_ref)
-
-
-def pack_kernel(rows_ref, packed_ref):
-    pack(rows_ref[...].astype(F32), packed_ref)
 
 
 def normed_times(all_ref, gain_ref, weights):
@@ -522,11 +521,15 @@
         (notes, notes, table.T),
         flops=LONG,
         scalars=1,
-        scratch=(pltpu.VMEM((ALL + ROOM, SHARE), F32),),
+        left=(2,),
+        scratch=(
+            pltpu.VMEM((ALL + ROOM, SHARE), F32),
+            pltpu.VMEM((vocab, ALL), BF16),
+            pltpu.VMEM((SHARE, vocab), BF16),
+            pltpu.SemaphoreType.DMA,
+        ),
     )
     got = exchange(picked, "prefix").reshape(RING * TAKE, SHARE)
-    own = shape((TOKENS, SHARE), BF16), shape((RING, PACKED, HEAD), BF16)
-    placed = tuple(call(unpack_kernel, list(own), (at, got), flops=LONG))
 
     def take_all(_):
         everyone = exchange(jnp.broadcast_to(token_ids, (RING, STEPS, ROWS)), "prefix")
@@ -535,10 +538,16 @@
         rows = jnp.take(table, jnp.clip(inside_at, 0, vocab - 1), axis=0)
         rows = jnp.where(inside[..., None], rows, jnp.zeros_like(rows))
         rows = exchange(rows, "prefix").astype(F32).sum(axis=0).astype(BF16)
-        rows = rows.reshape(TOKENS, SHARE)
-        return rows, call(pack_kernel, own[1], (rows,))
-
-    embedded, packed = lax.cond(crowded, take_all, lambda placed: placed, placed)
+        rows = jnp.pad(rows.reshape(TOKENS, SHARE), ((0, RING * TAKE - TOKENS), (0, 0)))
+        return jnp.arange(TOKENS, dtype=jnp.int32).reshape(TOKENS, 1), rows
+
+    at, got = lax.cond(crowded, take_all, lambda found: found, (at, got))
+    embedded, packed = call(
+        unpack_kernel,
+        [shape((TOKENS, SHARE), BF16), shape((RING, PACKED, HEAD), BF16)],
+        (at, got),
+        flops=LONG,
+    )
     everywhere = exchange(packed, "branch")
 
     queries, sent = call(

time: 154 us -> 152 us (0.987)
    unnamed x24 -> x22, local copies, waits for them, and re-layouts: 3.59 us -> 2.35 us
  transfers between devices with their start and end apart: 4 -> 4, of which waited for: 4 -> 4; matrix products, arithmetic and copies ran while one was open for 2% -> 2% of each run, Pallas kernels for 3% -> 2%
where the time goes in v5:
time: 152 us; the launch traced here: 150 us
  blocking collectives  76.1 us (50%)
  waiting for transfers between devices  25.1 us (17%)
  starting transfers between devices  23.5 us (15%)
  Pallas kernels  18.8 us (12%)
  local copies, waits for them, and re-layouts  3.29 us (2%)
    all_to_all x3, blocking collectives, exchange(): return lax.all_to_all(x, axis, split_axis=0, concat_axis=0, tiled=True)  76.1 us
    all_to_all x4, waiting for transfers between devices, exchange(): return lax.all_to_all(x, axis, split_axis=0, concat_axis=0, tiled=True)  25.1 us
    all_to_all x4, starting transfers between devices, exchange(): return lax.all_to_all(x, axis, split_axis=0, concat_axis=0, tiled=True)  23.5 us
    pallas_call x10, Pallas kernels, call(): pl.pallas_call(kernel, out_shape=out_shape, in_specs=[SMEM if n < scalars...  18.8 us
  transfers between devices with their start and end apart: 4, of which 4 were waited for; matrix products, arithmetic and copies ran while one was open for 2% of the time, Pallas kernels for 2%

profile of v5, /device:TPU:32, one launch (start us, length us, event | category | flops | bytes accessed | tf_op | source)
XLA Modules:
  0.0 149.7 jit_solution(9887141998250825742)
XLA Ops:
  0.0 0.0 copy-start.5
  0.0 0.7 copy-done.5
  0.7 0.0 copy-start.6
  0.7 0.0 copy-start.9
  0.7 2.0 %shard_map.127 = (s32[16,128]{1,0:T(8,128)}, s32[192,1]{1,0:T(8,128)S(1)}, s32[48,2]{1,0:T(8,128)S(1)}, s32[2,48]{1,0:T(2,128)S(1)}) custom-call(s32[4,48]{1,0:T(4,128)} %ids_ref.1, s32[1,48]{1,0:T(1,128)S(1)} %bitcast.36), custom_call_target="tpu_custom_call" | custom-call | flops 20000000000 | bytes 960 | tf_op jit(solution)/shard_map/pallas_call | solution.py:47
  2.7 8.6 %all-to-all-start.4 = ((s32[16,1,128]{2,1,0:T(1,128)}), s32[16,1,128]{2,1,0:T(1,128)S(1)}, u32[]{:S(2)}, u32[]{:S(2)}) async-start(s32[16,1,128]{2,1,0:T(1,128)} %bitcast.9), calls=%async_computation.4 | async-start | bytes 16384 | tf_op jit(solution)/shard_map/all_to_all | solution.py:467
  11.3 0.0 copy-done.6
  11.3 0.1 reshape.105
  11.4 0.0 copy-done.9
  11.4 0.1 convert_element_type.25
  11.5 0.1 tile.9
  11.6 0.4 fusion
  12.0 0.1 pad_maximum_fusion
  12.1 5.2 %all-to-all-done.4 = s32[16,1,128]{2,1,0:T(1,128)S(1)} async-done(((s32[16,1,128]{2,1,0:T(1,128)}), s32[16,1,128]{2,1,0:T(1,128)S(1)}, u32[]{:S(2)}, u32[]{:S(2)}) %all-to-all-start.4) | async-done | bytes 8224 | tf_op jit(solution)/shard_map/all_to_all | solution.py:467
  17.4 0.0 copy-start.7
  17.4 5.4 %shard_map.128 = bf16[16,24,288]{2,1,0:T(8,128)(2,1)} custom-call(s32[16,128]{1,0:T(8,128)S(1)} %bitcast.41, s32[16,128]{1,0:T(8,128)S(1)} %bitcast.42, bf16[288,8000]{1,0:T(8,128)(2,1)} %bitcast.38), custom_call_target="tpu_custom_call" | custom-call | flops 20000000000 | bytes 4624384 | tf_op jit(solution)/shard_map/pallas_call | solution.py:47
  22.8 4.8 %all-to-all-start.5 = ((bf16[16,24,288]{2,1,0:T(8,128)(2,1)}), bf16[16,24,288]{2,1,0:T(8,128)(2,1)S(1)}, u32[]{:S(2)}, u32[]{:S(2)}) async-start(bf16[16,24,288]{2,1,0:T(8,128)(2,1)} %shard_map.128), calls=%async_computation.5 | async-start | bytes 589824 | tf_op jit(solution)/shard_map/all_to_all | solution.py:467
  27.6 0.1 slice_reduce_fusion.1
  27.7 0.1 slice_reduce_fusion
  27.8 0.7 reduce_max.19
  29.2 8.7 %all-to-all-done.5 = bf16[16,24,288]{2,1,0:T(8,128)(2,1)S(1)} async-done(((bf16[16,24,288]{2,1,0:T(8,128)(2,1)}), bf16[16,24,288]{2,1,0:T(8,128)(2,1)S(1)}, u32[]{:S(2)}, u32[]{:S(2)}) %all-to-all-start.5) | async-done | bytes 221216 | tf_op jit(solution)/shard_map/all_to_all | solution.py:467
  37.8 0.0 copy-done.7
  37.8 0.4 shard_map.129
  38.3 0.0 copy-start.1
  38.3 32.3 %all_to_all.53.all_ref = bf16[16,432,128]{2,1,0:T(8,128)(2,1)S(1)} all-to-all(bf16[16,432,128]{2,1,0:T(8,128)(2,1)S(1)} %get-tuple-element.76), channel_id=1, replica_groups=mesh['prefix'=16,'branch'=16] {'branch'}, dimensions={0} | all-to-all | bytes 3538944 | tf_op jit(solution)/shard_map/all_to_all | solution.py:467
  70.6 0.0 copy-done.1
  70.6 0.0 copy-start.3
  70.6 0.0 copy-start.4
  70.6 2.0 %shard_map.130 = (bf16[192,256]{1,0:T(8,128)(2,1)S(1)}, bf16[128,1024]{1,0:T(8,128)(2,1)}) custom-call(bf16[16,432,128]{2,1,0:T(8,128)(2,1)S(1)} %all_to_all.53.all_ref, f32[3,16,128]{2,1,0:T(8,128)S(1)} %pad_maximum_fusion.2.gain_ref, f32[192,128]{1,0:T(8,128)S(1)} %get-tuple-element.78.cos_ref, f32[192,128]{1,0:T(8,128)S(1)} %get-tuple-element.79.sin_ref, ...), custom_call_target="tpu_custom_call" | custom-call | flops 20000000000 | bytes 4350336 | tf_op jit(solution)/shard_map/pallas_call | solution.py:47
  72.6 0.1 copy.18.len_ref
  72.7 6.6 %all-to-all-start.7 = ((bf16[16,8,1024]{2,1,0:T(8,128)(2,1)}), bf16[16,8,1024]{2,1,0:T(8,128)(2,1)S(1)}, u32[]{:S(2)}, u32[]{:S(2)}) async-start(bf16[16,8,1024]{2,1,0:T(8,128)(2,1)} %bitcast.15), calls=%async_computation.7 | async-start | bytes 524288 | tf_op jit(solution)/shard_map/all_to_all | solution.py:467
  79.3 0.0 copy-done.3
  79.3 0.0 copy-done.4
  79.3 0.0 copy-start.2
  79.4 1.7 %copy-done.2 = bf16[2,4608,128]{2,1,0:T(8,128)(2,1)S(1)} copy-done((bf16[2,4608,128]{2,1,0:T(8,128)(2,1)S(1)}, bf16[2,4608,128]{2,1,0:T(8,128)(2,1)}, u32[]{:S(2)}) %copy-start.2) | copy-done | bytes 2359320
  81.0 0.0 copy-start.10
  81.0 3.0 %shard_map.131 = f32[48,1152]{1,0:T(8,128)S(1)} custom-call(bf16[16,432,128]{2,1,0:T(8,128)(2,1)S(1)} %all_to_all.53.all_ref, f32[3,16,128]{2,1,0:T(8,128)S(1)} %pad_maximum_fusion.2.gain_ref, f32[192,128]{1,0:T(8,128)S(1)} %get-tuple-element.78.cos_ref, f32[192,128]{1,0:T(8,128)S(1)} %get-tuple-element.79.sin_ref, bf16[2,4608,128]{2,1,0:T(8,128)(2,1)S(1)} %copy-done.2, ...), custom_call_target="tpu_custom_call" | custom-call | flops 20000000000 | bytes 4645056 | tf_op jit(solution)/shard_map/pallas_call | solution.py:47
  84.0 0.6 slice.27
  85.3 3.8 %all-to-all-done.7 = bf16[16,8,1024]{2,1,0:T(8,128)(2,1)S(1)} async-done(((bf16[16,8,1024]{2,1,0:T(8,128)(2,1)}), bf16[16,8,1024]{2,1,0:T(8,128)(2,1)S(1)}, u32[]{:S(2)}, u32[]{:S(2)}) %all-to-all-start.7) | async-done | bytes 262176 | tf_op jit(solution)/shard_map/all_to_all | solution.py:467
  89.0 0.0 copy-done.10
  89.0 0.0 copy-start
  89.0 2.8 %shard_map.132 = bf16[128,1152]{1,0:T(8,128)(2,1)S(1)} custom-call(bf16[128,1024]{1,0:T(8,128)(2,1)S(1)} %bitcast.32, s32[16,128]{1,0:T(8,128)S(1)} %bitcast.46, bf16[2,1024,128]{2,1,0:T(8,128)(2,1)} %keys_ref.1, bf16[2,1024,128]{2,1,0:T(8,128)(2,1)} %values_ref.1), custom_call_target="tpu_custom_call" | custom-call | flops 1073741824 | bytes 1318912 | tf_op jit(solution)/shard_map/pallas_call | solution.py:47
  91.9 14.9 %all_to_all.54 = bf16[16,8,1152]{2,1,0:T(8,128)(2,1)S(1)} all-to-all(bf16[16,8,1152]{2,1,0:T(8,128)(2,1)S(1)} %bitcast.31), channel_id=1, replica_groups=mesh['prefix'=16,'branch'=16] {'prefix'}, dimensions={0} | all-to-all | bytes 589824 | tf_op jit(solution)/shard_map/all_to_all | solution.py:467
  106.7 0.0 copy-done
  106.7 1.1 shard_map.133
  107.9 0.0 copy-start.8
  107.9 28.9 %all_to_all.55.parts_ref = bf16[16,432,128]{2,1,0:T(8,128)(2,1)S(1)} all-to-all(bf16[16,432,128]{2,1,0:T(8,128)(2,1)S(1)} %shard_map.133), channel_id=1, replica_groups=mesh['prefix'=16,'branch'=16] {'branch'}, dimensions={0} | all-to-all | bytes 3538944 | tf_op jit(solution)/shard_map/all_to_all | solution.py:467
  136.7 1.0 shard_map.134
  137.8 3.5 %all-to-all-start.10 = ((f32[16,2,128]{2,1,0:T(2,128)}), f32[16,2,128]{2,1,0:T(2,128)S(1)}, u32[]{:S(2)}, u32[]{:S(2)}) async-start(f32[16,2,128]{2,1,0:T(2,128)} %get-tuple-element.90), calls=%async_computation.10 | async-start | bytes 32768 | tf_op jit(solution)/shard_map/all_to_all | solution.py:467
  141.3 0.0 copy-done.8
  141.3 0.1 shard_map.135
  141.4 7.4 %all-to-all-done.10.squares_ref = f32[16,2,128]{2,1,0:T(2,128)S(1)} async-done(((f32[16,2,128]{2,1,0:T(2,128)}), f32[16,2,128]{2,1,0:T(2,128)S(1)}, u32[]{:S(2)}, u32[]{:S(2)}) %all-to-all-start.10) | async-done | bytes 16416 | tf_op jit(solution)/shard_map/all_to_all | solution.py:467
  148.8 0.9 shard_map.136
  (10 shorter events, 0.0 us)
Async XLA Ops:
  0.0 0.7 copy-start.5
  0.7 10.6 %copy-start.6 = (f32[4608]{0:T(1024)S(1)}, f32[4608]{0:T(1024)}, u32[]{:S(2)}) copy-start(f32[4608]{0:T(1024)} %param.21) | copy-start | bytes 55300
  0.7 10.7 %copy-start.9 = (s32[48]{0:T(128)S(1)}, s32[48]{0:T(128)}, u32[]{:S(2)}) copy-start(s32[48]{0:T(128)} %param.19) | copy-start | bytes 580
  2.7 14.7 %all-to-all-start.4 = ((s32[16,1,128]{2,1,0:T(1,128)}), s32[16,1,128]{2,1,0:T(1,128)S(1)}, u32[]{:S(2)}, u32[]{:S(2)}) async-start(s32[16,1,128]{2,1,0:T(1,128)} %bitcast.9), calls=%async_computation.4 | async-start | bytes 16384 | tf_op jit(solution)/shard_map/all_to_all | solution.py:467
  17.4 20.5 %copy-start.7 = (s32[4,48]{1,0:T(4,128)S(1)}, s32[4,48]{1,0:T(4,128)}, u32[]{:S(2)}) copy-start(s32[4,48]{1,0:T(4,128)} %ids_ref.1) | copy-start | bytes 2308
  22.8 15.1 %all-to-all-start.5 = ((bf16[16,24,288]{2,1,0:T(8,128)(2,1)}), bf16[16,24,288]{2,1,0:T(8,128)(2,1)S(1)}, u32[]{:S(2)}, u32[]{:S(2)}) async-start(bf16[16,24,288]{2,1,0:T(8,128)(2,1)} %shard_map.128), calls=%async_computation.5 | async-start | bytes 589824 | tf_op jit(solution)/shard_map/all_to_all | solution.py:467
  38.3 32.4 %copy-start.1 = (bf16[4608,256]{1,0:T(8,128)(2,1)S(1)}, bf16[4608,256]{1,0:T(8,128)(2,1)}, u32[]{:S(2)}) copy-start(bf16[4608,256]{1,0:T(8,128)(2,1)} %wq_ref.1) | copy-start | bytes 7077892
  70.6 8.7 %copy-start.3 = (bf16[48,8,128]{2,1,0:T(8,128)(2,1)S(1)}, bf16[48,8,128]{2,1,0:T(8,128)(2,1)}, u32[]{:S(2)}) copy-start(bf16[48,8,128]{2,1,0:T(8,128)(2,1)} %param.28) | copy-start | bytes 294916
  70.6 8.7 %copy-start.4 = (bf16[48,8,128]{2,1,0:T(8,128)(2,1)S(1)}, bf16[48,8,128]{2,1,0:T(8,128)(2,1)}, u32[]{:S(2)}) copy-start(bf16[48,8,128]{2,1,0:T(8,128)(2,1)} %param.29) | copy-start | bytes 294916
  72.7 16.3 %all-to-all-start.7 = ((bf16[16,8,1024]{2,1,0:T(8,128)(2,1)}), bf16[16,8,1024]{2,1,0:T(8,128)(2,1)S(1)}, u32[]{:S(2)}, u32[]{:S(2)}) async-start(bf16[16,8,1024]{2,1,0:T(8,128)(2,1)} %bitcast.15), calls=%async_computation.7 | async-start | bytes 524288 | tf_op jit(solution)/shard_map/all_to_all | solution.py:467
  79.3 1.7 %copy-start.2 = (bf16[2,4608,128]{2,1,0:T(8,128)(2,1)S(1)}, bf16[2,4608,128]{2,1,0:T(8,128)(2,1)}, u32[]{:S(2)}) copy-start(bf16[2,4608,128]{2,1,0:T(8,128)(2,1)} %wkv_ref.1) | copy-start | bytes 7077892
  81.0 8.0 %copy-start.10 = (bf16[2,1024,128]{2,1,0:T(8,128)(2,1)S(1)}, bf16[2,1024,128]{2,1,0:T(8,128)(2,1)}, u32[]{:S(2)}) copy-start(bf16[2,1024,128]{2,1,0:T(8,128)(2,1)} %keys_ref.1) | copy-start | bytes 1572868
  89.0 17.7 %copy-start = (bf16[256,4608]{1,0:T(8,128)(2,1)S(1)}, bf16[256,4608]{1,0:T(8,128)(2,1)}, u32[]{:S(2)}) copy-start(bf16[256,4608]{1,0:T(8,128)(2,1)} %w_ref.1) | copy-start | bytes 7077892
  107.9 33.4 %copy-start.8 = (f32[288]{0:T(512)S(1)}, f32[288]{0:T(512)}, u32[]{:S(2)}) copy-start(f32[288]{0:T(512)} %param.25) | copy-start | bytes 3460
  137.8 11.0 %all-to-all-start.10 = ((f32[16,2,128]{2,1,0:T(2,128)}), f32[16,2,128]{2,1,0:T(2,128)S(1)}, u32[]{:S(2)}, u32[]{:S(2)}) async-start(f32[16,2,128]{2,1,0:T(2,128)} %get-tuple-element.90), calls=%async_computation.10 | async-start | bytes 32768 | tf_op jit(solution)/shard_map/all_to_all | solution.py:467

commit v6 on v4

--- a/solution.py
+++ b/solution.py
@@ -14,6 +14,7 @@
 SUF = 8
 SOFT_CAP = 50.0
 EPSILON = 1e-06
+LOG2_E = 1.4426950408889634
 SCALE = float(D // HEADS) ** (-0.5)
 
 RING = 16
@@ -38,15 +39,18 @@
 BF16 = jnp.bfloat16
 VMEM = pl.BlockSpec(memory_space=pltpu.VMEM)
 SMEM = pl.BlockSpec(memory_space=pltpu.SMEM)
-
-
-def call(kernel, out_shape, args, flops=0, scalars=0, scratch=(), limit=24):
+ANY = pl.BlockSpec(memory_space=pl.ANY)
+
+
+def call(kernel, out_shape, args, flops=0, scalars=0, left=(), scratch=(), limit=24):
     nbytes = sum(a.size * a.dtype.itemsize for a in args)
     many = isinstance(out_shape, (list, tuple))
     return pl.pallas_call(
         kernel,
         out_shape=out_shape,
-        in_specs=[SMEM] * scalars + [VMEM] * (len(args) - scalars),
+        in_specs=[
+            SMEM if n < scalars else ANY if n in left else VMEM for n in range(len(args))
+        ],
         out_specs=[VMEM] * len(out_shape) if many else VMEM,
         scratch_shapes=list(scratch),
         compiler_params=pltpu.CompilerParams(vmem_limit_bytes=limit * 1024 * 1024),
@@ -63,7 +67,7 @@
 
 
 def capped_exp(scores):
-    return jnp.exp(SOFT_CAP * jnp.tanh(scores * (SCALE / SOFT_CAP)))
+    return jnp.exp2(SOFT_CAP * LOG2_E * jnp.tanh(scores * (SCALE / SOFT_CAP)))
 
 
 def lane_group(shape):
@@ -218,10 +222,6 @@
     pack(rows, packed_ref)
 
 
-def pack_kernel(rows_ref, packed_ref):
-    pack(rows_ref[...].astype(F32), packed_ref)
-
-
 def normed_times(all_ref, gain_ref, weights):
     group = lane_group((ROWS, HEAD))
     squares = jnp.zeros((TOKENS, HEAD), F32)
@@ -296,12 +296,18 @@
     send_ref[...] = dot(hot, wide).astype(BF16)
 
 
-def prefix_kernel(turn, own_ref, notes_ref, keys_ref, values_ref, out_ref):
+def prefix_kernel(
+    turn, own_ref, notes_ref, keys_ref, values_ref, out_ref, both_keys, both_values, done
+):
+    fetches = []
+    for m, (source, target) in enumerate(((keys_ref, both_keys), (values_ref, both_values))):
+        for n in range(2):
+            part = target.at[:, n * HEAD : (n + 1) * HEAD]
+            fetches.append(pltpu.make_async_copy(source.at[n], part, done.at[2 * m + n]))
+            fetches[-1].start()
     lanes = iota((RING, SLOT, HEAD), 2) - (ROOM + turn) == iota((RING, SLOT, HEAD), 1)
     notes = jnp.where(lanes, notes_ref[...][:, None, :], 0).reshape(RING * SLOT, HEAD)
     odd = jnp.sum(notes, axis=1, keepdims=True) == 1
-    keys = jnp.concatenate([keys_ref[0], keys_ref[1]], axis=1)
-    values = jnp.concatenate([values_ref[0], values_ref[1]], axis=1)
     slots = RING * SLOT
     lanes = iota((slots, HEAD), 1)
     denoms = jnp.zeros((slots, HEAD), F32)
@@ -317,9 +323,15 @@
                     axis=1,
                 )
             )
-        scores = dot(jnp.concatenate(parts, axis=0), keys, ((1,), (1,)))
+        if first == 0:
+            fetches[0].wait()
+            fetches[1].wait()
+        scores = dot(jnp.concatenate(parts, axis=0), both_keys[...], ((1,), (1,)))
         weights = capped_exp(scores).astype(BF16)
-        numer = dot(weights, values)
+        if first == 0:
+            fetches[2].wait()
+            fetches[3].wait()
+        numer = dot(weights, both_values[...])
         denom = jnp.sum(weights.astype(F32), axis=1, keepdims=True)
         for n, i in enumerate(some):
             part = numer[n * slots : (n + 1) * slots]
@@ -525,8 +537,6 @@
         scratch=(pltpu.VMEM((ALL + ROOM, SHARE), F32),),
     )
     got = exchange(picked, "prefix").reshape(RING * TAKE, SHARE)
-    own = shape((TOKENS, SHARE), BF16), shape((RING, PACKED, HEAD), BF16)
-    placed = tuple(call(unpack_kernel, list(own), (at, got), flops=LONG))
 
     def take_all(_):
         everyone = exchange(jnp.broadcast_to(token_ids, (RING, STEPS, ROWS)), "prefix")
@@ -535,10 +545,16 @@
         rows = jnp.take(table, jnp.clip(inside_at, 0, vocab - 1), axis=0)
         rows = jnp.where(inside[..., None], rows, jnp.zeros_like(rows))
         rows = exchange(rows, "prefix").astype(F32).sum(axis=0).astype(BF16)
-        rows = rows.reshape(TOKENS, SHARE)
-        return rows, call(pack_kernel, own[1], (rows,))
-
-    embedded, packed = lax.cond(crowded, take_all, lambda placed: placed, placed)
+        rows = jnp.pad(rows.reshape(TOKENS, SHARE), ((0, RING * TAKE - TOKENS), (0, 0)))
+        return jnp.arange(TOKENS, dtype=jnp.int32).reshape(TOKENS, 1), rows
+
+    at, got = lax.cond(crowded, take_all, lambda found: found, (at, got))
+    embedded, packed = call(
+        unpack_kernel,
+        [shape((TOKENS, SHARE), BF16), shape((RING, PACKED, HEAD), BF16)],
+        (at, got),
+        flops=LONG,
+    )
     everywhere = exchange(packed, "branch")
 
     queries, sent = call(
@@ -558,6 +574,12 @@
             functools.partial(prefix_kernel, turn),
             shape((RING * SLOT, BACK), BF16),
             (own, notes, prefix_keys, prefix_values),
+            left=(2, 3),
+            scratch=(
+                pltpu.VMEM((prompt_len, 2 * HEAD), BF16),
+                pltpu.VMEM((prompt_len, 2 * HEAD), BF16),
+                pltpu.SemaphoreType.DMA((4,)),
+            ),
             flops=8 * RING * SLOT * prompt_len * WIDE,
         )
         return exchange(sums.reshape(RING, SLOT, BACK), "prefix").reshape(RING * SLOT, BACK)

time: 154 us -> 152 us (0.987)
    unnamed x24 -> x22, local copies, waits for them, and re-layouts: 3.59 us -> 2.35 us
  transfers between devices with their start and end apart: 4 -> 4, of which waited for: 4 -> 4; matrix products, arithmetic and copies ran while one was open for 2% -> 2% of each run, Pallas kernels for 3% -> 2%
where the time goes in v6:
time: 152 us; the launch traced here: 150 us
  blocking collectives  76.1 us (50%)
  waiting for transfers between devices  25.1 us (17%)
  starting transfers between devices  23.5 us (15%)
  Pallas kernels  18.8 us (12%)
  local copies, waits for them, and re-layouts  3.29 us (2%)
    all_to_all x3, blocking collectives, exchange(): return lax.all_to_all(x, axis, split_axis=0, concat_axis=0, tiled=True)  76.1 us
    all_to_all x4, waiting for transfers between devices, exchange(): return lax.all_to_all(x, axis, split_axis=0, concat_axis=0, tiled=True)  25.1 us
    all_to_all x4, starting transfers between devices, exchange(): return lax.all_to_all(x, axis, split_axis=0, concat_axis=0, tiled=True)  23.5 us
    pallas_call x10, Pallas kernels, call(): pl.pallas_call(kernel, out_shape=out_shape, in_specs=[SMEM if n < scalars...  18.8 us
  transfers between devices with their start and end apart: 4, of which 4 were waited for; matrix products, arithmetic and copies ran while one was open for 2% of the time, Pallas kernels for 2%

profile of v6, /device:TPU:32, one launch (start us, length us, event | category | flops | bytes accessed | tf_op | source)
XLA Modules:
  0.0 149.7 jit_solution(4962636519210835938)
XLA Ops:
  0.0 0.0 copy-start.5
  0.0 0.7 copy-done.5
  0.7 0.0 copy-start.6
  0.7 0.0 copy-start.9
  0.7 2.0 %shard_map.127 = (s32[16,128]{1,0:T(8,128)}, s32[192,1]{1,0:T(8,128)S(1)}, s32[48,2]{1,0:T(8,128)S(1)}, s32[2,48]{1,0:T(2,128)S(1)}) custom-call(s32[4,48]{1,0:T(4,128)} %ids_ref.1, s32[1,48]{1,0:T(1,128)S(1)} %bitcast.36), custom_call_target="tpu_custom_call" | custom-call | flops 20000000000 | bytes 960 | tf_op jit(solution)/shard_map/pallas_call | solution.py:48
  2.7 8.6 %all-to-all-start.4 = ((s32[16,1,128]{2,1,0:T(1,128)}), s32[16,1,128]{2,1,0:T(1,128)S(1)}, u32[]{:S(2)}, u32[]{:S(2)}) async-start(s32[16,1,128]{2,1,0:T(1,128)} %bitcast.9), calls=%async_computation.4 | async-start | bytes 16384 | tf_op jit(solution)/shard_map/all_to_all | solution.py:480
  11.3 0.0 copy-done.6
  11.3 0.1 reshape.105
  11.4 0.0 copy-done.9
  11.4 0.1 convert_element_type.25
  11.5 0.1 tile.9
  11.6 0.4 fusion
  12.0 0.1 pad_maximum_fusion
  12.1 5.2 %all-to-all-done.4 = s32[16,1,128]{2,1,0:T(1,128)S(1)} async-done(((s32[16,1,128]{2,1,0:T(1,128)}), s32[16,1,128]{2,1,0:T(1,128)S(1)}, u32[]{:S(2)}, u32[]{:S(2)}) %all-to-all-start.4) | async-done | bytes 8224 | tf_op jit(solution)/shard_map/all_to_all | solution.py:480
  17.4 0.0 copy-start.7
  17.4 4.8 %shard_map.128 = bf16[16,24,288]{2,1,0:T(8,128)(2,1)} custom-call(s32[16,128]{1,0:T(8,128)S(1)} %bitcast.41, s32[16,128]{1,0:T(8,128)S(1)} %bitcast.42, bf16[288,8000]{1,0:T(8,128)(2,1)} %bitcast.38), custom_call_target="tpu_custom_call" | custom-call | flops 20000000000 | bytes 4624384 | tf_op jit(solution)/shard_map/pallas_call | solution.py:48
  22.2 4.8 %all-to-all-start.5 = ((bf16[16,24,288]{2,1,0:T(8,128)(2,1)}), bf16[16,24,288]{2,1,0:T(8,128)(2,1)S(1)}, u32[]{:S(2)}, u32[]{:S(2)}) async-start(bf16[16,24,288]{2,1,0:T(8,128)(2,1)} %shard_map.128), calls=%async_computation.5 | async-start | bytes 589824 | tf_op jit(solution)/shard_map/all_to_all | solution.py:480
  27.0 0.1 slice_reduce_fusion.1
  27.1 0.1 slice_reduce_fusion
  27.2 0.7 reduce_max.19
  28.5 8.7 %all-to-all-done.5 = bf16[16,24,288]{2,1,0:T(8,128)(2,1)S(1)} async-done(((bf16[16,24,288]{2,1,0:T(8,128)(2,1)}), bf16[16,24,288]{2,1,0:T(8,128)(2,1)S(1)}, u32[]{:S(2)}, u32[]{:S(2)}) %all-to-all-start.5) | async-done | bytes 221216 | tf_op jit(solution)/shard_map/all_to_all | solution.py:480
  37.2 0.0 copy-done.7
  37.2 0.4 shard_map.129
  37.6 0.0 copy-start.1
  37.7 32.3 %all_to_all.53.all_ref = bf16[16,432,128]{2,1,0:T(8,128)(2,1)S(1)} all-to-all(bf16[16,432,128]{2,1,0:T(8,128)(2,1)S(1)} %get-tuple-element.76), channel_id=1, replica_groups=mesh['prefix'=16,'branch'=16] {'branch'}, dimensions={0} | all-to-all | bytes 3538944 | tf_op jit(solution)/shard_map/all_to_all | solution.py:480
  70.0 0.0 copy-done.1
  70.0 0.0 copy-start.3
  70.0 0.0 copy-start.4
  70.0 2.0 %shard_map.130 = (bf16[192,256]{1,0:T(8,128)(2,1)S(1)}, bf16[128,1024]{1,0:T(8,128)(2,1)}) custom-call(bf16[16,432,128]{2,1,0:T(8,128)(2,1)S(1)} %all_to_all.53.all_ref, f32[3,16,128]{2,1,0:T(8,128)S(1)} %pad_maximum_fusion.2.gain_ref, f32[192,128]{1,0:T(8,128)S(1)} %get-tuple-element.78.cos_ref, f32[192,128]{1,0:T(8,128)S(1)} %get-tuple-element.79.sin_ref, ...), custom_call_target="tpu_custom_call" | custom-call | flops 20000000000 | bytes 4350336 | tf_op jit(solution)/shard_map/pallas_call | solution.py:48
  72.0 0.1 copy.18.len_ref
  72.1 6.6 %all-to-all-start.7 = ((bf16[16,8,1024]{2,1,0:T(8,128)(2,1)}), bf16[16,8,1024]{2,1,0:T(8,128)(2,1)S(1)}, u32[]{:S(2)}, u32[]{:S(2)}) async-start(bf16[16,8,1024]{2,1,0:T(8,128)(2,1)} %bitcast.15), calls=%async_computation.7 | async-start | bytes 524288 | tf_op jit(solution)/shard_map/all_to_all | solution.py:480
  78.7 0.0 copy-done.3
  78.7 0.0 copy-done.4
  78.7 0.0 copy-start.2
  78.7 1.7 %copy-done.2 = bf16[2,4608,128]{2,1,0:T(8,128)(2,1)S(1)} copy-done((bf16[2,4608,128]{2,1,0:T(8,128)(2,1)S(1)}, bf16[2,4608,128]{2,1,0:T(8,128)(2,1)}, u32[]{:S(2)}) %copy-start.2) | copy-done | bytes 2359320
  80.4 0.0 copy-start.10
  80.4 3.0 %shard_map.131 = f32[48,1152]{1,0:T(8,128)S(1)} custom-call(bf16[16,432,128]{2,1,0:T(8,128)(2,1)S(1)} %all_to_all.53.all_ref, f32[3,16,128]{2,1,0:T(8,128)S(1)} %pad_maximum_fusion.2.gain_ref, f32[192,128]{1,0:T(8,128)S(1)} %get-tuple-element.78.cos_ref, f32[192,128]{1,0:T(8,128)S(1)} %get-tuple-element.79.sin_ref, bf16[2,4608,128]{2,1,0:T(8,128)(2,1)S(1)} %copy-done.2, ...), custom_call_target="tpu_custom_call" | custom-call | flops 20000000000 | bytes 4645056 | tf_op jit(solution)/shard_map/pallas_call | solution.py:48
  83.4 0.6 slice.27
  84.6 3.8 %all-to-all-done.7 = bf16[16,8,1024]{2,1,0:T(8,128)(2,1)S(1)} async-done(((bf16[16,8,1024]{2,1,0:T(8,128)(2,1)}), bf16[16,8,1024]{2,1,0:T(8,128)(2,1)S(1)}, u32[]{:S(2)}, u32[]{:S(2)}) %all-to-all-start.7) | async-done | bytes 262176 | tf_op jit(solution)/shard_map/all_to_all | solution.py:480
  88.4 0.0 copy-done.10
  88.4 0.0 copy-start
  88.4 3.4 %shard_map.132 = bf16[128,1152]{1,0:T(8,128)(2,1)S(1)} custom-call(bf16[128,1024]{1,0:T(8,128)(2,1)S(1)} %bitcast.32, s32[16,128]{1,0:T(8,128)S(1)} %bitcast.46, bf16[2,1024,128]{2,1,0:T(8,128)(2,1)} %keys_ref.1, bf16[2,1024,128]{2,1,0:T(8,128)(2,1)} %values_ref.1), custom_call_target="tpu_custom_call" | custom-call | flops 1073741824 | bytes 1318912 | tf_op jit(solution)/shard_map/pallas_call | solution.py:48
  91.9 14.9 %all_to_all.54 = bf16[16,8,1152]{2,1,0:T(8,128)(2,1)S(1)} all-to-all(bf16[16,8,1152]{2,1,0:T(8,128)(2,1)S(1)} %bitcast.31), channel_id=1, replica_groups=mesh['prefix'=16,'branch'=16] {'prefix'}, dimensions={0} | all-to-all | bytes 589824 | tf_op jit(solution)/shard_map/all_to_all | solution.py:480
  106.8 0.0 copy-done
  106.8 1.1 shard_map.133
  107.9 0.0 copy-start.8
  107.9 28.9 %all_to_all.55.parts_ref = bf16[16,432,128]{2,1,0:T(8,128)(2,1)S(1)} all-to-all(bf16[16,432,128]{2,1,0:T(8,128)(2,1)S(1)} %shard_map.133), channel_id=1, replica_groups=mesh['prefix'=16,'branch'=16] {'branch'}, dimensions={0} | all-to-all | bytes 3538944 | tf_op jit(solution)/shard_map/all_to_all | solution.py:480
  136.8 1.0 shard_map.134
  137.8 3.5 %all-to-all-start.10 = ((f32[16,2,128]{2,1,0:T(2,128)}), f32[16,2,128]{2,1,0:T(2,128)S(1)}, u32[]{:S(2)}, u32[]{:S(2)}) async-start(f32[16,2,128]{2,1,0:T(2,128)} %get-tuple-element.90), calls=%async_computation.10 | async-start | bytes 32768 | tf_op jit(solution)/shard_map/all_to_all | solution.py:480
  141.3 0.0 copy-done.8
  141.3 0.1 shard_map.135
  141.4 7.4 %all-to-all-done.10.squares_ref = f32[16,2,128]{2,1,0:T(2,128)S(1)} async-done(((f32[16,2,128]{2,1,0:T(2,128)}), f32[16,2,128]{2,1,0:T(2,128)S(1)}, u32[]{:S(2)}, u32[]{:S(2)}) %all-to-all-start.10) | async-done | bytes 16416 | tf_op jit(solution)/shard_map/all_to_all | solution.py:480
  148.8 0.9 shard_map.136
  (10 shorter events, 0.0 us)
Async XLA Ops:
  0.0 0.7 copy-start.5
  0.7 10.6 %copy-start.6 = (f32[4608]{0:T(1024)S(1)}, f32[4608]{0:T(1024)}, u32[]{:S(2)}) copy-start(f32[4608]{0:T(1024)} %param.21) | copy-start | bytes 55300
  0.7 10.7 %copy-start.9 = (s32[48]{0:T(128)S(1)}, s32[48]{0:T(128)}, u32[]{:S(2)}) copy-start(s32[48]{0:T(128)} %param.19) | copy-start | bytes 580
  2.7 14.7 %all-to-all-start.4 = ((s32[16,1,128]{2,1,0:T(1,128)}), s32[16,1,128]{2,1,0:T(1,128)S(1)}, u32[]{:S(2)}, u32[]{:S(2)}) async-start(s32[16,1,128]{2,1,0:T(1,128)} %bitcast.9), calls=%async_computation.4 | async-start | bytes 16384 | tf_op jit(solution)/shard_map/all_to_all | solution.py:480
  17.4 19.8 %copy-start.7 = (s32[4,48]{1,0:T(4,128)S(1)}, s32[4,48]{1,0:T(4,128)}, u32[]{:S(2)}) copy-start(s32[4,48]{1,0:T(4,128)} %ids_ref.1) | copy-start | bytes 2308
  22.2 15.0 %all-to-all-start.5 = ((bf16[16,24,288]{2,1,0:T(8,128)(2,1)}), bf16[16,24,288]{2,1,0:T(8,128)(2,1)S(1)}, u32[]{:S(2)}, u32[]{:S(2)}) async-start(bf16[16,24,288]{2,1,0:T(8,128)(2,1)} %shard_map.128), calls=%async_computation.5 | async-start | bytes 589824 | tf_op jit(solution)/shard_map/all_to_all | solution.py:480
  37.6 32.4 %copy-start.1 = (bf16[4608,256]{1,0:T(8,128)(2,1)S(1)}, bf16[4608,256]{1,0:T(8,128)(2,1)}, u32[]{:S(2)}) copy-start(bf16[4608,256]{1,0:T(8,128)(2,1)} %wq_ref.1) | copy-start | bytes 7077892
  70.0 8.7 %copy-start.3 = (bf16[48,8,128]{2,1,0:T(8,128)(2,1)S(1)}, bf16[48,8,128]{2,1,0:T(8,128)(2,1)}, u32[]{:S(2)}) copy-start(bf16[48,8,128]{2,1,0:T(8,128)(2,1)} %param.28) | copy-start | bytes 294916
  70.0 8.7 %copy-start.4 = (bf16[48,8,128]{2,1,0:T(8,128)(2,1)S(1)}, bf16[48,8,128]{2,1,0:T(8,128)(2,1)}, u32[]{:S(2)}) copy-start(bf16[48,8,128]{2,1,0:T(8,128)(2,1)} %param.29) | copy-start | bytes 294916
  72.1 16.3 %all-to-all-start.7 = ((bf16[16,8,1024]{2,1,0:T(8,128)(2,1)}), bf16[16,8,1024]{2,1,0:T(8,128)(2,1)S(1)}, u32[]{:S(2)}, u32[]{:S(2)}) async-start(bf16[16,8,1024]{2,1,0:T(8,128)(2,1)} %bitcast.15), calls=%async_computation.7 | async-start | bytes 524288 | tf_op jit(solution)/shard_map/all_to_all | solution.py:480
  78.7 1.7 %copy-start.2 = (bf16[2,4608,128]{2,1,0:T(8,128)(2,1)S(1)}, bf16[2,4608,128]{2,1,0:T(8,128)(2,1)}, u32[]{:S(2)}) copy-start(bf16[2,4608,128]{2,1,0:T(8,128)(2,1)} %wkv_ref.1) | copy-start | bytes 7077892
  80.4 8.0 %copy-start.10 = (bf16[2,1024,128]{2,1,0:T(8,128)(2,1)S(1)}, bf16[2,1024,128]{2,1,0:T(8,128)(2,1)}, u32[]{:S(2)}) copy-start(bf16[2,1024,128]{2,1,0:T(8,128)(2,1)} %keys_ref.1) | copy-start | bytes 1572868
  88.4 18.3 %copy-start = (bf16[256,4608]{1,0:T(8,128)(2,1)S(1)}, bf16[256,4608]{1,0:T(8,128)(2,1)}, u32[]{:S(2)}) copy-start(bf16[256,4608]{1,0:T(8,128)(2,1)} %w_ref.1) | copy-start | bytes 7077892
  107.9 33.4 %copy-start.8 = (f32[288]{0:T(512)S(1)}, f32[288]{0:T(512)}, u32[]{:S(2)}) copy-start(f32[288]{0:T(512)} %param.25) | copy-start | bytes 3460
  137.8 11.0 %all-to-all-start.10 = ((f32[16,2,128]{2,1,0:T(2,128)}), f32[16,2,128]{2,1,0:T(2,128)S(1)}, u32[]{:S(2)}, u32[]{:S(2)}) async-start(f32[16,2,128]{2,1,0:T(2,128)} %get-tuple-element.90), calls=%async_computation.10 | async-start | bytes 32768 | tf_op jit(solution)/shard_map/all_to_all | solution.py:480

commit v7 on v4

--- a/solution.py
+++ b/solution.py
@@ -14,6 +14,7 @@
 SUF = 8
 SOFT_CAP = 50.0
 EPSILON = 1e-06
+LOG2_E = 1.4426950408889634
 SCALE = float(D // HEADS) ** (-0.5)
 
 RING = 16
@@ -63,7 +64,7 @@
 
 
 def capped_exp(scores):
-    return jnp.exp(SOFT_CAP * jnp.tanh(scores * (SCALE / SOFT_CAP)))
+    return jnp.exp2(SOFT_CAP * LOG2_E * jnp.tanh(scores * (SCALE / SOFT_CAP)))
 
 
 def lane_group(shape):
@@ -218,10 +219,6 @@
     pack(rows, packed_ref)
 
 
-def pack_kernel(rows_ref, packed_ref):
-    pack(rows_ref[...].astype(F32), packed_ref)
-
-
 def normed_times(all_ref, gain_ref, weights):
     group = lane_group((ROWS, HEAD))
     squares = jnp.zeros((TOKENS, HEAD), F32)
@@ -305,7 +302,7 @@
     slots = RING * SLOT
     lanes = iota((slots, HEAD), 1)
     denoms = jnp.zeros((slots, HEAD), F32)
-    batch = 4
+    batch = 8
     for first in range(0, PAIRS, batch):
         some = range(first, first + batch)
         parts = []
@@ -525,8 +522,6 @@
         scratch=(pltpu.VMEM((ALL + ROOM, SHARE), F32),),
     )
     got = exchange(picked, "prefix").reshape(RING * TAKE, SHARE)
-    own = shape((TOKENS, SHARE), BF16), shape((RING, PACKED, HEAD), BF16)
-    placed = tuple(call(unpack_kernel, list(own), (at, got), flops=LONG))
 
     def take_all(_):
         everyone = exchange(jnp.broadcast_to(token_ids, (RING, STEPS, ROWS)), "prefix")
@@ -535,10 +530,16 @@
         rows = jnp.take(table, jnp.clip(inside_at, 0, vocab - 1), axis=0)
         rows = jnp.where(inside[..., None], rows, jnp.zeros_like(rows))
         rows = exchange(rows, "prefix").astype(F32).sum(axis=0).astype(BF16)
-        rows = rows.reshape(TOKENS, SHARE)
-        return rows, call(pack_kernel, own[1], (rows,))
-
-    embedded, packed = lax.cond(crowded, take_all, lambda placed: placed, placed)
+        rows = jnp.pad(rows.reshape(TOKENS, SHARE), ((0, RING * TAKE - TOKENS), (0, 0)))
+        return jnp.arange(TOKENS, dtype=jnp.int32).reshape(TOKENS, 1), rows
+
+    at, got = lax.cond(crowded, take_all, lambda found: found, (at, got))
+    embedded, packed = call(
+        unpack_kernel,
+        [shape((TOKENS, SHARE), BF16), shape((RING, PACKED, HEAD), BF16)],
+        (at, got),
+        flops=LONG,
+    )
     everywhere = exchange(packed, "branch")
 
     queries, sent = call(

time: 154 us -> 152 us (0.987)
    unnamed x24 -> x22, local copies, waits for them, and re-layouts: 3.59 us -> 2.35 us
  transfers between devices with their start and end apart: 4 -> 4, of which waited for: 4 -> 4; matrix products, arithmetic and copies ran while one was open for 2% -> 2% of each run, Pallas kernels for 3% -> 2%
where the time goes in v7:
time: 152 us; the launch traced here: 149 us
  blocking collectives  76.1 us (50%)
  waiting for transfers between devices  25.1 us (17%)
  starting transfers between devices  23.5 us (15%)
  Pallas kernels  18.2 us (12%)
  local copies, waits for them, and re-layouts  3.29 us (2%)
    all_to_all x3, blocking collectives, exchange(): return lax.all_to_all(x, axis, split_axis=0, concat_axis=0, tiled=True)  76.1 us
    all_to_all x4, waiting for transfers between devices, exchange(): return lax.all_to_all(x, axis, split_axis=0, concat_axis=0, tiled=True)  25.1 us
    all_to_all x4, starting transfers between devices, exchange(): return lax.all_to_all(x, axis, split_axis=0, concat_axis=0, tiled=True)  23.5 us
    pallas_call x10, Pallas kernels, call(): pl.pallas_call(kernel, out_shape=out_shape, in_specs=[SMEM] * scalars + [...  18.2 us
  transfers between devices with their start and end apart: 4, of which 4 were waited for; matrix products, arithmetic and copies ran while one was open for 2% of the time, Pallas kernels for 2%

profile of v7, /device:TPU:32, one launch (start us, length us, event | category | flops | bytes accessed | tf_op | source)
XLA Modules:
  0.0 149.0 jit_solution(5834818777415311643)
XLA Ops:
  0.0 0.0 copy-start.5
  0.0 0.7 copy-done.5
  0.7 0.0 copy-start.6
  0.7 0.0 copy-start.9
  0.7 2.0 %shard_map.127 = (s32[16,128]{1,0:T(8,128)}, s32[192,1]{1,0:T(8,128)S(1)}, s32[48,2]{1,0:T(8,128)S(1)}, s32[2,48]{1,0:T(2,128)S(1)}) custom-call(s32[4,48]{1,0:T(4,128)} %ids_ref.1, s32[1,48]{1,0:T(1,128)S(1)} %bitcast.36), custom_call_target="tpu_custom_call" | custom-call | flops 20000000000 | bytes 960 | tf_op jit(solution)/shard_map/pallas_call | solution.py:47
  2.7 8.6 %all-to-all-start.4 = ((s32[16,1,128]{2,1,0:T(1,128)}), s32[16,1,128]{2,1,0:T(1,128)S(1)}, u32[]{:S(2)}, u32[]{:S(2)}) async-start(s32[16,1,128]{2,1,0:T(1,128)} %bitcast.9), calls=%async_computation.4 | async-start | bytes 16384 | tf_op jit(solution)/shard_map/all_to_all | solution.py:465
  11.3 0.0 copy-done.6
  11.3 0.1 reshape.105
  11.4 0.0 copy-done.9
  11.4 0.1 convert_element_type.25
  11.5 0.1 tile.9
  11.6 0.4 fusion
  12.0 0.1 pad_maximum_fusion
  12.1 5.2 %all-to-all-done.4 = s32[16,1,128]{2,1,0:T(1,128)S(1)} async-done(((s32[16,1,128]{2,1,0:T(1,128)}), s32[16,1,128]{2,1,0:T(1,128)S(1)}, u32[]{:S(2)}, u32[]{:S(2)}) %all-to-all-start.4) | async-done | bytes 8224 | tf_op jit(solution)/shard_map/all_to_all | solution.py:465
  17.4 0.0 copy-start.7
  17.4 4.8 %shard_map.128 = bf16[16,24,288]{2,1,0:T(8,128)(2,1)} custom-call(s32[16,128]{1,0:T(8,128)S(1)} %bitcast.41, s32[16,128]{1,0:T(8,128)S(1)} %bitcast.42, bf16[288,8000]{1,0:T(8,128)(2,1)} %bitcast.38), custom_call_target="tpu_custom_call" | custom-call | flops 20000000000 | bytes 4624384 | tf_op jit(solution)/shard_map/pallas_call | solution.py:47
  22.2 4.8 %all-to-all-start.5 = ((bf16[16,24,288]{2,1,0:T(8,128)(2,1)}), bf16[16,24,288]{2,1,0:T(8,128)(2,1)S(1)}, u32[]{:S(2)}, u32[]{:S(2)}) async-start(bf16[16,24,288]{2,1,0:T(8,128)(2,1)} %shard_map.128), calls=%async_computation.5 | async-start | bytes 589824 | tf_op jit(solution)/shard_map/all_to_all | solution.py:465
  27.0 0.1 slice_reduce_fusion.1
  27.1 0.1 slice_reduce_fusion
  27.2 0.7 reduce_max.19
  28.5 8.7 %all-to-all-done.5 = bf16[16,24,288]{2,1,0:T(8,128)(2,1)S(1)} async-done(((bf16[16,24,288]{2,1,0:T(8,128)(2,1)}), bf16[16,24,288]{2,1,0:T(8,128)(2,1)S(1)}, u32[]{:S(2)}, u32[]{:S(2)}) %all-to-all-start.5) | async-done | bytes 221216 | tf_op jit(solution)/shard_map/all_to_all | solution.py:465
  37.2 0.0 copy-done.7
  37.2 0.4 shard_map.129
  37.6 0.0 copy-start.1
  37.6 32.4 %all_to_all.53.all_ref = bf16[16,432,128]{2,1,0:T(8,128)(2,1)S(1)} all-to-all(bf16[16,432,128]{2,1,0:T(8,128)(2,1)S(1)} %get-tuple-element.76), channel_id=1, replica_groups=mesh['prefix'=16,'branch'=16] {'branch'}, dimensions={0} | all-to-all | bytes 3538944 | tf_op jit(solution)/shard_map/all_to_all | solution.py:465
  70.0 0.0 copy-done.1
  70.0 0.0 copy-start.3
  70.0 0.0 copy-start.4
  70.0 2.0 %shard_map.130 = (bf16[192,256]{1,0:T(8,128)(2,1)S(1)}, bf16[128,1024]{1,0:T(8,128)(2,1)}) custom-call(bf16[16,432,128]{2,1,0:T(8,128)(2,1)S(1)} %all_to_all.53.all_ref, f32[3,16,128]{2,1,0:T(8,128)S(1)} %pad_maximum_fusion.2.gain_ref, f32[192,128]{1,0:T(8,128)S(1)} %get-tuple-element.78.cos_ref, f32[192,128]{1,0:T(8,128)S(1)} %get-tuple-element.79.sin_ref, ...), custom_call_target="tpu_custom_call" | custom-call | flops 20000000000 | bytes 4350336 | tf_op jit(solution)/shard_map/pallas_call | solution.py:47
  72.0 0.1 copy.18.len_ref
  72.1 6.6 %all-to-all-start.7 = ((bf16[16,8,1024]{2,1,0:T(8,128)(2,1)}), bf16[16,8,1024]{2,1,0:T(8,128)(2,1)S(1)}, u32[]{:S(2)}, u32[]{:S(2)}) async-start(bf16[16,8,1024]{2,1,0:T(8,128)(2,1)} %bitcast.15), calls=%async_computation.7 | async-start | bytes 524288 | tf_op jit(solution)/shard_map/all_to_all | solution.py:465
  78.7 0.0 copy-done.3
  78.7 0.0 copy-done.4
  78.7 0.0 copy-start.2
  78.7 1.7 %copy-done.2 = bf16[2,4608,128]{2,1,0:T(8,128)(2,1)S(1)} copy-done((bf16[2,4608,128]{2,1,0:T(8,128)(2,1)S(1)}, bf16[2,4608,128]{2,1,0:T(8,128)(2,1)}, u32[]{:S(2)}) %copy-start.2) | copy-done | bytes 2359320
  80.4 0.0 copy-start.10
  80.4 3.0 %shard_map.131 = f32[48,1152]{1,0:T(8,128)S(1)} custom-call(bf16[16,432,128]{2,1,0:T(8,128)(2,1)S(1)} %all_to_all.53.all_ref, f32[3,16,128]{2,1,0:T(8,128)S(1)} %pad_maximum_fusion.2.gain_ref, f32[192,128]{1,0:T(8,128)S(1)} %get-tuple-element.78.cos_ref, f32[192,128]{1,0:T(8,128)S(1)} %get-tuple-element.79.sin_ref, bf16[2,4608,128]{2,1,0:T(8,128)(2,1)S(1)} %copy-done.2, ...), custom_call_target="tpu_custom_call" | custom-call | flops 20000000000 | bytes 4645056 | tf_op jit(solution)/shard_map/pallas_call | solution.py:47
  83.4 0.6 slice.27
  84.6 3.8 %all-to-all-done.7 = bf16[16,8,1024]{2,1,0:T(8,128)(2,1)S(1)} async-done(((bf16[16,8,1024]{2,1,0:T(8,128)(2,1)}), bf16[16,8,1024]{2,1,0:T(8,128)(2,1)S(1)}, u32[]{:S(2)}, u32[]{:S(2)}) %all-to-all-start.7) | async-done | bytes 262176 | tf_op jit(solution)/shard_map/all_to_all | solution.py:465
  88.4 0.0 copy-done.10
  88.4 0.0 copy-start
  88.4 2.8 %shard_map.132 = bf16[128,1152]{1,0:T(8,128)(2,1)S(1)} custom-call(bf16[128,1024]{1,0:T(8,128)(2,1)S(1)} %bitcast.32, s32[16,128]{1,0:T(8,128)S(1)} %bitcast.46, bf16[2,1024,128]{2,1,0:T(8,128)(2,1)} %keys_ref.1, bf16[2,1024,128]{2,1,0:T(8,128)(2,1)} %values_ref.1), custom_call_target="tpu_custom_call" | custom-call | flops 1073741824 | bytes 1318912 | tf_op jit(solution)/shard_map/pallas_call | solution.py:47
  91.2 14.9 %all_to_all.54 = bf16[16,8,1152]{2,1,0:T(8,128)(2,1)S(1)} all-to-all(bf16[16,8,1152]{2,1,0:T(8,128)(2,1)S(1)} %bitcast.31), channel_id=1, replica_groups=mesh['prefix'=16,'branch'=16] {'prefix'}, dimensions={0} | all-to-all | bytes 589824 | tf_op jit(solution)/shard_map/all_to_all | solution.py:465
  106.1 0.0 copy-done
  106.1 1.1 shard_map.133
  107.2 0.0 copy-start.8
  107.3 28.8 %all_to_all.55.parts_ref = bf16[16,432,128]{2,1,0:T(8,128)(2,1)S(1)} all-to-all(bf16[16,432,128]{2,1,0:T(8,128)(2,1)S(1)} %shard_map.133), channel_id=1, replica_groups=mesh['prefix'=16,'branch'=16] {'branch'}, dimensions={0} | all-to-all | bytes 3538944 | tf_op jit(solution)/shard_map/all_to_all | solution.py:465
  136.1 1.0 shard_map.134
  137.1 3.5 %all-to-all-start.10 = ((f32[16,2,128]{2,1,0:T(2,128)}), f32[16,2,128]{2,1,0:T(2,128)S(1)}, u32[]{:S(2)}, u32[]{:S(2)}) async-start(f32[16,2,128]{2,1,0:T(2,128)} %get-tuple-element.90), calls=%async_computation.10 | async-start | bytes 32768 | tf_op jit(solution)/shard_map/all_to_all | solution.py:465
  140.6 0.0 copy-done.8
  140.6 0.1 shard_map.135
  140.8 7.4 %all-to-all-done.10.squares_ref = f32[16,2,128]{2,1,0:T(2,128)S(1)} async-done(((f32[16,2,128]{2,1,0:T(2,128)}), f32[16,2,128]{2,1,0:T(2,128)S(1)}, u32[]{:S(2)}, u32[]{:S(2)}) %all-to-all-start.10) | async-done | bytes 16416 | tf_op jit(solution)/shard_map/all_to_all | solution.py:465
  148.1 0.9 shard_map.136
  (10 shorter events, 0.0 us)
Async XLA Ops:
  0.0 0.7 copy-start.5
  0.7 10.6 %copy-start.6 = (f32[4608]{0:T(1024)S(1)}, f32[4608]{0:T(1024)}, u32[]{:S(2)}) copy-start(f32[4608]{0:T(1024)} %param.21) | copy-start | bytes 55300
  0.7 10.7 %copy-start.9 = (s32[48]{0:T(128)S(1)}, s32[48]{0:T(128)}, u32[]{:S(2)}) copy-start(s32[48]{0:T(128)} %param.19) | copy-start | bytes 580
  2.7 14.7 %all-to-all-start.4 = ((s32[16,1,128]{2,1,0:T(1,128)}), s32[16,1,128]{2,1,0:T(1,128)S(1)}, u32[]{:S(2)}, u32[]{:S(2)}) async-start(s32[16,1,128]{2,1,0:T(1,128)} %bitcast.9), calls=%async_computation.4 | async-start | bytes 16384 | tf_op jit(solution)/shard_map/all_to_all | solution.py:465
  17.4 19.8 %copy-start.7 = (s32[4,48]{1,0:T(4,128)S(1)}, s32[4,48]{1,0:T(4,128)}, u32[]{:S(2)}) copy-start(s32[4,48]{1,0:T(4,128)} %ids_ref.1) | copy-start | bytes 2308
  22.2 15.0 %all-to-all-start.5 = ((bf16[16,24,288]{2,1,0:T(8,128)(2,1)}), bf16[16,24,288]{2,1,0:T(8,128)(2,1)S(1)}, u32[]{:S(2)}, u32[]{:S(2)}) async-start(bf16[16,24,288]{2,1,0:T(8,128)(2,1)} %shard_map.128), calls=%async_computation.5 | async-start | bytes 589824 | tf_op jit(solution)/shard_map/all_to_all | solution.py:465
  37.6 32.4 %copy-start.1 = (bf16[4608,256]{1,0:T(8,128)(2,1)S(1)}, bf16[4608,256]{1,0:T(8,128)(2,1)}, u32[]{:S(2)}) copy-start(bf16[4608,256]{1,0:T(8,128)(2,1)} %wq_ref.1) | copy-start | bytes 7077892
  70.0 8.7 %copy-start.3 = (bf16[48,8,128]{2,1,0:T(8,128)(2,1)S(1)}, bf16[48,8,128]{2,1,0:T(8,128)(2,1)}, u32[]{:S(2)}) copy-start(bf16[48,8,128]{2,1,0:T(8,128)(2,1)} %param.28) | copy-start | bytes 294916
  70.0 8.7 %copy-start.4 = (bf16[48,8,128]{2,1,0:T(8,128)(2,1)S(1)}, bf16[48,8,128]{2,1,0:T(8,128)(2,1)}, u32[]{:S(2)}) copy-start(bf16[48,8,128]{2,1,0:T(8,128)(2,1)} %param.29) | copy-start | bytes 294916
  72.1 16.3 %all-to-all-start.7 = ((bf16[16,8,1024]{2,1,0:T(8,128)(2,1)}), bf16[16,8,1024]{2,1,0:T(8,128)(2,1)S(1)}, u32[]{:S(2)}, u32[]{:S(2)}) async-start(bf16[16,8,1024]{2,1,0:T(8,128)(2,1)} %bitcast.15), calls=%async_computation.7 | async-start | bytes 524288 | tf_op jit(solution)/shard_map/all_to_all | solution.py:465
  78.7 1.7 %copy-start.2 = (bf16[2,4608,128]{2,1,0:T(8,128)(2,1)S(1)}, bf16[2,4608,128]{2,1,0:T(8,128)(2,1)}, u32[]{:S(2)}) copy-start(bf16[2,4608,128]{2,1,0:T(8,128)(2,1)} %wkv_ref.1) | copy-start | bytes 7077892
  80.4 8.0 %copy-start.10 = (bf16[2,1024,128]{2,1,0:T(8,128)(2,1)S(1)}, bf16[2,1024,128]{2,1,0:T(8,128)(2,1)}, u32[]{:S(2)}) copy-start(bf16[2,1024,128]{2,1,0:T(8,128)(2,1)} %keys_ref.1) | copy-start | bytes 1572868
  88.4 17.7 %copy-start = (bf16[256,4608]{1,0:T(8,128)(2,1)S(1)}, bf16[256,4608]{1,0:T(8,128)(2,1)}, u32[]{:S(2)}) copy-start(bf16[256,4608]{1,0:T(8,128)(2,1)} %w_ref.1) | copy-start | bytes 7077892
  107.2 33.4 %copy-start.8 = (f32[288]{0:T(512)S(1)}, f32[288]{0:T(512)}, u32[]{:S(2)}) copy-start(f32[288]{0:T(512)} %param.25) | copy-start | bytes 3460
  137.1 11.0 %all-to-all-start.10 = ((f32[16,2,128]{2,1,0:T(2,128)}), f32[16,2,128]{2,1,0:T(2,128)S(1)}, u32[]{:S(2)}, u32[]{:S(2)}) async-start(f32[16,2,128]{2,1,0:T(2,128)} %get-tuple-element.90), calls=%async_computation.10 | async-start | bytes 32768 | tf_op jit(solution)/shard_map/all_to_all | solution.py:465
